TPU v7x, 32 devices: a whole 2x2x4 slice. The times are simulated.
32 devices in a mesh: grp: 2 (over y), doc: 4 (over z), feat: 4 (over x, core).
Axes of the slice: x: 2, y: 2, z: 4, core: 2. Of those that a mesh axis runs over, the one named last changes fastest.
Arguments:
- matrix: float32 [4096, 16384], P(('grp', 'doc'), 'feat'), parts along dimension 0, may hold values from 10 to 8000
- doc_factor: float32 [4096, 256], P(('grp', 'doc')), parts along dimension 0, may hold values from 0.25 to 10
- feat_factor: float32 [512, 16384], P(('grp', 'doc'), 'feat'), parts along dimension 0, may hold values from 0.25 to 2.5
Outputs:
- new_doc: float32 [4096, 256], P(('grp', 'doc')), parts along dimension 0
- new_feat: float32 [512, 16384], P(('grp', 'doc'), 'feat'), parts along dimension 0
There are 2 independent parts, one for each index of `grp`. A program takes and returns all parts, laid end to end along the dimension named above; each array names one. Nothing has to cross between parts.
All inputs are finite; a program needn't handle non-finite values.
Results may differ from a plain program's by a relative error of at most 0.0001.
Values sent between devices are 32-bit elements; how exact they have to be, the bound alone decides.
No kernel may reach another device: no remote copies, remote signals or barrier semaphores. Data moves between devices by JAX's collectives and lax.ppermute only.
A program may use at most 128 MiB of HBM per device.

v0:
```python
import jax
import jax.numpy as jnp
from jax import lax
from jax.sharding import PartitionSpec as P

INNER = 2


highest = lax.Precision.HIGHEST


def form_product(doc_factor, feat_factor):
    return jnp.dot(
        doc_factor,
        lax.all_gather(feat_factor, "doc", axis=0, tiled=True),
        precision=highest,
        preferred_element_type=jnp.float32,
    )


def gather_rows(feat_factor):
    return lax.all_gather(feat_factor, "doc", axis=0, tiled=True)


def transpose_product(doc_factor, ratio):
    return lax.dot_general(
        doc_factor,
        ratio,
        (((0,), (0,)), ((), ())),
        precision=highest,
        preferred_element_type=jnp.float32,
    )


def share_numerator(doc_factor, ratio):
    return lax.psum_scatter(
        transpose_product(doc_factor, ratio), "doc", scatter_dimension=0, tiled=True
    )


def body(matrix, doc_factor, feat_factor):
    rows_dev = feat_factor.shape[0]
    offset = lax.axis_index("doc") * rows_dev
    column_local = jnp.sum(doc_factor, axis=0)
    column_total = lax.psum(column_local, "doc")
    column_share = lax.dynamic_slice_in_dim(column_total, offset, rows_dev)
    gathered = feat_factor
    for inner_step in range(INNER):
        final_turn = inner_step == INNER - 1
        if final_turn:
            gathered = gather_rows(feat_factor)
            product = jnp.dot(
                doc_factor, gathered, precision=highest, preferred_element_type=jnp.float32
            )
            ratio = matrix / product
            numer_local = transpose_product(doc_factor, ratio)
            numer_total, column_whole = lax.psum((numer_local, column_local), "doc")
            gathered = gathered * numer_total / column_whole[:, None]
            feat_factor = lax.dynamic_slice_in_dim(gathered, offset, rows_dev, 0)
        else:
            product = form_product(doc_factor, feat_factor)
            ratio = matrix / product
            numer_share = share_numerator(doc_factor, ratio)
            feat_factor = feat_factor * numer_share / column_share[:, None]
    product = jnp.dot(doc_factor, gathered, precision=highest, preferred_element_type=jnp.float32)
    ratio = matrix / product
    wnumer_local = lax.dot_general(
        ratio,
        gathered,
        (((1,), (1,)), ((), ())),
        precision=highest,
        preferred_element_type=jnp.float32,
    )
    rowsum_local = jnp.sum(gathered, axis=1)
    wnumer, rowsum = lax.psum((wnumer_local, rowsum_local), "feat")
    doc_factor = doc_factor * wnumer / rowsum[None, :]
    return (doc_factor, feat_factor)


def solution(mesh):
    placed = (P(("grp", "doc"), "feat"), P(("grp", "doc"), None), P(("grp", "doc"), "feat"))
    return jax.shard_map(
        body,
        mesh=mesh,
        in_specs=placed,
        out_specs=(P(("grp", "doc"), None), P(("grp", "doc"), "feat")),
        check_vma=False,
    )
```

profile of v0, /device:TPU:0, one launch (start us, length us, event | category | flops | bytes accessed | tf_op | source)
XLA Modules:
  0.0 527.3 jit_solution(8107482743941760437)
XLA Ops:
  7.2 0.0 all-gather.3.cloned.1.call-start
  7.2 0.7 all-gather.3.cloned.1.call-update
  7.9 0.0 copy-start.1
  7.9 0.0 reduce-scatter.4.cloned.1.call-start
  8.0 85.1 %all-gather.3.cloned.1.call-done = f32[256,4096]{1,0:T(8,128)} async-done(((f32[64,4096]{1,0:T(8,128)}), f32[256,4096]{1,0:T(8,128)}) %all-gather.3.cloned.1.call-update) | async-done | bytes 4194320 | tf_op jit(solution)/shard_map/all_gather | solution.py:15
  93.1 0.0 copy-start.2
  93.1 9.5 %fusion.9 = f32[512,4096]{1,0:T(8,128)S(1)} fusion(f32[512,256]{1,0:T(8,128)} %param.4, f32[256,4096]{1,0:T(8,128)} %all-gather.3.cloned.1.call-done), kind=kOutput, calls=%fused_computation.13 | convolution fusion | flops 6442450944 | bytes 13107200 | tf_op jit(solution)/shard_map/dot_general | solution.py:13
  102.5 0.0 copy-done.1
  102.5 0.0 copy-done.2
  102.6 14.9 %fusion.4 = f32[256,4096]{0,1:T(8,128)} fusion(f32[512,256]{1,0:T(8,128)S(1)} %copy-done.1, f32[512,4096]{1,0:T(8,128)S(1)} %copy-done.2, f32[512,4096]{1,0:T(8,128)S(1)} %fusion.9), kind=kOutput, calls=%fused_computation.6 | convolution fusion | flops 6444548096 | bytes 21495808 | tf_op jit(solution)/shard_map/dot_general | solution.py:26
  117.5 5.6 %copy.16 = f32[256,4096]{1,0:T(8,128)} copy(f32[256,4096]{0,1:T(8,128)} %fusion.4) | data formatting | bytes 8388608
  123.1 0.0 copy-start.4
  123.1 0.0 reduce-scatter.4.cloned.1.call-update
  123.1 0.0 all-gather.5.cloned.1.call-start
  123.2 0.1 reduce_sum.18
  123.3 9.3 %psum.31 = f32[256]{0:T(256)S(1)} all-reduce(f32[256]{0:T(256)S(1)} %reduce_sum.18), channel_id=1, replica_groups=mesh['grp'=2,'doc'=4,'feat'=4] {'doc'}, use_global_device_ids=true, to_apply=%region_2.0 | all-reduce | flops 256 | bytes 2048 | tf_op jit(solution)/shard_map/psum | solution.py:45
  132.5 0.1 dynamic_slice.6
  132.6 66.1 %reduce-scatter.4.cloned.1.call-done = f32[64,4096]{1,0:T(8,128)} async-done(((f32[256,4096]{1,0:T(8,128)}), f32[64,4096]{1,0:T(8,128)}) %reduce-scatter.4.cloned.1.call-update) | async-done | bytes 1048592 | tf_op jit(solution)/shard_map/reduce_scatter | solution.py:36
  198.7 0.0 copy-done.4
  198.7 2.4 multiply_divide_fusion.1
  201.1 0.0 all-gather.5.cloned.1.call-update
  201.1 0.2 all-reduce.3.cloned.1.call-start
  201.3 9.1 %copy.14 = f32[512,4096]{0,1:T(8,128)} copy(f32[512,4096]{1,0:T(8,128)} %param.3) | data formatting | bytes 16777216 | tf_op args[0]
  210.4 72.0 %all-gather.5.cloned.1.call-done = f32[256,4096]{1,0:T(8,128)} async-done(((f32[64,4096]{1,0:T(8,128)}), f32[256,4096]{1,0:T(8,128)}) %all-gather.5.cloned.1.call-update) | async-done | bytes 4194320 | tf_op jit(solution)/shard_map/all_gather | solution.py:22
  282.4 0.0 copy-start.3
  282.4 16.0 %fusion.10 = f32[4096,512]{1,0:T(8,128)S(1)} fusion(f32[256,4096]{1,0:T(8,128)} %all-gather.5.cloned.1.call-done, f32[512,256]{1,0:T(8,128)S(1)} %copy-done.1), kind=kOutput, calls=%fused_computation.14 | convolution fusion | flops 6442450944 | bytes 13107200 | tf_op jit(solution)/shard_map/dot_general | solution.py:52
  298.4 0.0 copy-done.3
  298.4 8.5 %fusion.7 = f32[256,4096]{0,1:T(8,128)} fusion(f32[512,256]{1,0:T(8,128)S(1)} %copy-done.1, f32[512,4096]{0,1:T(8,128)S(1)} %copy-done.3, f32[4096,512]{1,0:T(8,128)S(1)} %fusion.10), kind=kOutput, calls=%fused_computation.7 | convolution fusion | flops 6444548096 | bytes 21495808 | tf_op jit(solution)/shard_map/dot_general | solution.py:26
  306.9 0.0 all-reduce.3.cloned.1.call-update
  307.0 0.0 all-reduce.5.cloned.1.call-start
  307.0 5.8 %copy.13 = f32[256,4096]{0,1:T(8,128)} copy(f32[256,4096]{1,0:T(8,128)} %all-gather.5.cloned.1.call-done) | data formatting | bytes 8388608 | tf_op jit(solution)/shard_map/all_gather | solution.py:22
  312.8 147.8 %all-reduce.3.cloned.1.call-done = f32[256,4096]{0,1:T(8,128)} async-done(((f32[256,4096]{0,1:T(8,128)}), f32[256,4096]{0,1:T(8,128)}) %all-reduce.3.cloned.1.call-update) | async-done | bytes 4194320 | tf_op jit(solution)/shard_map/psum | solution.py:57
  460.6 0.0 slice-start
  460.6 4.3 fusion.8
  464.9 0.0 copy-start
  464.9 0.0 slice-start.1
  464.9 6.9 %fusion.11 = f32[4096,512]{1,0:T(8,128)S(1)} fusion(f32[256,4096]{0,1:T(8,128)S(1)} %get-tuple-element.9, f32[512,256]{1,0:T(8,128)S(1)} %copy-done.1), kind=kOutput, calls=%fused_computation.15 | convolution fusion | flops 6442450944 | bytes 13107200 | tf_op jit(solution)/shard_map/dot_general | solution.py:65
  471.8 0.0 copy-done
  471.8 0.0 slice-done
  471.8 0.0 slice-done.1
  471.9 14.2 %fusion = f32[512,256]{1,0:T(8,128)} fusion(f32[256,4096]{0,1:T(8,128)S(1)} %get-tuple-element.9, f32[512,4096]{0,1:T(8,128)S(1)} %bitcast.23, f32[4096,512]{1,0:T(8,128)S(1)} %fusion.11), kind=kOutput, calls=%fused_computation.1 | convolution fusion | flops 6444548096 | bytes 21495808 | tf_op jit(solution)/shard_map/dot_general | solution.py:67
  486.1 0.0 all-reduce.5.cloned.1.call-update
  486.1 2.2 constant_dynamic-slice_fusion
  488.3 1.6 copy.15
  489.9 6.9 %psum.34 = f32[256]{0:T(256)S(1)} all-reduce(f32[256]{0:T(256)S(1)} %get-tuple-element.8), channel_id=1, replica_groups=mesh['grp'=2,'doc'=4,'feat'=4] {'feat'}, use_global_device_ids=true, to_apply=%region_6.0 | all-reduce | flops 256 | bytes 2048 | tf_op jit(solution)/shard_map/psum | solution.py:75
  496.8 21.7 %all-reduce.5.cloned.1.call-done = f32[512,256]{1,0:T(8,128)} async-done(((f32[512,256]{1,0:T(8,128)}), f32[512,256]{1,0:T(8,128)}) %all-reduce.5.cloned.1.call-update) | async-done | bytes 524304 | tf_op jit(solution)/shard_map/psum | solution.py:75
  518.4 1.9 multiply_divide_fusion.2
  (1 shorter events, 0.0 us)
Async XLA Ops:
  7.2 85.9 %all-gather.3.cloned.1.call-start = ((), (), s32[]{:S(2)}) async-start(), calls=%async_computation.1 | async-start | bytes 5242880 | tf_op jit(solution)/shard_map/all_gather | solution.py:15
  7.9 94.6 %copy-start.1 = (f32[512,256]{1,0:T(8,128)S(1)}, f32[512,256]{1,0:T(8,128)}, u32[]{:S(2)}) copy-start(f32[512,256]{1,0:T(8,128)} %param.4) | copy-start | bytes 1572868
  7.9 190.8 %reduce-scatter.4.cloned.1.call-start = ((), (), s32[]{:S(2)}) async-start(), calls=%async_computation.5 | async-start | bytes 5242880 | tf_op jit(solution)/shard_map/reduce_scatter | solution.py:36
  93.1 9.5 %copy-start.2 = (f32[512,4096]{1,0:T(8,128)S(1)}, f32[512,4096]{1,0:T(8,128)}, u32[]{:S(2)}) copy-start(f32[512,4096]{1,0:T(8,128)} %param.3) | copy-start | bytes 25165828
  123.1 75.6 %copy-start.4 = (f32[64,4096]{1,0:T(8,128)S(1)}, f32[64,4096]{1,0:T(8,128)}, u32[]{:S(2)}) copy-start(f32[64,4096]{1,0:T(8,128)} %param.5) | copy-start | bytes 3145732
  123.1 159.3 %all-gather.5.cloned.1.call-start = ((), (), s32[]{:S(2)}) async-start(), calls=%async_computation.2 | async-start | bytes 5242880 | tf_op jit(solution)/shard_map/all_gather | solution.py:22
  201.1 259.5 %all-reduce.3.cloned.1.call-start = ((), (), s32[]{:S(2)}) async-start(), calls=%async_computation.3 | async-start | bytes 8388608 | tf_op jit(solution)/shard_map/psum | solution.py:57
  282.4 16.0 %copy-start.3 = (f32[512,4096]{0,1:T(8,128)S(1)}, f32[512,4096]{0,1:T(8,128)}, u32[]{:S(2)}) copy-start(f32[512,4096]{0,1:T(8,128)} %copy.14) | copy-start | bytes 25165828
  307.0 211.5 %all-reduce.5.cloned.1.call-start = ((), (), s32[]{:S(2)}) async-start(), calls=%async_computation.4 | async-start | bytes 1048576 | tf_op jit(solution)/shard_map/psum | solution.py:75
  460.6 11.2 %slice-start = ((s8[8388608]{0:T(1024)(128)(4,1)}), s8[4194304]{0:T(1024)(128)(4,1)S(1)}, s32[]{:S(2)}) async-start(s8[8388608]{0:T(1024)(128)(4,1)} %bitcast.22), calls=%async_computation.6 | async-start | bytes 8388608
  464.9 6.9 %copy-start = (f32[256,4096]{0,1:T(8,128)}, f32[256,4096]{0,1:T(8,128)S(1)}, u32[]{:S(2)}) copy-start(f32[256,4096]{0,1:T(8,128)S(1)} %get-tuple-element.9) | copy-start | bytes 12582916
  464.9 7.0 %slice-start.1 = ((s8[8388608]{0:T(1024)(128)(4,1)}), s8[4194304]{0:T(1024)(128)(4,1)S(1)}, s32[]{:S(2)}) async-start(s8[8388608]{0:T(1024)(128)(4,1)} %bitcast.22), calls=%async_computation.7 | async-start | bytes 8388608
Sparse Core Ops, SparseCore 0:
  9.6 83.4 all-gather.2
  123.2 75.4 reduce-scatter.3
  201.2 81.1 all-gather.4
  307.1 153.4 all-reduce.2
  486.3 32.1 all-reduce.4
where the time goes:
time: 536 us; the launch traced here: 527 us
  waiting for transfers between devices  393 us (73%)
  matrix products  70 us (13%)
  local copies, waits for them, and re-layouts  24.4 us (5%)
  blocking collectives  16.1 us (3%)
  between operations  14.3 us (3%)
  other arithmetic  8.59 us (2%)
    psum x1, waiting for transfers between devices, body(): numer_total, column_whole = lax.psum((numer_local, column_local), 'doc')  148 us
    all_gather x1, waiting for transfers between devices, form_product(): lax.all_gather(feat_factor, 'doc', axis=0, tiled=True)  85.1 us
    all_gather x1, waiting for transfers between devices, gather_rows(): return lax.all_gather(feat_factor, 'doc', axis=0, tiled=True)  72 us
    reduce_scatter x1, waiting for transfers between devices, share_numerator(): lax.psum_scatter(transpose_product(doc_factor, ratio), 'doc', scatter_dim...  66.1 us
    dot_general x2, matrix products, transpose_product(): lax.dot_general(doc_factor, ratio, (((0,), (0,)), ((), ())), precision=hi...  23.4 us
    dot_general x2, matrix products, body(): jnp.dot(doc_factor, gathered, precision=highest, preferred_element_type=j...  22.9 us
    psum x1, waiting for transfers between devices, body(): wnumer, rowsum = lax.psum((wnumer_local, rowsum_local), 'feat')  21.7 us
    unnamed x17, local copies, waits for them, and re-layouts  16.4 us
  transfers between devices with their start and end apart: 5, of which 5 were waited for; matrix products, arithmetic and copies ran while one was open for 4% of the time, Pallas kernels for 0%

commit v1 on v0

v1 whole, which is shorter than its diff:
```python
import functools

import jax
import jax.numpy as jnp
from jax import lax
from jax.experimental import pallas as pl
from jax.experimental.pallas import tpu as pltpu
from jax.sharding import PartitionSpec as P

INNER = 2
WIDTH = 256
PAD = 8
VMEM = 48 * 1024 * 1024
NT = (((1,), (1,)), ((), ()))


def xor_pairs(count, mask):
    return [(i, i ^ mask) for i in range(count)]


def split(value):
    high = value.astype(jnp.bfloat16)
    low = (value - high.astype(jnp.float32)).astype(jnp.bfloat16)
    return high, low


def dot(left, right):
    return jnp.dot(left, right, preferred_element_type=jnp.float32)


def dot3(left, right):
    return dot(left[0], right[0]) + (dot(left[0], right[1]) + dot(left[1], right[0]))


def dot_nt(left, right):
    return lax.dot_general(left, right, NT, preferred_element_type=jnp.float32)


def prepare_kernel(blocks, *refs):
    w_refs, (high_ref, low_ref, high_t_ref, low_t_ref, sum_ref) = refs[:blocks], refs[blocks:]
    rows = w_refs[0].shape[0]
    total = jnp.zeros(sum_ref.shape, jnp.float32)
    for b in range(blocks):
        value = w_refs[b][...]
        high, low = split(value)
        high_ref[b * rows : (b + 1) * rows, :] = high
        low_ref[b * rows : (b + 1) * rows, :] = low
        turned = value.T
        high, low = split(turned)
        high_t_ref[:, b * rows : (b + 1) * rows] = high
        low_t_ref[:, b * rows : (b + 1) * rows] = low
        total = total + jnp.sum(turned, axis=1, keepdims=True)
    sum_ref[...] = total


def prepare(w_blocks):
    blocks = len(w_blocks)
    rows, rank = w_blocks[0].shape
    docs = blocks * rows
    half = jnp.bfloat16
    shapes = [
        jax.ShapeDtypeStruct((docs, rank), half),
        jax.ShapeDtypeStruct((docs, rank), half),
        jax.ShapeDtypeStruct((rank, docs), half),
        jax.ShapeDtypeStruct((rank, docs), half),
        jax.ShapeDtypeStruct((rank, 1), jnp.float32),
    ]
    return pl.pallas_call(
        functools.partial(prepare_kernel, blocks),
        out_shape=shapes,
        in_specs=[pl.BlockSpec(memory_space=pltpu.VMEM)] * blocks,
        out_specs=[pl.BlockSpec(memory_space=pltpu.VMEM)] * len(shapes),
        compiler_params=pltpu.CompilerParams(vmem_limit_bytes=VMEM),
        cost_estimate=pl.CostEstimate(flops=0, bytes_accessed=docs * rank * 12, transcendentals=0),
        name="prepare_w",
    )(*w_blocks)


def piece_kernel(blocks, parts, first, *refs):
    m_refs = refs[:blocks]
    high_ref, low_ref, high_t_ref, low_t_ref, sum_ref, h_ref = refs[blocks : blocks + 6]
    rest = refs[blocks + 6 :]
    wn_in = None if first else rest[0]
    h_out, wn_out = rest[0 if first else 1 :]
    rows = m_refs[0].shape[0]
    width = h_ref.shape[1]
    part_rows = rows // parts

    def ratio(b, factor):
        near = slice(b * rows, (b + 1) * rows)
        product = dot3((high_ref[near, :], low_ref[near, :]), factor)
        return split(m_refs[b][...] / product)

    factor = h_ref[...]
    for _ in range(INNER):
        pair = split(factor)
        total = None
        for b in range(blocks):
            near = slice(b * rows, (b + 1) * rows)
            term = dot3((high_t_ref[:, near], low_t_ref[:, near]), ratio(b, pair))
            total = term if total is None else total + term
        factor = factor * total / sum_ref[...]
    h_out[...] = factor
    pair = split(factor)
    ones = jnp.ones((PAD, width), jnp.bfloat16)
    row_sum = dot_nt(ones, pair[0]) + dot_nt(ones, pair[1])
    for b in range(blocks):
        high, low = ratio(b, pair)
        term = dot_nt(high, pair[0]) + (dot_nt(high, pair[1]) + dot_nt(low, pair[0]))
        for q in range(parts):
            body_rows = term[q * part_rows : (q + 1) * part_rows, :]
            if first:
                wn_out[b, q, :part_rows, :] = body_rows
                wn_out[b, q, part_rows:, :] = row_sum
            else:
                wn_out[b, q, :part_rows, :] = wn_in[b, q, :part_rows, :] + body_rows
                wn_out[b, q, part_rows:, :] = wn_in[b, q, part_rows:, :] + row_sum


def update_piece(m_blocks, weights, factor, sums, parts):
    blocks = len(m_blocks)
    rows, width = m_blocks[0].shape
    rank = factor.shape[0]
    first = sums is None
    sums_shape = (blocks, parts, rows // parts + PAD, rank)
    given = [*m_blocks, *weights, factor] + ([] if first else [sums])
    space = pl.BlockSpec(memory_space=pltpu.VMEM)
    return pl.pallas_call(
        functools.partial(piece_kernel, blocks, parts, first),
        out_shape=[
            jax.ShapeDtypeStruct((rank, width), jnp.float32),
            jax.ShapeDtypeStruct(sums_shape, jnp.float32),
        ],
        in_specs=[space] * len(given),
        out_specs=[space] * 2,
        input_output_aliases={} if first else {len(given) - 1: 1},
        compiler_params=pltpu.CompilerParams(vmem_limit_bytes=VMEM),
        cost_estimate=pl.CostEstimate(
            flops=30 * blocks * rows * width * rank,
            bytes_accessed=blocks * rows * (4 * width + 16 * rank),
            transcendentals=0,
        ),
        name="update_piece",
    )(*given)


def update_plain(m_blocks, w_blocks, factor, parts):
    highest = lax.Precision.HIGHEST
    whole_w = jnp.concatenate(w_blocks, axis=0)
    whole_m = jnp.concatenate(m_blocks, axis=0)
    blocks = len(m_blocks)
    rows, rank = w_blocks[0].shape
    column = jnp.sum(whole_w, axis=0)[:, None]
    for _ in range(INNER):
        ratio = whole_m / jnp.dot(whole_w, factor, precision=highest)
        numer = lax.dot_general(whole_w, ratio, (((0,), (0,)), ((), ())), precision=highest)
        factor = factor * numer / column
    ratio = whole_m / jnp.dot(whole_w, factor, precision=highest)
    wnumer = lax.dot_general(ratio, factor, NT, precision=highest)
    wnumer = wnumer.reshape(blocks, parts, rows // parts, rank)
    row_sum = jnp.broadcast_to(jnp.sum(factor, axis=1), (blocks, parts, PAD, rank))
    return factor, jnp.concatenate([wnumer, row_sum], axis=2)


def gather_feat(value, bits, feat, lead):
    for j in reversed(range(bits)):
        other = lax.ppermute(value, "feat", xor_pairs(1 << bits, 1 << j))
        axis = lead + bits - 1 - j
        low_side = (feat >> j) & 1 == 0
        value = jnp.where(
            low_side, jnp.stack([value, other], axis), jnp.stack([other, value], axis)
        )
    shape = value.shape
    return value.reshape(shape[:lead] + (-1,) + shape[-1:])


def scatter_feat(value, bits, feat):
    blocks = value.shape[0]
    value = value.reshape((blocks,) + (2,) * bits + value.shape[2:])
    for j in range(bits):
        bit = (feat >> j) & 1
        axis = bits - j
        kept = lax.dynamic_index_in_dim(value, bit, axis, keepdims=False)
        sent = lax.dynamic_index_in_dim(value, 1 - bit, axis, keepdims=False)
        value = kept + lax.ppermute(sent, "feat", xor_pairs(1 << bits, 1 << j))
    return value


def body(n_doc, n_feat, matrix, doc_factor, feat_factor):
    doc, feat = lax.axis_index("doc"), lax.axis_index("feat")
    bits = n_feat.bit_length() - 1
    rows, columns = matrix.shape
    share, rank = feat_factor.shape[0], doc_factor.shape[1]
    owned = columns // n_doc
    width = WIDTH if owned % WIDTH == 0 else owned
    pieces = owned // width
    part_rows = rows // n_feat

    def send(value, k):
        return lax.ppermute(value, "doc", xor_pairs(n_doc, k)) if k else value

    def m_piece(p):
        return [
            send(lax.dynamic_slice(matrix, (0, (doc ^ k) * owned + p * width), (rows, width)), k)
            for k in range(n_doc)
        ]

    w_part = lax.dynamic_slice_in_dim(doc_factor, feat * part_rows, part_rows, 0)
    w_parts = [send(w_part, k) for k in range(1, n_doc)]
    h_blocks = [
        send(lax.dynamic_slice(feat_factor, (0, (doc ^ k) * owned), (share, owned)), k)
        for k in range(n_doc)
    ]
    m_pieces = [m_piece(p) for p in range(pieces)]

    w_others = gather_feat(jnp.stack(w_parts), bits, feat, 1)
    w_blocks = [doc_factor] + [w_others[k] for k in range(n_doc - 1)]
    factor = jnp.zeros((rank, owned), jnp.float32)
    for k in range(n_doc):
        factor = lax.dynamic_update_slice(factor, h_blocks[k], ((doc ^ k) * share, 0))

    in_kernel = n_doc * rows * rank * 32 < VMEM
    if in_kernel:
        weights = prepare(w_blocks)
    new_feat = jnp.zeros((share, columns), jnp.float32)
    sums = None
    for p in range(pieces):
        h_piece = factor[:, p * width : (p + 1) * width]
        if in_kernel:
            h_new, sums = update_piece(m_pieces[p], weights, h_piece, sums, n_feat)
        else:
            h_new, more = update_plain(m_pieces[p], w_blocks, h_piece, n_feat)
            sums = more if sums is None else sums + more
        for k in range(n_doc):
            back = lax.dynamic_slice(h_new, ((doc ^ k) * share, 0), (share, width))
            new_feat = lax.dynamic_update_slice(
                new_feat, send(back, k), (0, (doc ^ k) * owned + p * width)
            )

    sums = scatter_feat(sums, bits, feat)
    total = sums[0]
    for k in range(1, n_doc):
        total = total + send(sums[k], k)
    new_part = w_part * total[:part_rows] / total[part_rows]
    new_doc = gather_feat(new_part, bits, feat, 0)
    return new_doc, new_feat


def solution(mesh):
    placed = (P(("grp", "doc"), "feat"), P(("grp", "doc"), None), P(("grp", "doc"), "feat"))
    return jax.shard_map(
        functools.partial(body, mesh.shape["doc"], mesh.shape["feat"]),
        mesh=mesh,
        in_specs=placed,
        out_specs=(P(("grp", "doc"), None), P(("grp", "doc"), "feat")),
        check_vma=False,
    )
```

time: 536 us -> 291 us (0.54); the launches traced: 527 us -> 291 us
  waiting for transfers between devices: 393 us -> 160 us
  matrix products: 70 us -> 0 us
  starting transfers between devices: 0.37 us -> 56.9 us
  Pallas kernels: 0 us -> 40.7 us
  blocking collectives: 16.1 us -> 0 us
  between operations: 14.3 us -> 0.99 us
    psum x2 -> x0, waiting for transfers between devices: 169 us -> none  [the longest x1 148 us: body(): numer_total, column_whole = lax.psum((numer_local, column_local), 'doc')]
    ppermute x0 -> x39, waiting for transfers between devices: none -> 160 us  [the longest x33 154 us: send(): return lax.ppermute(value, 'doc', xor_pairs(n_doc, k)) if k else value]
    all_gather x2 -> x0, waiting for transfers between devices: 157 us -> none  [the longest x1 85.1 us: form_product(): lax.all_gather(feat_factor, 'doc', axis=0, tiled=True)]
    dot_general x6 -> x0, matrix products: 70 us -> none  [the longest x2 23.4 us: transpose_product(): lax.dot_general(doc_factor, ratio, (((0,), (0,)), ((), ())), precision=hi...]
    reduce_scatter x1 -> x0, waiting for transfers between devices: 66.1 us -> none  [share_numerator(): lax.psum_scatter(transpose_product(doc_factor, ratio), 'doc', scatter_dim...]
    ppermute x0 -> x39, starting transfers between devices: none -> 56.9 us  [the longest x33 54.6 us: send(): return lax.ppermute(value, 'doc', xor_pairs(n_doc, k)) if k else value]
    pallas_call x0 -> x5, Pallas kernels: none -> 40.7 us  [the longest x4 39 us: update_piece(): pl.pallas_call(functools.partial(piece_kernel, blocks, parts, first), out...]
    psum x2 -> x0, blocking collectives: 16.1 us -> none  [the longest x1 9.25 us: body(): column_total = lax.psum(column_local, 'doc')]
  transfers between devices with their start and end apart: 5 -> 39, of which waited for: 5 -> 20; matrix products, arithmetic and copies ran while one was open for 4% -> 9% of each run, Pallas kernels for 0% -> 11%
where the time goes in v1:
time: 291 us
  waiting for transfers between devices  160 us (55%)
  starting transfers between devices  56.9 us (20%)
  Pallas kernels  40.7 us (14%)
  local copies, waits for them, and re-layouts  27.9 us (10%)
  other arithmetic  4.67 us (2%)
    ppermute x33, waiting for transfers between devices, send(): return lax.ppermute(value, 'doc', xor_pairs(n_doc, k)) if k else value  154 us
    ppermute x33, starting transfers between devices, send(): return lax.ppermute(value, 'doc', xor_pairs(n_doc, k)) if k else value  54.6 us
    pallas_call x4, Pallas kernels, update_piece(): pl.pallas_call(functools.partial(piece_kernel, blocks, parts, first), out...  39 us
    dynamic_slice x1, local copies, waits for them, and re-layouts, m_piece(): lax.dynamic_slice(matrix, (0, (doc ^ k) * owned + p * width), (rows, width))  6.16 us
  transfers between devices with their start and end apart: 39, of which 20 were waited for; matrix products, arithmetic and copies ran while one was open for 9% of the time, Pallas kernels for 11%

profile of v1, /device:TPU:0, one launch (start us, length us, event | category | flops | bytes accessed | tf_op | source)
XLA Modules:
  0.0 290.9 jit_solution(14555586162705511916)
XLA Ops:
  0.6 1.0 constant_dynamic-slice_fusion.31
  1.7 5.1 %collective-permute-start.5 = (f32[128,256]{1,0:T(8,128)S(1)}, f32[128,256]{1,0:T(8,128)S(1)}, u32[]{:S(2)}, u32[]{:S(2)}) collective-permute-start(f32[128,256]{1,0:T(8,128)S(1)} %constant_dynamic-slice_fusion.31), channel_id=1, source_target_pairs={{0,12},{4,8},{8,4},{12,0},{1,13},{5,9},{9,5},{13,1},{2,14},{6,10},... | collective-permute-start | bytes 393224 | tf_op jit(solution)/shard_map/ppermute | solution.py:200
  7.4 3.8 %collective-permute-done.5 = f32[128,256]{1,0:T(8,128)S(1)} collective-permute-done((f32[128,256]{1,0:T(8,128)S(1)}, f32[128,256]{1,0:T(8,128)S(1)}, u32[]{:S(2)}, u32[]{:S(2)}) %collective-permute-start.5) | collective-permute-done | bytes 131104 | tf_op jit(solution)/shard_map/ppermute | solution.py:200
  11.2 6.6 %collective-permute-done.4 = f32[128,256]{1,0:T(8,128)S(1)} collective-permute-done((f32[128,256]{1,0:T(8,128)S(1)}, f32[128,256]{1,0:T(8,128)S(1)}, u32[]{:S(2)}, u32[]{:S(2)}) %collective-permute-start.4) | collective-permute-done | bytes 131104 | tf_op jit(solution)/shard_map/ppermute | solution.py:200
  17.9 1.6 collective-permute-start.6
  19.5 1.1 broadcast_in_dim.6
  20.6 1.0 constant_dynamic-slice_fusion.24
  21.6 3.0 %collective-permute-start.9 = (f32[64,1024]{1,0:T(8,128)}, f32[64,1024]{1,0:T(8,128)}, u32[]{:S(2)}, u32[]{:S(2)}) collective-permute-start(f32[64,1024]{1,0:T(8,128)} %get-tuple-element.54), channel_id=1, source_target_pairs={{0,8},{4,12},{8,0},{12,4},{1,9},{5,13},{9,1},{13,5},{2,10},{6,14},... | collective-permute-start | bytes 786440 | tf_op jit(solution)/shard_map/ppermute | solution.py:200
  24.6 1.3 collective-permute-start.10
  26.0 2.2 collective-permute-done.6
  28.2 0.9 maximum_select_fusion.2
  29.1 6.2 %constant_dynamic-slice_fusion.12 = (f32[512,256]{1,0:T(8,128)}, f32[512,256]{1,0:T(8,128)}, f32[512,256]{1,0:T(8,128)S(1)}, f32[512,256]{1,0:T(8,128)}, f32[512...) fusion(f32[512,4096]{1,0:T(8,128)} %param.3, ...), kind=kLoop, calls=%fused_computation.48 | loop fusion | bytes 16777280 | tf_op jit(solution)/shard_map/dynamic_slice | solution.py:204
  35.4 2.0 collective-permute-start.17
  37.4 1.7 constant_dynamic-update-slice_fusion.13
  39.0 4.4 %collective-permute-done.9 = f32[64,1024]{1,0:T(8,128)} collective-permute-done((f32[64,1024]{1,0:T(8,128)}, f32[64,1024]{1,0:T(8,128)}, u32[]{:S(2)}, u32[]{:S(2)}) %collective-permute-start.9) | collective-permute-done | bytes 262176 | tf_op jit(solution)/shard_map/ppermute | solution.py:200
  43.4 1.7 constant_dynamic-update-slice_fusion.12
  45.1 2.4 collective-permute-start.19
  47.4 1.7 constant_dynamic-update-slice_fusion.11
  49.1 1.3 fusion.7
  50.5 3.7 %collective-permute-start.14 = (f32[512,256]{1,0:T(8,128)S(1)}, f32[512,256]{1,0:T(8,128)S(1)}, u32[]{:S(2)}, u32[]{:S(2)}) collective-permute-start(f32[512,256]{1,0:T(8,128)S(1)} %copy-done.10), channel_id=1, source_target_pairs={{0,4},{4,0},{8,12},{12,8},{1,5},{5,1},{9,13},{13,9},{2,6},{6,2},{1... | collective-permute-start | bytes 1572872 | tf_op jit(solution)/shard_map/ppermute | solution.py:200
  54.2 1.6 maximum_select_fusion
  55.8 8.7 %collective-permute-done.11.refs_1_ = f32[512,256]{1,0:T(8,128)S(1)} collective-permute-done((f32[512,256]{1,0:T(8,128)}, f32[512,256]{1,0:T(8,128)S(1)}, u32[]{:S(2)}, u32[]{:S(2)}) %collective-permute-start.11) | collective-permute-done | bytes 524320 | tf_op jit(solution)/shard_map/ppermute | solution.py:200
  64.8 22.1 %collective-permute-done.17.refs_1_ = f32[512,256]{1,0:T(8,128)S(1)} collective-permute-done((f32[512,256]{1,0:T(8,128)}, f32[512,256]{1,0:T(8,128)S(1)}, u32[]{:S(2)}, u32[]{:S(2)}) %collective-permute-start.17) | collective-permute-done | bytes 524320 | tf_op jit(solution)/shard_map/ppermute | solution.py:200
  86.8 2.2 collective-permute-start.16
  89.3 0.9 copy-done
  90.2 1.7 prepare_w.1
  91.9 1.7 collective-permute-start.13
  93.6 9.2 %update_piece.4 = (f32[256,256]{1,0:T(8,128)S(1)}, f32[4,4,136,256]{3,2,1,0:T(8,128)}) custom-call(f32[512,256]{1,0:T(8,128)S(1)} %get-tuple-element.30.refs_0_, f32[512,256]{1,0:T(8,128)S(1)} %collective-permute-done.17.refs_1_, f32[512,256]{1,0:T(8,128)S(1)} %collective-permute-done.18.refs_2_, f32[512,256]{1,0:T(8,128)S(1)} %collective-permute-done.19.refs_3_, ...), custom_call_target="tpu_custom_call" | custom-call | flops 4026531840 | bytes 10485760 | tf_op jit(solution)/shard_map/update_piece/pallas_call | solution.py:128
  102.8 0.7 collective-permute-done.14.refs_1_
  103.6 1.6 collective-permute-start
  105.2 45.0 %collective-permute-done.15.refs_2_ = f32[512,256]{1,0:T(8,128)S(1)} collective-permute-done((f32[512,256]{1,0:T(8,128)S(1)}, f32[512,256]{1,0:T(8,128)S(1)}, u32[]{:S(2)}, u32[]{:S(2)}) %collective-permute-start.15) | collective-permute-done | bytes 524320 | tf_op jit(solution)/shard_map/ppermute | solution.py:200
  150.2 2.4 collective-permute-start.2
  152.6 10.0 %update_piece.5 = (f32[256,256]{1,0:T(8,128)S(1)}, f32[4,4,136,256]{3,2,1,0:T(8,128)}) custom-call(f32[512,256]{1,0:T(8,128)S(1)} %get-tuple-element.34.refs_0_, f32[512,256]{1,0:T(8,128)S(1)} %collective-permute-done.14.refs_1_, f32[512,256]{1,0:T(8,128)S(1)} %collective-permute-done.15.refs_2_, ...), custom_call_target="tpu_custom_call", output_to_operand_aliasing={{1}: (10, {})} | custom-call | flops 4026531840 | bytes 10485760 | tf_op jit(solution)/shard_map/update_piece/pallas_call | solution.py:128
  162.6 32.5 %collective-permute-done.12.refs_2_ = f32[512,256]{1,0:T(8,128)S(1)} collective-permute-done((f32[512,256]{1,0:T(8,128)S(1)}, f32[512,256]{1,0:T(8,128)S(1)}, u32[]{:S(2)}, u32[]{:S(2)}) %collective-permute-start.12) | collective-permute-done | bytes 524320 | tf_op jit(solution)/shard_map/ppermute | solution.py:200
  195.1 9.9 %update_piece.6 = (f32[256,256]{1,0:T(8,128)S(1)}, f32[4,4,136,256]{3,2,1,0:T(8,128)}) custom-call(f32[512,256]{1,0:T(8,128)S(1)} %get-tuple-element.38.refs_0_, f32[512,256]{1,0:T(8,128)S(1)} %collective-permute-done.11.refs_1_, f32[512,256]{1,0:T(8,128)S(1)} %collective-permute-done.12.refs_2_, ...), custom_call_target="tpu_custom_call", output_to_operand_aliasing={{1}: (10, {})} | custom-call | flops 4026531840 | bytes 10485760 | tf_op jit(solution)/shard_map/update_piece/pallas_call | solution.py:128
  205.0 12.6 %collective-permute-done.1.refs_2_ = f32[512,256]{1,0:T(8,128)S(1)} collective-permute-done((f32[512,256]{1,0:T(8,128)S(1)}, f32[512,256]{1,0:T(8,128)S(1)}, u32[]{:S(2)}, u32[]{:S(2)}) %collective-permute-start.1) | collective-permute-done | bytes 524320 | tf_op jit(solution)/shard_map/ppermute | solution.py:200
  217.6 9.9 %update_piece.7 = (f32[256,256]{1,0:T(8,128)S(1)}, f32[4,4,136,256]{3,2,1,0:T(8,128)}) custom-call(f32[512,256]{1,0:T(8,128)S(1)} %get-tuple-element.42.refs_0_, f32[512,256]{1,0:T(8,128)S(1)} %collective-permute-done.refs_1_, f32[512,256]{1,0:T(8,128)S(1)} %collective-permute-done.1.refs_2_, ...), custom_call_target="tpu_custom_call", output_to_operand_aliasing={{1}: (10, {})} | custom-call | flops 4026531840 | bytes 10485760 | tf_op jit(solution)/shard_map/update_piece/pallas_call | solution.py:128
  227.4 1.3 dynamic-slice_bitcast_fusion
  229.0 9.6 %collective-permute-start.27 = (f32[64,256]{1,0:T(8,128)S(1)}, f32[64,256]{1,0:T(8,128)S(1)}, u32[]{:S(2)}, u32[]{:S(2)}) collective-permute-start(f32[64,256]{1,0:T(8,128)S(1)} %get-tuple-element.75), channel_id=1, source_target_pairs={{0,4},{4,0},{8,12},{12,8},{1,5},{5,1},{9,13},{13,9},{2,6},{6,2},{1... | collective-permute-start | bytes 196616 | tf_op jit(solution)/shard_map/ppermute | solution.py:200
  238.6 0.9 collective-permute-start.28
  239.4 1.6 collective-permute-start.29
  241.3 5.7 %collective-permute-done.28 = f32[64,256]{1,0:T(8,128)S(1)} collective-permute-done((f32[64,256]{1,0:T(8,128)S(1)}, f32[64,256]{1,0:T(8,128)S(1)}, u32[]{:S(2)}, u32[]{:S(2)}) %collective-permute-start.28) | collective-permute-done | bytes 65568 | tf_op jit(solution)/shard_map/ppermute | solution.py:200
  247.2 1.0 copy-done.2
  248.1 1.4 collective-permute-start.30
  249.5 1.2 collective-permute-start.31
  250.7 1.8 collective-permute-start.32
  253.6 1.7 bitcast_add_fusion
  255.4 0.9 dynamic-slice_bitcast_fusion.1
  256.2 0.9 collective-permute-done.31
  258.4 0.6 constant_dynamic-slice_fusion.2
  259.1 0.9 collective-permute-start.33
  260.0 1.8 collective-permute-start.34
  261.8 1.7 collective-permute-start.35
  264.1 2.0 collective-permute-done.34
  266.7 2.2 collective-permute-done.21
  269.0 2.4 collective-permute-start.24
  271.8 1.7 collective-permute-start.22
  274.1 0.6 constant_dynamic-slice_fusion.1
  275.1 2.3 collective-permute-done.24
  277.4 4.1 %collective-permute-done.23 = f32[136,256]{1,0:T(8,128)S(1)} collective-permute-done((f32[136,256]{1,0:T(8,128)S(1)}, f32[136,256]{1,0:T(8,128)S(1)}, u32[]{:S(2)}, u32[]{:S(2)}) %collective-permute-start.23) | collective-permute-done | bytes 139296 | tf_op jit(solution)/shard_map/ppermute | solution.py:200
  282.5 2.4 collective-permute-start.38
  285.5 1.1 collective-permute-done.25
  286.8 1.9 collective-permute-done.37
  290.0 0.8 copy.17
  (86 shorter events, 10.0 us)
Async XLA Ops:
  0.6 20.0 %copy-start.1 = (f32[64,4096]{1,0:T(8,128)S(1)}, f32[64,4096]{1,0:T(8,128)}, u32[]{:S(2)}) copy-start(f32[64,4096]{1,0:T(8,128)} %param.5) | copy-start | bytes 3145732
  1.7 9.5 %collective-permute-start.5 = (f32[128,256]{1,0:T(8,128)S(1)}, f32[128,256]{1,0:T(8,128)S(1)}, u32[]{:S(2)}, u32[]{:S(2)}) collective-permute-start(f32[128,256]{1,0:T(8,128)S(1)} %constant_dynamic-slice_fusion.31), channel_id=1, source_target_pairs={{0,12},{4,8},{8,4},{12,0},{1,13},{5,9},{9,5},{13,1},{2,14},{6,10},... | collective-permute-start | bytes 393224 | tf_op jit(solution)/shard_map/ppermute | solution.py:200
  6.8 11.1 %collective-permute-start.4 = (f32[128,256]{1,0:T(8,128)S(1)}, f32[128,256]{1,0:T(8,128)S(1)}, u32[]{:S(2)}, u32[]{:S(2)}) collective-permute-start(f32[128,256]{1,0:T(8,128)S(1)} %constant_dynamic-slice_fusion.31), channel_id=1, source_target_pairs={{0,8},{4,12},{8,0},{12,4},{1,9},{5,13},{9,1},{13,5},{2,10},{6,14},... | collective-permute-start | bytes 393224 | tf_op jit(solution)/shard_map/ppermute | solution.py:200
  6.8 11.1 %collective-permute-start.3 = (f32[128,256]{1,0:T(8,128)S(1)}, f32[128,256]{1,0:T(8,128)S(1)}, u32[]{:S(2)}, u32[]{:S(2)}) collective-permute-start(f32[128,256]{1,0:T(8,128)S(1)} %constant_dynamic-slice_fusion.31), channel_id=1, source_target_pairs={{0,4},{4,0},{8,12},{12,8},{1,5},{5,1},{9,13},{13,9},{2,6},{6,2},{1... | collective-permute-start | bytes 393224 | tf_op jit(solution)/shard_map/ppermute | solution.py:200
  17.9 10.2 %collective-permute-start.6 = (f32[3,128,256]{2,1,0:T(8,128)S(1)}, f32[3,128,256]{2,1,0:T(8,128)S(1)}, u32[]{:S(2)}, u32[]{:S(2)}) collective-permute-start(f32[3,128,256]{2,1,0:T(8,128)S(1)} %get-tuple-element.60), channel_id=1, source_target_pairs={{0,2},{1,3},{2,0},{3,1},{4,6},{5,7},{6,4},{7,5},{8,10},{9,11},{10,... | collective-permute-start | bytes 1179656 | tf_op jit(solution)/shard_map/ppermute | solution.py:167
  21.6 13.8 %collective-permute-start.8 = (f32[64,1024]{1,0:T(8,128)}, f32[64,1024]{1,0:T(8,128)}, u32[]{:S(2)}, u32[]{:S(2)}) collective-permute-start(f32[64,1024]{1,0:T(8,128)} %get-tuple-element.52), channel_id=1, source_target_pairs={{0,4},{4,0},{8,12},{12,8},{1,5},{5,1},{9,13},{13,9},{2,6},{6,2},{1... | collective-permute-start | bytes 786440 | tf_op jit(solution)/shard_map/ppermute | solution.py:200
  21.6 21.8 %collective-permute-start.9 = (f32[64,1024]{1,0:T(8,128)}, f32[64,1024]{1,0:T(8,128)}, u32[]{:S(2)}, u32[]{:S(2)}) collective-permute-start(f32[64,1024]{1,0:T(8,128)} %get-tuple-element.54), channel_id=1, source_target_pairs={{0,8},{4,12},{8,0},{12,4},{1,9},{5,13},{9,1},{13,5},{2,10},{6,14},... | collective-permute-start | bytes 786440 | tf_op jit(solution)/shard_map/ppermute | solution.py:200
  24.6 20.5 %collective-permute-start.10 = (f32[64,1024]{1,0:T(8,128)}, f32[64,1024]{1,0:T(8,128)}, u32[]{:S(2)}, u32[]{:S(2)}) collective-permute-start(f32[64,1024]{1,0:T(8,128)} %get-tuple-element.51), channel_id=1, source_target_pairs={{0,12},{4,8},{8,4},{12,0},{1,13},{5,9},{9,5},{13,1},{2,14},{6,10},... | collective-permute-start | bytes 786440 | tf_op jit(solution)/shard_map/ppermute | solution.py:200
  29.1 21.4 %collective-permute-start.7 = (f32[3,2,128,256]{3,2,0,1:T(8,128)}, f32[3,2,128,256]{3,2,0,1:T(8,128)}, u32[]{:S(2)}, u32[]{:S(2)}) collective-permute-start(f32[3,2,128,256]{3,2,0,1:T(8,128)} %maximum_select_fusion.2), channel_id=1, source_target_pairs={{0,1},{1,0},{2,3},{3,2},{4,5},{5,4},{6,7},{7,6},{8,9},{9,8},{10,11... | collective-permute-start | bytes 2359304 | tf_op jit(solution)/shard_map/ppermute | solution.py:167
  35.3 29.2 %collective-permute-start.11 = (f32[512,256]{1,0:T(8,128)}, f32[512,256]{1,0:T(8,128)S(1)}, u32[]{:S(2)}, u32[]{:S(2)}) collective-permute-start(f32[512,256]{1,0:T(8,128)} %get-tuple-element.37), channel_id=1, source_target_pairs={{0,4},{4,0},{8,12},{12,8},{1,5},{5,1},{9,13},{13,9},{2,6},{6,2},{1... | collective-permute-start | bytes 1572872 | tf_op jit(solution)/shard_map/ppermute | solution.py:200
  35.4 51.5 %collective-permute-start.17 = (f32[512,256]{1,0:T(8,128)}, f32[512,256]{1,0:T(8,128)S(1)}, u32[]{:S(2)}, u32[]{:S(2)}) collective-permute-start(f32[512,256]{1,0:T(8,128)} %get-tuple-element.29), channel_id=1, source_target_pairs={{0,4},{4,0},{8,12},{12,8},{1,5},{5,1},{9,13},{13,9},{2,6},{6,2},{1... | collective-permute-start | bytes 1572872 | tf_op jit(solution)/shard_map/ppermute | solution.py:200
  43.4 48.5 %collective-permute-start.18 = (f32[512,256]{1,0:T(8,128)}, f32[512,256]{1,0:T(8,128)S(1)}, u32[]{:S(2)}, u32[]{:S(2)}) collective-permute-start(f32[512,256]{1,0:T(8,128)} %get-tuple-element.43), channel_id=1, source_target_pairs={{0,8},{4,12},{8,0},{12,4},{1,9},{5,13},{9,1},{13,5},{2,10},{6,14},... | collective-permute-start | bytes 1572872 | tf_op jit(solution)/shard_map/ppermute | solution.py:200
  45.1 46.8 %collective-permute-start.19 = (f32[512,256]{1,0:T(8,128)}, f32[512,256]{1,0:T(8,128)S(1)}, u32[]{:S(2)}, u32[]{:S(2)}) collective-permute-start(f32[512,256]{1,0:T(8,128)} %get-tuple-element.28), channel_id=1, source_target_pairs={{0,12},{4,8},{8,4},{12,0},{1,13},{5,9},{9,5},{13,1},{2,14},{6,10},... | collective-permute-start | bytes 1572872 | tf_op jit(solution)/shard_map/ppermute | solution.py:200
  49.1 1.4 copy-start.10
  50.5 53.0 %collective-permute-start.14 = (f32[512,256]{1,0:T(8,128)S(1)}, f32[512,256]{1,0:T(8,128)S(1)}, u32[]{:S(2)}, u32[]{:S(2)}) collective-permute-start(f32[512,256]{1,0:T(8,128)S(1)} %copy-done.10), channel_id=1, source_target_pairs={{0,4},{4,0},{8,12},{12,8},{1,5},{5,1},{9,13},{13,9},{2,6},{6,2},{1... | collective-permute-start | bytes 1572872 | tf_op jit(solution)/shard_map/ppermute | solution.py:200
  54.2 10.3 %copy-start.9 = (f32[512,256]{1,0:T(8,128)S(1)}, f32[512,256]{1,0:T(8,128)}, u32[]{:S(2)}) copy-start(f32[512,256]{1,0:T(8,128)} %get-tuple-element.32) | copy-start | bytes 1572868
  54.2 32.6 %copy-start.8 = (f32[512,256]{1,0:T(8,128)S(1)}, f32[512,256]{1,0:T(8,128)}, u32[]{:S(2)}) copy-start(f32[512,256]{1,0:T(8,128)} %get-tuple-element.31) | copy-start | bytes 1572868
  64.5 85.6 %collective-permute-start.15 = (f32[512,256]{1,0:T(8,128)S(1)}, f32[512,256]{1,0:T(8,128)S(1)}, u32[]{:S(2)}, u32[]{:S(2)}) collective-permute-start(f32[512,256]{1,0:T(8,128)S(1)} %copy-done.9), channel_id=1, source_target_pairs={{0,8},{4,12},{8,0},{12,4},{1,9},{5,13},{9,1},{13,5},{2,10},{6,14},... | collective-permute-start | bytes 1572872 | tf_op jit(solution)/shard_map/ppermute | solution.py:200
  86.8 63.3 %collective-permute-start.16 = (f32[512,256]{1,0:T(8,128)S(1)}, f32[512,256]{1,0:T(8,128)S(1)}, u32[]{:S(2)}, u32[]{:S(2)}) collective-permute-start(f32[512,256]{1,0:T(8,128)S(1)} %copy-done.8), channel_id=1, source_target_pairs={{0,12},{4,8},{8,4},{12,0},{1,13},{5,9},{9,5},{13,1},{2,14},{6,10},... | collective-permute-start | bytes 1572872 | tf_op jit(solution)/shard_map/ppermute | solution.py:200
  89.1 1.0 copy-start
  89.2 2.6 copy-start.7
  89.3 2.6 copy-start.6
  91.9 103.2 %collective-permute-start.12 = (f32[512,256]{1,0:T(8,128)S(1)}, f32[512,256]{1,0:T(8,128)S(1)}, u32[]{:S(2)}, u32[]{:S(2)}) collective-permute-start(f32[512,256]{1,0:T(8,128)S(1)} %copy-done.7), channel_id=1, source_target_pairs={{0,8},{4,12},{8,0},{12,4},{1,9},{5,13},{9,1},{13,5},{2,10},{6,14},... | collective-permute-start | bytes 1572872 | tf_op jit(solution)/shard_map/ppermute | solution.py:200
  91.9 103.2 %collective-permute-start.13 = (f32[512,256]{1,0:T(8,128)S(1)}, f32[512,256]{1,0:T(8,128)S(1)}, u32[]{:S(2)}, u32[]{:S(2)}) collective-permute-start(f32[512,256]{1,0:T(8,128)S(1)} %copy-done.6), channel_id=1, source_target_pairs={{0,12},{4,8},{8,4},{12,0},{1,13},{5,9},{9,5},{13,1},{2,14},{6,10},... | collective-permute-start | bytes 1572872 | tf_op jit(solution)/shard_map/ppermute | solution.py:200
  93.6 10.0 %copy-start.5 = (f32[512,256]{1,0:T(8,128)S(1)}, f32[512,256]{1,0:T(8,128)}, u32[]{:S(2)}) copy-start(f32[512,256]{1,0:T(8,128)} %get-tuple-element.41) | copy-start | bytes 1572868
  93.6 56.6 %copy-start.4 = (f32[512,256]{1,0:T(8,128)S(1)}, f32[512,256]{1,0:T(8,128)}, u32[]{:S(2)}) copy-start(f32[512,256]{1,0:T(8,128)} %get-tuple-element.40) | copy-start | bytes 1572868
  93.6 56.6 %copy-start.3 = (f32[512,256]{1,0:T(8,128)S(1)}, f32[512,256]{1,0:T(8,128)}, u32[]{:S(2)}) copy-start(f32[512,256]{1,0:T(8,128)} %get-tuple-element.39) | copy-start | bytes 1572868
  103.6 101.4 %collective-permute-start = (f32[512,256]{1,0:T(8,128)S(1)}, f32[512,256]{1,0:T(8,128)S(1)}, u32[]{:S(2)}, u32[]{:S(2)}) collective-permute-start(f32[512,256]{1,0:T(8,128)S(1)} %copy-done.5), channel_id=1, source_target_pairs={{0,4},{4,0},{8,12},{12,8},{1,5},{5,1},{9,13},{13,9},{2,6},{6,2},{1... | collective-permute-start | bytes 1572872 | tf_op jit(solution)/shard_map/ppermute | solution.py:200
  150.2 67.4 %collective-permute-start.1 = (f32[512,256]{1,0:T(8,128)S(1)}, f32[512,256]{1,0:T(8,128)S(1)}, u32[]{:S(2)}, u32[]{:S(2)}) collective-permute-start(f32[512,256]{1,0:T(8,128)S(1)} %copy-done.4), channel_id=1, source_target_pairs={{0,8},{4,12},{8,0},{12,4},{1,9},{5,13},{9,1},{13,5},{2,10},{6,14},... | collective-permute-start | bytes 1572872 | tf_op jit(solution)/shard_map/ppermute | solution.py:200
  150.2 67.4 %collective-permute-start.2 = (f32[512,256]{1,0:T(8,128)S(1)}, f32[512,256]{1,0:T(8,128)S(1)}, u32[]{:S(2)}, u32[]{:S(2)}) collective-permute-start(f32[512,256]{1,0:T(8,128)S(1)} %copy-done.3), channel_id=1, source_target_pairs={{0,12},{4,8},{8,4},{12,0},{1,13},{5,9},{9,5},{13,1},{2,14},{6,10},... | collective-permute-start | bytes 1572872 | tf_op jit(solution)/shard_map/ppermute | solution.py:200
  228.8 24.9 %collective-permute-start.20 = (f32[4,2,136,256]{3,2,1,0:T(8,128)S(1)}, f32[4,2,136,256]{3,2,1,0:T(8,128)}, u32[]{:S(2)}, u32[]{:S(2)}) collective-permute-start(f32[4,2,136,256]{3,2,1,0:T(8,128)S(1)} %dynamic-slice_bitcast_fusion), channel_id=1, source_target_pairs={{0,1},{1,0},{2,3},{3,2},{4,5},{5,4},{6,7},{7,6},{8,9},{9,8},{10,11... | collective-permute-start | bytes 3342344 | tf_op jit(solution)/shard_map/ppermute | solution.py:185
  229.0 12.4 %collective-permute-start.27 = (f32[64,256]{1,0:T(8,128)S(1)}, f32[64,256]{1,0:T(8,128)S(1)}, u32[]{:S(2)}, u32[]{:S(2)}) collective-permute-start(f32[64,256]{1,0:T(8,128)S(1)} %get-tuple-element.75), channel_id=1, source_target_pairs={{0,4},{4,0},{8,12},{12,8},{1,5},{5,1},{9,13},{13,9},{2,6},{6,2},{1... | collective-permute-start | bytes 196616 | tf_op jit(solution)/shard_map/ppermute | solution.py:200
  238.6 8.5 %collective-permute-start.28 = (f32[64,256]{1,0:T(8,128)S(1)}, f32[64,256]{1,0:T(8,128)S(1)}, u32[]{:S(2)}, u32[]{:S(2)}) collective-permute-start(f32[64,256]{1,0:T(8,128)S(1)} %get-tuple-element.74), channel_id=1, source_target_pairs={{0,8},{4,12},{8,0},{12,4},{1,9},{5,13},{9,1},{13,5},{2,10},{6,14},... | collective-permute-start | bytes 196616 | tf_op jit(solution)/shard_map/ppermute | solution.py:200
  239.4 7.6 %collective-permute-start.29 = (f32[64,256]{1,0:T(8,128)S(1)}, f32[64,256]{1,0:T(8,128)S(1)}, u32[]{:S(2)}, u32[]{:S(2)}) collective-permute-start(f32[64,256]{1,0:T(8,128)S(1)} %get-tuple-element.73), channel_id=1, source_target_pairs={{0,12},{4,8},{8,4},{12,0},{1,13},{5,9},{9,5},{13,1},{2,14},{6,10},... | collective-permute-start | bytes 196616 | tf_op jit(solution)/shard_map/ppermute | solution.py:200
  247.1 1.0 copy-start.2
  248.1 4.9 %collective-permute-start.30 = (f32[64,256]{1,0:T(8,128)S(1)}, f32[64,256]{1,0:T(8,128)S(1)}, u32[]{:S(2)}, u32[]{:S(2)}) collective-permute-start(f32[64,256]{1,0:T(8,128)S(1)} %get-tuple-element.71), channel_id=1, source_target_pairs={{0,4},{4,0},{8,12},{12,8},{1,5},{5,1},{9,13},{13,9},{2,6},{6,2},{1... | collective-permute-start | bytes 196616 | tf_op jit(solution)/shard_map/ppermute | solution.py:200
  249.5 7.7 %collective-permute-start.31 = (f32[64,256]{1,0:T(8,128)S(1)}, f32[64,256]{1,0:T(8,128)S(1)}, u32[]{:S(2)}, u32[]{:S(2)}) collective-permute-start(f32[64,256]{1,0:T(8,128)S(1)} %get-tuple-element.70), channel_id=1, source_target_pairs={{0,8},{4,12},{8,0},{12,4},{1,9},{5,13},{9,1},{13,5},{2,10},{6,14},... | collective-permute-start | bytes 196616 | tf_op jit(solution)/shard_map/ppermute | solution.py:200
  250.7 7.1 %collective-permute-start.32 = (f32[64,256]{1,0:T(8,128)S(1)}, f32[64,256]{1,0:T(8,128)S(1)}, u32[]{:S(2)}, u32[]{:S(2)}) collective-permute-start(f32[64,256]{1,0:T(8,128)S(1)} %get-tuple-element.69), channel_id=1, source_target_pairs={{0,12},{4,8},{8,4},{12,0},{1,13},{5,9},{9,5},{13,1},{2,14},{6,10},... | collective-permute-start | bytes 196616 | tf_op jit(solution)/shard_map/ppermute | solution.py:200
  256.2 12.7 %collective-permute-start.21 = (f32[4,136,256]{2,1,0:T(8,128)}, f32[4,136,256]{2,1,0:T(8,128)S(1)}, u32[]{:S(2)}, u32[]{:S(2)}) collective-permute-start(f32[4,136,256]{2,1,0:T(8,128)} %dynamic-slice_bitcast_fusion.1), channel_id=1, source_target_pairs={{0,2},{1,3},{2,0},{3,1},{4,6},{5,7},{6,4},{7,5},{8,10},{9,11},{10,... | collective-permute-start | bytes 1671176 | tf_op jit(solution)/shard_map/ppermute | solution.py:185
  259.1 4.4 %collective-permute-start.33 = (f32[64,256]{1,0:T(8,128)S(1)}, f32[64,256]{1,0:T(8,128)S(1)}, u32[]{:S(2)}, u32[]{:S(2)}) collective-permute-start(f32[64,256]{1,0:T(8,128)S(1)} %get-tuple-element.67), channel_id=1, source_target_pairs={{0,4},{4,0},{8,12},{12,8},{1,5},{5,1},{9,13},{13,9},{2,6},{6,2},{1... | collective-permute-start | bytes 196616 | tf_op jit(solution)/shard_map/ppermute | solution.py:200
  260.0 6.1 %collective-permute-start.34 = (f32[64,256]{1,0:T(8,128)S(1)}, f32[64,256]{1,0:T(8,128)S(1)}, u32[]{:S(2)}, u32[]{:S(2)}) collective-permute-start(f32[64,256]{1,0:T(8,128)S(1)} %get-tuple-element.66), channel_id=1, source_target_pairs={{0,8},{4,12},{8,0},{12,4},{1,9},{5,13},{9,1},{13,5},{2,10},{6,14},... | collective-permute-start | bytes 196616 | tf_op jit(solution)/shard_map/ppermute | solution.py:200
  261.8 11.7 %collective-permute-start.35 = (f32[64,256]{1,0:T(8,128)S(1)}, f32[64,256]{1,0:T(8,128)S(1)}, u32[]{:S(2)}, u32[]{:S(2)}) collective-permute-start(f32[64,256]{1,0:T(8,128)S(1)} %get-tuple-element.65), channel_id=1, source_target_pairs={{0,12},{4,8},{8,4},{12,0},{1,13},{5,9},{9,5},{13,1},{2,14},{6,10},... | collective-permute-start | bytes 196616 | tf_op jit(solution)/shard_map/ppermute | solution.py:200
  269.0 8.4 %collective-permute-start.24 = (f32[136,256]{1,0:T(8,128)S(1)}, f32[136,256]{1,0:T(8,128)S(1)}, u32[]{:S(2)}, u32[]{:S(2)}) collective-permute-start(f32[136,256]{1,0:T(8,128)S(1)} %get-tuple-element.56), channel_id=1, source_target_pairs={{0,12},{4,8},{8,4},{12,0},{1,13},{5,9},{9,5},{13,1},{2,14},{6,10},... | collective-permute-start | bytes 417800 | tf_op jit(solution)/shard_map/ppermute | solution.py:200
  271.4 10.1 %collective-permute-start.23 = (f32[136,256]{1,0:T(8,128)S(1)}, f32[136,256]{1,0:T(8,128)S(1)}, u32[]{:S(2)}, u32[]{:S(2)}) collective-permute-start(f32[136,256]{1,0:T(8,128)S(1)} %get-tuple-element.57), channel_id=1, source_target_pairs={{0,8},{4,12},{8,0},{12,4},{1,9},{5,13},{9,1},{13,5},{2,10},{6,14},... | collective-permute-start | bytes 417800 | tf_op jit(solution)/shard_map/ppermute | solution.py:200
  271.8 9.8 %collective-permute-start.22 = (f32[136,256]{1,0:T(8,128)S(1)}, f32[136,256]{1,0:T(8,128)S(1)}, u32[]{:S(2)}, u32[]{:S(2)}) collective-permute-start(f32[136,256]{1,0:T(8,128)S(1)} %get-tuple-element.55), channel_id=1, source_target_pairs={{0,4},{4,0},{8,12},{12,8},{1,5},{5,1},{9,13},{13,9},{2,6},{6,2},{1... | collective-permute-start | bytes 417800 | tf_op jit(solution)/shard_map/ppermute | solution.py:200
  274.8 10.1 %collective-permute-start.36 = (f32[64,256]{1,0:T(8,128)S(1)}, f32[64,256]{1,0:T(8,128)S(1)}, u32[]{:S(2)}, u32[]{:S(2)}) collective-permute-start(f32[64,256]{1,0:T(8,128)S(1)} %get-tuple-element.63), channel_id=1, source_target_pairs={{0,4},{4,0},{8,12},{12,8},{1,5},{5,1},{9,13},{13,9},{2,6},{6,2},{1... | collective-permute-start | bytes 196616 | tf_op jit(solution)/shard_map/ppermute | solution.py:200
  281.6 5.0 %collective-permute-start.25 = (f32[128,256]{1,0:T(8,128)S(1)}, f32[128,256]{1,0:T(8,128)S(1)}, u32[]{:S(2)}, u32[]{:S(2)}) collective-permute-start(f32[128,256]{1,0:T(8,128)S(1)} %fusion.3), channel_id=1, source_target_pairs={{0,2},{1,3},{2,0},{3,1},{4,6},{5,7},{6,4},{7,5},{8,10},{9,11},{10,... | collective-permute-start | bytes 393224 | tf_op jit(solution)/shard_map/ppermute | solution.py:167
  282.3 6.4 %collective-permute-start.37 = (f32[64,256]{1,0:T(8,128)S(1)}, f32[64,256]{1,0:T(8,128)S(1)}, u32[]{:S(2)}, u32[]{:S(2)}) collective-permute-start(f32[64,256]{1,0:T(8,128)S(1)} %get-tuple-element.62), channel_id=1, source_target_pairs={{0,8},{4,12},{8,0},{12,4},{1,9},{5,13},{9,1},{13,5},{2,10},{6,14},... | collective-permute-start | bytes 196616 | tf_op jit(solution)/shard_map/ppermute | solution.py:200
  282.5 6.8 %collective-permute-start.38 = (f32[64,256]{1,0:T(8,128)S(1)}, f32[64,256]{1,0:T(8,128)S(1)}, u32[]{:S(2)}, u32[]{:S(2)}) collective-permute-start(f32[64,256]{1,0:T(8,128)S(1)} %get-tuple-element.61), channel_id=1, source_target_pairs={{0,12},{4,8},{8,4},{12,0},{1,13},{5,9},{9,5},{13,1},{2,14},{6,10},... | collective-permute-start | bytes 196616 | tf_op jit(solution)/shard_map/ppermute | solution.py:200
  286.7 3.3 %collective-permute-start.26 = (f32[2,128,256]{2,1,0:T(8,128)S(1)}, f32[2,128,256]{2,1,0:T(8,128)S(1)}, u32[]{:S(2)}, u32[]{:S(2)}) collective-permute-start(f32[2,128,256]{2,1,0:T(8,128)S(1)} %maximum_select_fusion.5), channel_id=1, source_target_pairs={{0,1},{1,0},{2,3},{3,2},{4,5},{5,4},{6,7},{7,6},{8,9},{9,8},{10,11... | collective-permute-start | bytes 786440 | tf_op jit(solution)/shard_map/ppermute | solution.py:167

commit v2 on v1

v2 whole, which is shorter than its diff:
```python
import functools

import jax
import jax.numpy as jnp
from jax import lax
from jax.experimental import pallas as pl
from jax.experimental.pallas import tpu as pltpu
from jax.sharding import PartitionSpec as P

INNER = 2
WIDTH = 256
PAD = 8
VMEM = 48 * 1024 * 1024
NT = (((1,), (1,)), ((), ()))


def xor_pairs(count, mask):
    return [(i, i ^ mask) for i in range(count)]


def split(value):
    high = value.astype(jnp.bfloat16)
    low = (value - high.astype(jnp.float32)).astype(jnp.bfloat16)
    return high, low


def dot(left, right):
    return jnp.dot(left, right, preferred_element_type=jnp.float32)


def dot3(left, right):
    return dot(left[0], right[0]) + (dot(left[0], right[1]) + dot(left[1], right[0]))


def dot_nt(left, right):
    return lax.dot_general(left, right, NT, preferred_element_type=jnp.float32)


def any_space(count):
    return [pl.BlockSpec(memory_space=pl.ANY)] * count


def vmem_space(count):
    return [pl.BlockSpec(memory_space=pltpu.VMEM)] * count


def cut_kernel(spec, *refs):
    owned, start, h_starts, width, masks, sources, w_mask = spec
    given, outs, sems = refs[:sources], refs[sources:-1], refs[-1]
    doc, feat = lax.axis_index("doc"), lax.axis_index("feat")
    copies = []
    for mask, out in zip(masks, outs):
        row = 0
        for ref, first in [(given[0], start)] + [(given[1], first) for first in h_starts]:
            rows = ref.shape[0]
            begin = pl.multiple_of((doc ^ mask) * owned + first, 128)
            copies.append((ref.at[:, pl.ds(begin, width)], out.at[pl.ds(row, rows), :]))
            row += rows
        if mask == w_mask:
            rows = out.shape[0] - row
            near = pl.multiple_of(feat * rows, 8)
            copies.append((given[2].at[pl.ds(near, rows), :], out.at[pl.ds(row, rows), :]))
    copies = [pltpu.make_async_copy(*pair, sems.at[i]) for i, pair in enumerate(copies)]
    for copy in copies:
        copy.start()
    for copy in copies:
        copy.wait()


def cut(given, owned, start, h_starts, width, masks, rows, w_mask, w_rows):
    spec = (owned, start, tuple(h_starts), width, tuple(masks), len(given), w_mask)
    count = (1 + len(h_starts)) * len(masks) + 1
    heights = [rows + w_rows * (mask == w_mask) for mask in masks]
    return pl.pallas_call(
        functools.partial(cut_kernel, spec),
        out_shape=[jax.ShapeDtypeStruct((height, width), jnp.float32) for height in heights],
        in_specs=any_space(len(given)),
        out_specs=vmem_space(len(masks)),
        scratch_shapes=[pltpu.SemaphoreType.DMA((count,))],
        cost_estimate=pl.CostEstimate(
            flops=0, bytes_accessed=8 * rows * width * len(masks), transcendentals=0
        ),
        name="cut_piece",
    )(*given)


def cut_plain(given, doc, feat, owned, start, h_starts, width, masks, rows, w_mask, w_rows):
    outs = []
    for mask in masks:
        begin = (doc ^ mask) * owned
        sources = [(given[0], start)] + [(given[1], first) for first in h_starts]
        parts = [lax.dynamic_slice(g, (0, begin + f), (g.shape[0], width)) for g, f in sources]
        if mask == w_mask:
            parts.append(lax.dynamic_slice_in_dim(given[2], feat * w_rows, w_rows, 0))
        outs.append(jnp.concatenate(parts, axis=0))
    return outs


def prepare_kernel(blocks, own_ref, *refs):
    part_refs, (high_ref, low_ref, high_t_ref, low_t_ref, sum_ref) = refs[:-5], refs[-5:]
    feat = lax.axis_index("feat")
    rows = own_ref.shape[0]
    part_rows = rows // len(part_refs)

    def place(value, row, count):
        near = pl.ds(row, count)
        high_ref[near, :], low_ref[near, :] = split(value)
        turned = value.T
        high_t_ref[:, near], low_t_ref[:, near] = split(turned)
        return jnp.sum(turned, axis=1, keepdims=True)

    total = place(own_ref[...], 0, rows)
    for mask, ref in enumerate(part_refs):
        at = (feat ^ mask) * part_rows
        for b in range(1, blocks):
            value = ref[(b - 1) * part_rows : b * part_rows, :]
            total = total + place(value, pl.multiple_of(b * rows + at, 128), part_rows)
    sum_ref[...] = total


def prepare(own, parts, blocks):
    rows, rank = own.shape
    docs = blocks * rows
    half = jnp.bfloat16
    shapes = [
        jax.ShapeDtypeStruct((docs, rank), half),
        jax.ShapeDtypeStruct((docs, rank), half),
        jax.ShapeDtypeStruct((rank, docs), half),
        jax.ShapeDtypeStruct((rank, docs), half),
        jax.ShapeDtypeStruct((rank, 1), jnp.float32),
    ]
    return pl.pallas_call(
        functools.partial(prepare_kernel, blocks),
        out_shape=shapes,
        in_specs=vmem_space(1 + len(parts)),
        out_specs=vmem_space(len(shapes)),
        compiler_params=pltpu.CompilerParams(vmem_limit_bytes=VMEM),
        cost_estimate=pl.CostEstimate(flops=0, bytes_accessed=docs * rank * 12, transcendentals=0),
        name="prepare_w",
    )(own, *parts)


def assemble(doc, h_blocks, h_ref):
    share = h_blocks[0].shape[0]
    for b, block in enumerate(h_blocks):
        h_ref[pl.ds(pl.multiple_of((doc ^ b) * share, 8), share), :] = block[...]
    return h_ref[...]


def ratio_of(m_ref, rows, weights, b, pair):
    near = slice(b * rows, (b + 1) * rows)
    return split(m_ref[:rows, :] / dot3((weights[0][near, :], weights[1][near, :]), pair))


def numerator(m_refs, rows, weights, which, pair, total):
    for m_ref, b in zip(m_refs, which):
        near = slice(b * rows, (b + 1) * rows)
        turned = (weights[2][:, near], weights[3][:, near])
        term = dot3(turned, ratio_of(m_ref, rows, weights, b, pair))
        total = term if total is None else total + term
    return total


def begin_kernel(blocks, rows, which, *refs):
    count = len(which)
    m_refs, h_blocks = refs[:count], refs[count : count + blocks]
    weights, total_ref, h_ref = refs[count + blocks : -2], refs[-2], refs[-1]
    factor = assemble(lax.axis_index("doc"), h_blocks, h_ref)
    total_ref[...] = numerator(m_refs, rows, weights, which, split(factor), None)


def piece_kernel(blocks, parts, rows, begun, first, *refs):
    m_refs, h_blocks = refs[:blocks], refs[blocks : 2 * blocks]
    weights, rest = refs[2 * blocks : 2 * blocks + 5], list(refs[2 * blocks + 5 :])
    begun_ref = rest.pop(0) if begun else None
    sums_in = (None, None) if first else (rest.pop(0), rest.pop(0))
    *back_refs, kept_out, sent_out, h_ref = rest
    width = h_ref.shape[1]
    share = h_blocks[0].shape[0]
    part_rows = rows // parts
    doc, feat = lax.axis_index("doc"), lax.axis_index("feat")
    even = (feat & 1) == 0

    factor = assemble(doc, h_blocks, h_ref)
    for step in range(INNER):
        pair = split(factor)
        which = [b for b in range(blocks) if step or b not in begun]
        total = begun_ref[...] if begun and not step else None
        total = numerator([m_refs[b] for b in which], rows, weights, which, pair, total)
        factor = factor * total / weights[4][...]
    h_ref[...] = factor
    for b in range(blocks):
        back_refs[b][...] = h_ref[pl.ds(pl.multiple_of((doc ^ b) * share, 8), share), :]
    pair = split(factor)
    ones = jnp.ones((PAD, width), jnp.bfloat16)
    row_sum = dot_nt(ones, pair[0]) + dot_nt(ones, pair[1])

    def put(b, half, near, left, right):
        kept, gone = jnp.where(even, left, right), jnp.where(even, right, left)
        for value, out, before in ((kept, kept_out, sums_in[0]), (gone, sent_out, sums_in[1])):
            out[b, half, near, :] = value if first else before[b, half, near, :] + value

    for b in range(blocks):
        high, low = ratio_of(m_refs[b], rows, weights, b, pair)
        term = dot_nt(high, pair[0]) + (dot_nt(high, pair[1]) + dot_nt(low, pair[0]))
        for half in range(parts // 2):
            at = 2 * half * part_rows
            left, right = term[at : at + part_rows, :], term[at + part_rows : at + 2 * part_rows, :]
            put(b, half, slice(0, part_rows), left, right)
            put(b, half, slice(part_rows, part_rows + PAD), row_sum, row_sum)


def update_piece(m_blocks, h_blocks, rows, weights, sums, parts, early):
    blocks = len(m_blocks)
    width = m_blocks[0].shape[1]
    rank = weights[0].shape[1]
    share = rank // blocks
    first = sums is None
    half_shape = jax.ShapeDtypeStruct((blocks, parts // 2, rows // parts + PAD, rank), jnp.float32)
    back_shape = jax.ShapeDtypeStruct((share, width), jnp.float32)
    total_shape = jax.ShapeDtypeStruct((rank, width), jnp.float32)
    extra = {
        "scratch_shapes": [pltpu.VMEM((rank, width), jnp.float32)],
        "compiler_params": pltpu.CompilerParams(vmem_limit_bytes=VMEM),
    }

    def cost(dots):
        return pl.CostEstimate(
            flops=2 * dots * blocks * rows * width * rank,
            bytes_accessed=blocks * rows * (4 * width + 16 * rank),
            transcendentals=0,
        )

    begun = []
    if early:
        begun = [
            pl.pallas_call(
                functools.partial(begin_kernel, blocks, rows, early),
                out_shape=total_shape,
                in_specs=vmem_space(len(early) + blocks + 5),
                out_specs=vmem_space(1)[0],
                cost_estimate=cost(6),
                name="begin_piece",
                **extra,
            )(*[m_blocks[b] for b in early], *h_blocks, *weights)
        ]
    sums = [] if first else list(sums)
    given = [*m_blocks, *h_blocks, *weights, *begun, *sums]
    *backs, kept, sent = pl.pallas_call(
        functools.partial(piece_kernel, blocks, parts, rows, early, first),
        out_shape=[back_shape] * blocks + [half_shape] * 2,
        in_specs=vmem_space(len(given)),
        out_specs=vmem_space(blocks + 2),
        input_output_aliases={} if first else {len(given) - 2 + i: blocks + i for i in range(2)},
        cost_estimate=cost(15),
        name="update_piece",
        **extra,
    )(*given)
    return backs, (kept, sent)


def update_plain(m_blocks, h_blocks, rows, whole_w, sums, parts, doc, feat):
    highest = lax.Precision.HIGHEST
    blocks, rank = len(m_blocks), whole_w.shape[1]
    share, width = rank // blocks, m_blocks[0].shape[1]
    whole_m = jnp.concatenate([m[:rows] for m in m_blocks], axis=0)
    factor = jnp.zeros((rank, width), jnp.float32)
    for k in range(blocks):
        factor = lax.dynamic_update_slice(factor, h_blocks[k], ((doc ^ k) * share, 0))
    column = jnp.sum(whole_w, axis=0)[:, None]
    for _ in range(INNER):
        ratio = whole_m / jnp.dot(whole_w, factor, precision=highest)
        numer = lax.dot_general(whole_w, ratio, (((0,), (0,)), ((), ())), precision=highest)
        factor = factor * numer / column
    ratio = whole_m / jnp.dot(whole_w, factor, precision=highest)
    wnumer = lax.dot_general(ratio, factor, NT, precision=highest)
    wnumer = wnumer.reshape(blocks, parts, rows // parts, rank)
    row_sum = jnp.broadcast_to(jnp.sum(factor, axis=1), (blocks, parts, PAD, rank))
    more = jnp.concatenate([wnumer, row_sum], axis=2)
    more = more.reshape(blocks, parts // 2, 2, *more.shape[2:])
    halves = [lax.dynamic_index_in_dim(more, (feat & 1) ^ i, 2, keepdims=False) for i in range(2)]
    if sums is not None:
        halves = [old + new for old, new in zip(sums, halves)]
    backs = [lax.dynamic_slice_in_dim(factor, (doc ^ k) * share, share, 0) for k in range(blocks)]
    return backs, halves


def spread_feat(value, bits):
    got = {0: value}
    for j in reversed(range(bits)):
        for mask, held in list(got.items()):
            pairs = xor_pairs(1 << bits, 1 << j)
            got[mask | 1 << j] = lax.ppermute(held, "feat", pairs)
    return [got[mask] for mask in range(1 << bits)]


def in_order(parts, feat):
    rows = parts[0].shape[0]
    whole = jnp.zeros((rows * len(parts), *parts[0].shape[1:]), parts[0].dtype)
    for mask, part in enumerate(parts):
        whole = lax.dynamic_update_slice_in_dim(whole, part, (feat ^ mask) * rows, 0)
    return whole


def add_feat(kept, sent, bits, feat):
    held = [kept, lax.ppermute(sent, "feat", xor_pairs(1 << bits, 1))]
    shape = kept.shape
    held = [h.reshape((shape[0],) + (2,) * (bits - 1) + shape[2:]) for h in held]
    for j in range(1, bits):
        bit = (feat >> j) & 1
        axis = bits - j

        def half(side):
            return sum(lax.dynamic_index_in_dim(h, side, axis, keepdims=False) for h in held)

        other = lax.ppermute(half(1 - bit), "feat", xor_pairs(1 << bits, 1 << j))
        held = [half(bit), other]
    return held


def after(value, earlier):
    return lax.optimization_barrier((value, *earlier))[0] if earlier else value


def piece_widths(owned):
    return [owned] if owned % WIDTH else [WIDTH] * (owned // WIDTH)


def body(n_doc, n_feat, matrix, doc_factor, feat_factor):
    doc, feat = lax.axis_index("doc"), lax.axis_index("feat")
    bits = n_feat.bit_length() - 1
    rows, columns = matrix.shape
    share, rank = feat_factor.shape[0], doc_factor.shape[1]
    owned = columns // n_doc
    widths = piece_widths(owned)
    pieces = len(widths)
    starts = [sum(widths[:p]) for p in range(pieces)]
    part_rows = rows // n_feat
    others = list(range(n_doc - 1, 0, -1))
    in_kernel = n_doc * rows * rank * 32 < VMEM and widths[0] % 128 == 0 and part_rows % 128 == 0
    w_rides = widths[0] == rank

    def send(value, k):
        return lax.ppermute(value, "doc", xor_pairs(n_doc, k)) if k else value

    riders = [[0, 1][:pieces]] + [[p + 1] if p + 1 < pieces else [] for p in range(1, pieces)]
    w_row = rows + share * len(riders[0])

    def m_piece(p, *earlier):
        given = [after(matrix, earlier), feat_factor]
        height = rows + share * len(riders[p])
        w_mask = n_doc // 2 if w_rides and p == 0 else -1
        given += [doc_factor] if w_mask > 0 else []
        masks = [*others, 0]
        place = (owned, starts[p], [starts[q] for q in riders[p]], widths[p], masks, height)
        place += (w_mask, part_rows)
        arrays = cut(given, *place) if in_kernel else cut_plain(given, doc, feat, *place)
        got = {k: send(piece, k) for k, piece in zip(masks, arrays)}
        return [got[k] for k in range(n_doc)]

    m_pieces = []
    for p in range(pieces):
        gate = m_pieces[p - 2][1:] if p > 1 else m_pieces[0][1:2] if p else []
        m_pieces.append(m_piece(p, *gate))

    w_part = lax.dynamic_slice_in_dim(doc_factor, feat * part_rows, part_rows, 0)
    far = n_doc // 2
    got = {0: w_part, far: m_pieces[0][far][w_row:] if w_rides else send(w_part, far)}
    while far > 1:
        far //= 2
        got |= {mask | far: send(held, far) for mask, held in got.items()}
    w_parts = [got[k] for k in range(1, n_doc)]
    w_parts = spread_feat(jnp.concatenate(w_parts, axis=0), bits)
    if in_kernel:
        weights = prepare(doc_factor, w_parts, n_doc)
    else:
        w_parts = [w.reshape(n_doc - 1, part_rows, rank).swapaxes(0, 1) for w in w_parts]
        w_others = in_order(w_parts, feat).swapaxes(0, 1).reshape(-1, rank)
        whole_w = jnp.concatenate([doc_factor, w_others], axis=0)

    sums = None
    backs = []
    for p in range(pieces):
        source = 0 if p < 2 else p - 1
        at = rows + share * (p == 1)
        ready = backs[-1][:1] if backs else []
        h_blocks = [after(m[at : at + share], ready) for m in m_pieces[source]]
        place = (m_pieces[p], h_blocks, rows)
        if in_kernel:
            early = list(range(n_doc - 1)) if p and p == pieces - 1 else []
            rows_back, sums = update_piece(*place, weights, sums, n_feat, early)
        else:
            rows_back, sums = update_plain(*place, whole_w, sums, n_feat, doc, feat)
        backs.append(rows_back)

    kept, other = add_feat(*sums, bits, feat)
    batches = [b for b in (backs[:-1], backs[-1:]) if b]

    def give_back(batch, *earlier):
        rows_of = [jnp.concatenate([b[k] for b in batch], axis=0) for k in range(n_doc)]
        return [send(after(r, earlier), k) for k, r in enumerate(rows_of)]

    returned = [give_back(b) for b in batches[:-1]]
    kept = after(kept, [r for rows_of in returned for r in rows_of[1:]])
    total = kept[0] + other[0]
    for k in range(1, n_doc):
        total = total + send(kept[k] + other[k], k)
    returned.append(give_back(batches[-1], total))
    new_part = w_part * total[:part_rows] / total[part_rows]
    new_parts = spread_feat(new_part, bits)
    new_doc = in_order(new_parts, feat)
    new_feat = jnp.zeros((share, columns), jnp.float32)
    start = 0
    for batch, rows_of in zip(batches, returned):
        for k, value in enumerate(rows_of):
            value = value.reshape(len(batch), share, -1).swapaxes(0, 1).reshape(share, -1)
            value = after(value, new_parts[-1:])
            new_feat = lax.dynamic_update_slice(new_feat, value, (0, (doc ^ k) * owned + start))
        start += value.shape[1]
    return new_doc, new_feat


def solution(mesh):
    placed = (P(("grp", "doc"), "feat"), P(("grp", "doc"), None), P(("grp", "doc"), "feat"))
    return jax.shard_map(
        functools.partial(body, mesh.shape["doc"], mesh.shape["feat"]),
        mesh=mesh,
        in_specs=placed,
        out_specs=(P(("grp", "doc"), None), P(("grp", "doc"), "feat")),
        check_vma=False,
    )
```

time: 291 us -> 281 us (0.966)
  waiting for transfers between devices: 160 us -> 134 us
  Pallas kernels: 40.7 us -> 57.2 us
  starting transfers between devices: 56.9 us -> 72.8 us
  local copies, waits for them, and re-layouts: 27.9 us -> 12.3 us
    ppermute x33 -> x23, waiting for transfers between devices: 154 us -> 131 us  [send(): return lax.ppermute(value, 'doc', xor_pairs(n_doc, k)) if k else value]
    pallas_call x4 -> x9, Pallas kernels: 39 us -> 55.5 us  [the longest x4 39.6 us: update_piece(): pl.pallas_call(functools.partial(piece_kernel, blocks, parts, rows, early...]
    ppermute x33 -> x23, starting transfers between devices: 54.6 us -> 68.5 us  [send(): return lax.ppermute(value, 'doc', xor_pairs(n_doc, k)) if k else value]
    dynamic_update_slice x15 -> x11, local copies, waits for them, and re-layouts: 10.7 us -> 0.18 us  [the longest x8 0.13 us: body(): lax.dynamic_update_slice(new_feat, value, (0, (doc ^ k) * owned + start))]
    dynamic_slice x6 -> x0, local copies, waits for them, and re-layouts: 8.49 us -> none  [the longest x1 6.16 us: m_piece(): lax.dynamic_slice(matrix, (0, (doc ^ k) * owned + p * width), (rows, width))]
    slice x5 -> x13, local copies, waits for them, and re-layouts: 1.54 us -> 8.54 us  [the longest x12 8.53 us: body(): h_blocks = [after(m[at:at + share], ready) for m in m_pieces[source]]]
  transfers between devices with their start and end apart: 39 -> 31, of which waited for: 20 -> 11; matrix products, arithmetic and copies ran while one was open for 9% -> 4% of each run, Pallas kernels for 11% -> 16%
where the time goes in v2:
time: 281 us; the launch traced here: 280 us
  waiting for transfers between devices  134 us (48%)
  starting transfers between devices  72.8 us (26%)
  Pallas kernels  57.2 us (20%)
  local copies, waits for them, and re-layouts  12.3 us (4%)
  other arithmetic  2.95 us (1%)
    ppermute x23, waiting for transfers between devices, send(): return lax.ppermute(value, 'doc', xor_pairs(n_doc, k)) if k else value  131 us
    ppermute x23, starting transfers between devices, send(): return lax.ppermute(value, 'doc', xor_pairs(n_doc, k)) if k else value  68.5 us
    pallas_call x4, Pallas kernels, update_piece(): pl.pallas_call(functools.partial(piece_kernel, blocks, parts, rows, early...  39.6 us
    pallas_call x4, Pallas kernels, cut(): pl.pallas_call(functools.partial(cut_kernel, spec), out_shape=[jax.ShapeD...  12.7 us
    slice x12, local copies, waits for them, and re-layouts, body(): h_blocks = [after(m[at:at + share], ready) for m in m_pieces[source]]  8.53 us
  transfers between devices with their start and end apart: 31, of which 11 were waited for; matrix products, arithmetic and copies ran while one was open for 4% of the time, Pallas kernels for 16%

profile of v2, /device:TPU:0, one launch (start us, length us, event | category | flops | bytes accessed | tf_op | source)
XLA Modules:
  0.0 280.2 jit_solution(817514520130417105)
XLA Ops:
  0.6 3.4 %cut_piece.4 = (f32[640,256]{1,0:T(8,128)}, f32[768,256]{1,0:T(8,128)}, f32[640,256]{1,0:T(8,128)}, f32[640,256]{1,0:T(8,128)}) custom-call(f32[512,4096]{1,0:T(8,128)} %refs_0_.4, f32[64,4096]{1,0:T(8,128)} %refs_1_.7, f32[512,256]{1,0:T(8,128)} %own_ref.1), custom_call_target="tpu_custom_call" | custom-call | bytes 5242880 | tf_op jit(solution)/shard_map/cut_piece/pallas_call | solution.py:74
  4.0 4.1 %collective-permute-start.7 = (f32[768,256]{1,0:T(8,128)}, f32[768,256]{1,0:T(8,128)S(1)}, u32[]{:S(2)}, u32[]{:S(2)}) collective-permute-start(f32[768,256]{1,0:T(8,128)} %get-tuple-element.85), channel_id=1, source_target_pairs={{0,8},{4,12},{8,0},{12,4},{1,9},{5,13},{9,1},{13,5},{2,10},{6,14},... | collective-permute-start | bytes 2359304 | tf_op jit(solution)/shard_map/ppermute | solution.py:344
  8.1 1.6 collective-permute-start
  9.7 30.8 %collective-permute-done.refs_1_ = f32[640,256]{1,0:T(8,128)S(1)} collective-permute-done((f32[640,256]{1,0:T(8,128)}, f32[640,256]{1,0:T(8,128)S(1)}, u32[]{:S(2)}, u32[]{:S(2)}) %collective-permute-start) | collective-permute-done | bytes 655392 | tf_op jit(solution)/shard_map/ppermute | solution.py:344
  40.5 3.4 %cut_piece.5 = (f32[576,256]{1,0:T(8,128)}, f32[576,256]{1,0:T(8,128)}, f32[576,256]{1,0:T(8,128)}, f32[576,256]{1,0:T(8,128)}) custom-call(f32[512,4096]{1,0:T(8,128)} %refs_0_.4, f32[64,4096]{1,0:T(8,128)} %refs_1_.7), custom_call_target="tpu_custom_call" | custom-call | bytes 4718592 | tf_op jit(solution)/shard_map/cut_piece/pallas_call | solution.py:74
  43.9 2.4 collective-permute-start.1
  46.3 1.9 collective-permute-start.12
  48.3 9.4 %collective-permute-done.7.refs_2_ = f32[768,256]{1,0:T(8,128)S(1)} collective-permute-done((f32[768,256]{1,0:T(8,128)}, f32[768,256]{1,0:T(8,128)S(1)}, u32[]{:S(2)}, u32[]{:S(2)}) %collective-permute-start.7) | collective-permute-done | bytes 786464 | tf_op jit(solution)/shard_map/ppermute | solution.py:344
  57.6 0.2 collective-permute-start.13
  57.8 24.8 %collective-permute-done.12 = f32[128,256]{1,0:T(8,128)S(1)} collective-permute-done((f32[128,256]{1,0:T(8,128)S(1)}, f32[128,256]{1,0:T(8,128)S(1)}, u32[]{:S(2)}, u32[]{:S(2)}) %collective-permute-start.12) | collective-permute-done | bytes 131104 | tf_op jit(solution)/shard_map/ppermute | solution.py:344
  82.6 1.3 collective-permute-start.3
  83.9 1.5 collective-permute-done.13
  85.4 1.6 collective-permute-start.15
  87.0 0.9 fusion.13
  87.9 0.8 slice.82.refs_4_
  88.7 3.1 %cut_piece.7 = (f32[576,256]{1,0:T(8,128)}, f32[576,256]{1,0:T(8,128)}, f32[576,256]{1,0:T(8,128)}, f32[576,256]{1,0:T(8,128)}) custom-call(f32[512,4096]{1,0:T(8,128)} %refs_0_.4, f32[64,4096]{1,0:T(8,128)} %refs_1_.7), custom_call_target="tpu_custom_call" | custom-call | bytes 4718592 | tf_op jit(solution)/shard_map/cut_piece/pallas_call | solution.py:74
  91.8 2.3 collective-permute-start.10
  94.1 2.6 collective-permute-start.11
  96.7 38.2 %collective-permute-done.2.refs_2_ = f32[576,256]{1,0:T(8,128)} collective-permute-done((f32[576,256]{1,0:T(8,128)}, f32[576,256]{1,0:T(8,128)}, u32[]{:S(2)}, u32[]{:S(2)}) %collective-permute-start.2) | collective-permute-done | bytes 589856 | tf_op jit(solution)/shard_map/ppermute | solution.py:344
  135.1 0.5 collective-permute-start.16
  135.6 0.9 fusion.11
  136.5 0.8 slice.81.refs_3_.refs_4_
  137.3 2.9 %cut_piece.6 = (f32[512,256]{1,0:T(8,128)}, f32[512,256]{1,0:T(8,128)}, f32[512,256]{1,0:T(8,128)}, f32[512,256]{1,0:T(8,128)}) custom-call(f32[512,4096]{1,0:T(8,128)} %refs_0_.4, f32[64,4096]{1,0:T(8,128)} %refs_1_.7), custom_call_target="tpu_custom_call" | custom-call | bytes 4194304 | tf_op jit(solution)/shard_map/cut_piece/pallas_call | solution.py:74
  140.2 0.8 slice.117.refs_7_
  141.1 0.8 slice.116.refs_6_
  141.9 0.8 slice.115.refs_5_
  142.8 30.0 %collective-permute-start.4 = (f32[512,256]{1,0:T(8,128)}, f32[512,256]{1,0:T(8,128)S(1)}, u32[]{:S(2)}, u32[]{:S(2)}) collective-permute-start(f32[512,256]{1,0:T(8,128)} %get-tuple-element.82), channel_id=1, source_target_pairs={{0,4},{4,0},{8,12},{12,8},{1,5},{5,1},{9,13},{13,9},{2,6},{6,2},{1... | collective-permute-start | bytes 1572872 | tf_op jit(solution)/shard_map/ppermute | solution.py:344
  172.8 0.8 slice.120.refs_6_.refs_7_
  173.7 1.9 collective-permute-start.5
  175.6 0.8 slice.119.refs_5_.refs_6_
  176.5 1.5 collective-permute-start.6
  178.0 0.8 slice.118.refs_4_.refs_5_
  178.8 1.8 prepare_w.1
  180.6 1.0 copy-done.1
  181.6 9.8 %update_piece.4 = (f32[64,256]{1,0:T(8,128)S(1)}, f32[64,256]{1,0:T(8,128)S(1)}, f32[64,256]{1,0:T(8,128)S(1)}, f32[64,256]{1,0:T(8,128)S(1)}, f32[4,2,136,256]{3,2,1,0:T(8,128)}, /*index=5*/f32[4,2,136,256]{3,2,1,0:T(8,128)}) custom-call(f32[640,256]{1,0:T(8,128)S(1)} %copy-done.4, f32[640,256]{1,0:T(8,128)S(1)} %copy-done.6, ...), custom_call_target="tpu_custom_call" | custom-call | flops 4026531840 | bytes 10485760 | tf_op jit(solution)/shard_map/update_piece/pallas_call | solution.py:249
  191.4 10.7 %update_piece.5 = (f32[64,256]{1,0:T(8,128)S(1)}, f32[64,256]{1,0:T(8,128)S(1)}, f32[64,256]{1,0:T(8,128)S(1)}, f32[64,256]{1,0:T(8,128)S(1)}, f32[4,2,136,256]{3,2,1,0:T(8,128)}, /*index=5*/f32[4,2,136,256]{3,2,1,0:T(8,128)}) custom-call(f32[576,256]{1,0:T(8,128)S(1)} %copy-done.7, ...), custom_call_target="tpu_custom_call", output_to_operand_aliasing={{4}: (13, {}), {5}: (14, {})} | custom-call | flops 4026531840 | bytes 10485760 | tf_op jit(solution)/shard_map/update_piece/pallas_call | solution.py:249
  202.1 10.5 %update_piece.6 = (f32[64,256]{1,0:T(8,128)S(1)}, f32[64,256]{1,0:T(8,128)S(1)}, f32[64,256]{1,0:T(8,128)S(1)}, f32[64,256]{1,0:T(8,128)S(1)}, f32[4,2,136,256]{3,2,1,0:T(8,128)}, /*index=5*/f32[4,2,136,256]{3,2,1,0:T(8,128)}) custom-call(f32[576,256]{1,0:T(8,128)S(1)} %copy-done.8, ...), custom_call_target="tpu_custom_call", output_to_operand_aliasing={{4}: (13, {}), {5}: (14, {})} | custom-call | flops 4026531840 | bytes 10485760 | tf_op jit(solution)/shard_map/update_piece/pallas_call | solution.py:249
  212.6 3.1 %begin_piece.1.refs_13_ = f32[256,256]{1,0:T(8,128)S(1)} custom-call(f32[512,256]{1,0:T(8,128)S(1)} %copy-done.3, f32[512,256]{1,0:T(8,128)S(1)} %collective-permute-done.4.refs_1_, f32[512,256]{1,0:T(8,128)S(1)} %collective-permute-done.5.refs_2_, f32[64,256]{1,0:T(8,128)S(1)} %slice.81.refs_3_.refs_4_, f32[64,256]{1,0:T(8,128)S(1)} %slice.118.refs_4_.refs_5_, ...), custom_call_target="tpu_custom_call" | custom-call | flops 1610612736 | bytes 10485760 | tf_op jit(solution)/shard_map/begin_piece/pallas_call | solution.py:237
  215.7 8.7 %update_piece.7 = (f32[64,256]{1,0:T(8,128)S(1)}, f32[64,256]{1,0:T(8,128)S(1)}, f32[64,256]{1,0:T(8,128)S(1)}, f32[64,256]{1,0:T(8,128)S(1)}, f32[4,2,136,256]{3,2,1,0:T(8,128)}, /*index=5*/f32[4,2,136,256]{3,2,1,0:T(8,128)}) custom-call(f32[512,256]{1,0:T(8,128)S(1)} %copy-done.3, ...), custom_call_target="tpu_custom_call", output_to_operand_aliasing={{4}: (14, {}), {5}: (15, {})} | custom-call | flops 4026531840 | bytes 10485760 | tf_op jit(solution)/shard_map/update_piece/pallas_call | solution.py:249
  224.4 3.0 %collective-permute-done.17 = f32[4,2,136,256]{3,2,1,0:T(8,128)S(1)} collective-permute-done((f32[4,2,136,256]{3,2,1,0:T(8,128)}, f32[4,2,136,256]{3,2,1,0:T(8,128)S(1)}, u32[]{:S(2)}, u32[]{:S(2)}) %collective-permute-start.17) | collective-permute-done | bytes 1114144 | tf_op jit(solution)/shard_map/ppermute | solution.py:306
  227.3 1.6 add_bitcast_fusion
  228.9 1.5 collective-permute-start.21
  230.5 2.9 %collective-permute-start.20 = (f32[192,256]{1,0:T(8,128)S(1)}, f32[192,256]{1,0:T(8,128)S(1)}, u32[]{:S(2)}, u32[]{:S(2)}) collective-permute-start(f32[192,256]{1,0:T(8,128)S(1)} %pad_maximum_fusion.3), channel_id=1, source_target_pairs={{0,12},{4,8},{8,4},{12,0},{1,13},{5,9},{9,5},{13,1},{2,14},{6,10},... | collective-permute-start | bytes 589832 | tf_op jit(solution)/shard_map/ppermute | solution.py:344
  233.4 6.1 %collective-permute-start.19 = (f32[192,256]{1,0:T(8,128)S(1)}, f32[192,256]{1,0:T(8,128)S(1)}, u32[]{:S(2)}, u32[]{:S(2)}) collective-permute-start(f32[192,256]{1,0:T(8,128)S(1)} %pad_maximum_fusion.2), channel_id=1, source_target_pairs={{0,8},{4,12},{8,0},{12,4},{1,9},{5,13},{9,1},{13,5},{2,10},{6,14},... | collective-permute-start | bytes 589832 | tf_op jit(solution)/shard_map/ppermute | solution.py:344
  239.5 0.6 collective-permute-start.18
  240.2 1.1 fusion
  241.3 11.5 %collective-permute-done.19 = f32[192,256]{1,0:T(8,128)S(1)} collective-permute-done((f32[192,256]{1,0:T(8,128)S(1)}, f32[192,256]{1,0:T(8,128)S(1)}, u32[]{:S(2)}, u32[]{:S(2)}) %collective-permute-start.19) | collective-permute-done | bytes 196640 | tf_op jit(solution)/shard_map/ppermute | solution.py:344
  252.8 0.1 collective-permute-start.22
  252.9 3.2 %collective-permute-start.23 = (f32[136,256]{1,0:T(8,128)S(1)}, f32[136,256]{1,0:T(8,128)S(1)}, u32[]{:S(2)}, u32[]{:S(2)}) collective-permute-start(f32[136,256]{1,0:T(8,128)S(1)} %get-tuple-element.152), channel_id=1, source_target_pairs={{0,8},{4,12},{8,0},{12,4},{1,9},{5,13},{9,1},{13,5},{2,10},{6,14},... | collective-permute-start | bytes 417800 | tf_op jit(solution)/shard_map/ppermute | solution.py:344
  256.1 1.2 collective-permute-start.24
  257.3 2.8 %collective-permute-done.22 = f32[136,256]{1,0:T(8,128)S(1)} collective-permute-done((f32[136,256]{1,0:T(8,128)S(1)}, f32[136,256]{1,0:T(8,128)S(1)}, u32[]{:S(2)}, u32[]{:S(2)}) %collective-permute-start.22) | collective-permute-done | bytes 139296 | tf_op jit(solution)/shard_map/ppermute | solution.py:344
  260.1 6.0 %collective-permute-done.23 = f32[136,256]{1,0:T(8,128)S(1)} collective-permute-done((f32[136,256]{1,0:T(8,128)S(1)}, f32[136,256]{1,0:T(8,128)S(1)}, u32[]{:S(2)}, u32[]{:S(2)}) %collective-permute-start.23) | collective-permute-done | bytes 139296 | tf_op jit(solution)/shard_map/ppermute | solution.py:344
  266.3 0.6 collective-permute-start.26
  267.0 0.1 copy.19
  267.2 0.1 copy.22
  267.3 0.1 copy.21
  267.5 0.1 copy.20
  267.7 2.5 collective-permute-start.30
  270.2 1.2 collective-permute-start.29
  271.4 0.8 collective-permute-start.28
  272.2 2.0 collective-permute-done.30
  274.2 3.9 %collective-permute-done.29 = f32[64,256]{1,0:T(8,128)S(1)} collective-permute-done((f32[64,256]{1,0:T(8,128)S(1)}, f32[64,256]{1,0:T(8,128)S(1)}, u32[]{:S(2)}, u32[]{:S(2)}) %collective-permute-start.29) | collective-permute-done | bytes 65568 | tf_op jit(solution)/shard_map/ppermute | solution.py:344
  278.4 0.9 copy-done.11
  279.4 0.8 copy-done.12
  (80 shorter events, 0.9 us)
Async XLA Ops:
  4.0 53.6 %collective-permute-start.7 = (f32[768,256]{1,0:T(8,128)}, f32[768,256]{1,0:T(8,128)S(1)}, u32[]{:S(2)}, u32[]{:S(2)}) collective-permute-start(f32[768,256]{1,0:T(8,128)} %get-tuple-element.85), channel_id=1, source_target_pairs={{0,8},{4,12},{8,0},{12,4},{1,9},{5,13},{9,1},{13,5},{2,10},{6,14},... | collective-permute-start | bytes 2359304 | tf_op jit(solution)/shard_map/ppermute | solution.py:344
  8.1 32.3 %collective-permute-start = (f32[640,256]{1,0:T(8,128)}, f32[640,256]{1,0:T(8,128)S(1)}, u32[]{:S(2)}, u32[]{:S(2)}) collective-permute-start(f32[640,256]{1,0:T(8,128)} %get-tuple-element.75), channel_id=1, source_target_pairs={{0,4},{4,0},{8,12},{12,8},{1,5},{5,1},{9,13},{13,9},{2,6},{6,2},{1... | collective-permute-start | bytes 1966088 | tf_op jit(solution)/shard_map/ppermute | solution.py:344
  9.7 79.1 %collective-permute-start.8 = (f32[640,256]{1,0:T(8,128)}, f32[640,256]{1,0:T(8,128)}, u32[]{:S(2)}, u32[]{:S(2)}) collective-permute-start(f32[640,256]{1,0:T(8,128)} %get-tuple-element.86), channel_id=1, source_target_pairs={{0,12},{4,8},{8,4},{12,0},{1,13},{5,9},{9,5},{13,1},{2,14},{6,10},... | collective-permute-start | bytes 1966088 | tf_op jit(solution)/shard_map/ppermute | solution.py:344
  9.7 36.6 %copy-start = (f32[512,256]{1,0:T(8,128)S(1)}, f32[512,256]{1,0:T(8,128)}, u32[]{:S(2)}) copy-start(f32[512,256]{1,0:T(8,128)} %own_ref.1) | copy-start | bytes 1572868
  40.5 94.5 %copy-start.5 = (f32[640,256]{1,0:T(8,128)}, f32[640,256]{1,0:T(8,128)S(1)}, u32[]{:S(2)}) copy-start(f32[640,256]{1,0:T(8,128)S(1)} %collective-permute-done.refs_1_) | copy-start | bytes 1966084
  43.9 50.2 %collective-permute-start.1 = (f32[576,256]{1,0:T(8,128)}, f32[576,256]{1,0:T(8,128)}, u32[]{:S(2)}, u32[]{:S(2)}) collective-permute-start(f32[576,256]{1,0:T(8,128)} %get-tuple-element.77), channel_id=1, source_target_pairs={{0,4},{4,0},{8,12},{12,8},{1,5},{5,1},{9,13},{13,9},{2,6},{6,2},{1... | collective-permute-start | bytes 1769480 | tf_op jit(solution)/shard_map/ppermute | solution.py:344
  46.3 88.7 %collective-permute-start.2 = (f32[576,256]{1,0:T(8,128)}, f32[576,256]{1,0:T(8,128)}, u32[]{:S(2)}, u32[]{:S(2)}) collective-permute-start(f32[576,256]{1,0:T(8,128)} %get-tuple-element.78), channel_id=1, source_target_pairs={{0,8},{4,12},{8,0},{12,4},{1,9},{5,13},{9,1},{13,5},{2,10},{6,14},... | collective-permute-start | bytes 1769480 | tf_op jit(solution)/shard_map/ppermute | solution.py:344
  46.3 36.3 %collective-permute-start.12 = (f32[128,256]{1,0:T(8,128)S(1)}, f32[128,256]{1,0:T(8,128)S(1)}, u32[]{:S(2)}, u32[]{:S(2)}) collective-permute-start(f32[128,256]{1,0:T(8,128)S(1)} %constant_dynamic-slice_fusion), channel_id=1, source_target_pairs={{0,4},{4,0},{8,12},{12,8},{1,5},{5,1},{9,13},{13,9},{2,6},{6,2},{1... | collective-permute-start | bytes 393224 | tf_op jit(solution)/shard_map/ppermute | solution.py:344
  57.6 27.8 %collective-permute-start.13 = (f32[128,256]{1,0:T(8,128)S(1)}, f32[128,256]{1,0:T(8,128)S(1)}, u32[]{:S(2)}, u32[]{:S(2)}) collective-permute-start(f32[128,256]{1,0:T(8,128)S(1)} %slice.111), channel_id=1, source_target_pairs={{0,4},{4,0},{8,12},{12,8},{1,5},{5,1},{9,13},{13,9},{2,6},{6,2},{1... | collective-permute-start | bytes 393224 | tf_op jit(solution)/shard_map/ppermute | solution.py:344
  82.6 52.4 %collective-permute-start.3 = (f32[576,256]{1,0:T(8,128)}, f32[576,256]{1,0:T(8,128)}, u32[]{:S(2)}, u32[]{:S(2)}) collective-permute-start(f32[576,256]{1,0:T(8,128)} %get-tuple-element.79), channel_id=1, source_target_pairs={{0,12},{4,8},{8,4},{12,0},{1,13},{5,9},{9,5},{13,1},{2,14},{6,10},... | collective-permute-start | bytes 1769480 | tf_op jit(solution)/shard_map/ppermute | solution.py:344
  85.4 49.6 %collective-permute-start.15 = (f32[384,256]{1,0:T(8,128)S(1)}, f32[384,256]{1,0:T(8,128)S(1)}, u32[]{:S(2)}, u32[]{:S(2)}) collective-permute-start(f32[384,256]{1,0:T(8,128)S(1)} %pad_maximum_fusion.refs_0_), channel_id=1, source_target_pairs={{0,2},{1,3},{2,0},{3,1},{4,6},{5,7},{6,4},{7,5},{8,10},{9,11},{10,... | collective-permute-start | bytes 1179656 | tf_op jit(solution)/shard_map/ppermute | solution.py:293
  91.8 81.9 %collective-permute-start.10 = (f32[576,256]{1,0:T(8,128)}, f32[576,256]{1,0:T(8,128)}, u32[]{:S(2)}, u32[]{:S(2)}) collective-permute-start(f32[576,256]{1,0:T(8,128)} %get-tuple-element.90), channel_id=1, source_target_pairs={{0,8},{4,12},{8,0},{12,4},{1,9},{5,13},{9,1},{13,5},{2,10},{6,14},... | collective-permute-start | bytes 1769480 | tf_op jit(solution)/shard_map/ppermute | solution.py:344
  94.1 48.7 %collective-permute-start.11 = (f32[576,256]{1,0:T(8,128)}, f32[576,256]{1,0:T(8,128)}, u32[]{:S(2)}, u32[]{:S(2)}) collective-permute-start(f32[576,256]{1,0:T(8,128)} %get-tuple-element.91), channel_id=1, source_target_pairs={{0,12},{4,8},{8,4},{12,0},{1,13},{5,9},{9,5},{13,1},{2,14},{6,10},... | collective-permute-start | bytes 1769480 | tf_op jit(solution)/shard_map/ppermute | solution.py:344
  135.0 41.5 %collective-permute-start.9 = (f32[576,256]{1,0:T(8,128)}, f32[576,256]{1,0:T(8,128)}, u32[]{:S(2)}, u32[]{:S(2)}) collective-permute-start(f32[576,256]{1,0:T(8,128)} %get-tuple-element.89), channel_id=1, source_target_pairs={{0,4},{4,0},{8,12},{12,8},{1,5},{5,1},{9,13},{13,9},{2,6},{6,2},{1... | collective-permute-start | bytes 1769480 | tf_op jit(solution)/shard_map/ppermute | solution.py:344
  135.0 43.8 %collective-permute-start.14 = (f32[384,256]{1,0:T(8,128)S(1)}, f32[384,256]{1,0:T(8,128)S(1)}, u32[]{:S(2)}, u32[]{:S(2)}) collective-permute-start(f32[384,256]{1,0:T(8,128)S(1)} %pad_maximum_fusion.refs_0_), channel_id=1, source_target_pairs={{0,1},{1,0},{2,3},{3,2},{4,5},{5,4},{6,7},{7,6},{8,9},{9,8},{10,11... | collective-permute-start | bytes 1179656 | tf_op jit(solution)/shard_map/ppermute | solution.py:293
  135.1 43.8 %collective-permute-start.16 = (f32[384,256]{1,0:T(8,128)S(1)}, f32[384,256]{1,0:T(8,128)S(1)}, u32[]{:S(2)}, u32[]{:S(2)}) collective-permute-start(f32[384,256]{1,0:T(8,128)S(1)} %collective-permute-done.15.refs_2_), channel_id=1, source_target_pairs={{0,1},{1,0},{2,3},{3,2},{4,5},{5,4},{6,7},{7,6},{8,9},{9,8},{10,11... | collective-permute-start | bytes 1179656 | tf_op jit(solution)/shard_map/ppermute | solution.py:293
  142.8 69.8 %collective-permute-start.4 = (f32[512,256]{1,0:T(8,128)}, f32[512,256]{1,0:T(8,128)S(1)}, u32[]{:S(2)}, u32[]{:S(2)}) collective-permute-start(f32[512,256]{1,0:T(8,128)} %get-tuple-element.82), channel_id=1, source_target_pairs={{0,4},{4,0},{8,12},{12,8},{1,5},{5,1},{9,13},{13,9},{2,6},{6,2},{1... | collective-permute-start | bytes 1572872 | tf_op jit(solution)/shard_map/ppermute | solution.py:344
  173.7 38.9 %collective-permute-start.5 = (f32[512,256]{1,0:T(8,128)}, f32[512,256]{1,0:T(8,128)S(1)}, u32[]{:S(2)}, u32[]{:S(2)}) collective-permute-start(f32[512,256]{1,0:T(8,128)} %get-tuple-element.83), channel_id=1, source_target_pairs={{0,8},{4,12},{8,0},{12,4},{1,9},{5,13},{9,1},{13,5},{2,10},{6,14},... | collective-permute-start | bytes 1572872 | tf_op jit(solution)/shard_map/ppermute | solution.py:344
  176.4 5.1 %copy-start.4 = (f32[640,256]{1,0:T(8,128)S(1)}, f32[640,256]{1,0:T(8,128)}, u32[]{:S(2)}) copy-start(f32[640,256]{1,0:T(8,128)} %get-tuple-element.93.refs_0_) | copy-start | bytes 1966084
  176.5 5.1 %copy-start.6 = (f32[640,256]{1,0:T(8,128)S(1)}, f32[640,256]{1,0:T(8,128)}, u32[]{:S(2)}) copy-start(f32[640,256]{1,0:T(8,128)} %copy-done.5) | copy-start | bytes 1966084
  176.5 39.2 %collective-permute-start.6 = (f32[512,256]{1,0:T(8,128)}, f32[512,256]{1,0:T(8,128)S(1)}, u32[]{:S(2)}, u32[]{:S(2)}) collective-permute-start(f32[512,256]{1,0:T(8,128)} %get-tuple-element.84), channel_id=1, source_target_pairs={{0,12},{4,8},{8,4},{12,0},{1,13},{5,9},{9,5},{13,1},{2,14},{6,10},... | collective-permute-start | bytes 1572872 | tf_op jit(solution)/shard_map/ppermute | solution.py:344
  180.6 1.0 copy-start.1
  181.6 9.8 %copy-start.2 = (bf16[256,2048]{1,0:T(8,128)(2,1)S(1)}, bf16[256,2048]{1,0:T(8,128)(2,1)}, u32[]{:S(2)}) copy-start(bf16[256,2048]{1,0:T(8,128)(2,1)} %copy-done.1) | copy-start | bytes 3145732
  181.6 9.8 %copy-start.7 = (f32[576,256]{1,0:T(8,128)S(1)}, f32[576,256]{1,0:T(8,128)}, u32[]{:S(2)}) copy-start(f32[576,256]{1,0:T(8,128)} %get-tuple-element.92.refs_0_) | copy-start | bytes 1769476
  191.4 10.7 %copy-start.8 = (f32[576,256]{1,0:T(8,128)S(1)}, f32[576,256]{1,0:T(8,128)}, u32[]{:S(2)}) copy-start(f32[576,256]{1,0:T(8,128)} %get-tuple-element.88.refs_0_) | copy-start | bytes 1769476
  202.1 10.5 %copy-start.3 = (f32[512,256]{1,0:T(8,128)S(1)}, f32[512,256]{1,0:T(8,128)}, u32[]{:S(2)}) copy-start(f32[512,256]{1,0:T(8,128)} %get-tuple-element.81.refs_0_) | copy-start | bytes 1572868
  224.4 3.0 %collective-permute-start.17 = (f32[4,2,136,256]{3,2,1,0:T(8,128)}, f32[4,2,136,256]{3,2,1,0:T(8,128)S(1)}, u32[]{:S(2)}, u32[]{:S(2)}) collective-permute-start(f32[4,2,136,256]{3,2,1,0:T(8,128)} %get-tuple-element.121), channel_id=1, source_target_pairs={{0,1},{1,0},{2,3},{3,2},{4,5},{5,4},{6,7},{7,6},{8,9},{9,8},{10,11... | collective-permute-start | bytes 3342344 | tf_op jit(solution)/shard_map/ppermute | solution.py:306
  227.3 12.2 %copy-start.9 = (f32[4,2,136,256]{3,2,1,0:T(8,128)}, f32[4,2,136,256]{3,2,1,0:T(8,128)S(1)}, u32[]{:S(2)}) copy-start(f32[4,2,136,256]{3,2,1,0:T(8,128)S(1)} %collective-permute-done.17) | copy-start | bytes 3342340
  227.3 12.8 %copy-start.10 = (f32[4,2,136,256]{3,2,1,0:T(8,128)S(1)}, f32[4,2,136,256]{3,2,1,0:T(8,128)}, u32[]{:S(2)}) copy-start(f32[4,2,136,256]{3,2,1,0:T(8,128)} %get-tuple-element.120) | copy-start | bytes 3342340
  228.9 23.8 %collective-permute-start.21 = (f32[4,136,256]{2,1,0:T(8,128)S(1)}, f32[4,136,256]{2,1,0:T(8,128)S(1)}, u32[]{:S(2)}, u32[]{:S(2)}) collective-permute-start(f32[4,136,256]{2,1,0:T(8,128)S(1)} %add_bitcast_fusion), channel_id=1, source_target_pairs={{0,2},{1,3},{2,0},{3,1},{4,6},{5,7},{6,4},{7,5},{8,10},{9,11},{10,... | collective-permute-start | bytes 1671176 | tf_op jit(solution)/shard_map/ppermute | solution.py:316
  230.5 10.8 %collective-permute-start.20 = (f32[192,256]{1,0:T(8,128)S(1)}, f32[192,256]{1,0:T(8,128)S(1)}, u32[]{:S(2)}, u32[]{:S(2)}) collective-permute-start(f32[192,256]{1,0:T(8,128)S(1)} %pad_maximum_fusion.3), channel_id=1, source_target_pairs={{0,12},{4,8},{8,4},{12,0},{1,13},{5,9},{9,5},{13,1},{2,14},{6,10},... | collective-permute-start | bytes 589832 | tf_op jit(solution)/shard_map/ppermute | solution.py:344
  233.4 19.3 %collective-permute-start.19 = (f32[192,256]{1,0:T(8,128)S(1)}, f32[192,256]{1,0:T(8,128)S(1)}, u32[]{:S(2)}, u32[]{:S(2)}) collective-permute-start(f32[192,256]{1,0:T(8,128)S(1)} %pad_maximum_fusion.2), channel_id=1, source_target_pairs={{0,8},{4,12},{8,0},{12,4},{1,9},{5,13},{9,1},{13,5},{2,10},{6,14},... | collective-permute-start | bytes 589832 | tf_op jit(solution)/shard_map/ppermute | solution.py:344
  239.5 13.2 %collective-permute-start.18 = (f32[192,256]{1,0:T(8,128)S(1)}, f32[192,256]{1,0:T(8,128)S(1)}, u32[]{:S(2)}, u32[]{:S(2)}) collective-permute-start(f32[192,256]{1,0:T(8,128)S(1)} %pad_maximum_fusion.1), channel_id=1, source_target_pairs={{0,4},{4,0},{8,12},{12,8},{1,5},{5,1},{9,13},{13,9},{2,6},{6,2},{1... | collective-permute-start | bytes 589832 | tf_op jit(solution)/shard_map/ppermute | solution.py:344
  252.8 7.3 %collective-permute-start.22 = (f32[136,256]{1,0:T(8,128)S(1)}, f32[136,256]{1,0:T(8,128)S(1)}, u32[]{:S(2)}, u32[]{:S(2)}) collective-permute-start(f32[136,256]{1,0:T(8,128)S(1)} %get-tuple-element.150), channel_id=1, source_target_pairs={{0,4},{4,0},{8,12},{12,8},{1,5},{5,1},{9,13},{13,9},{2,6},{6,2},{1... | collective-permute-start | bytes 417800 | tf_op jit(solution)/shard_map/ppermute | solution.py:344
  252.9 13.2 %collective-permute-start.23 = (f32[136,256]{1,0:T(8,128)S(1)}, f32[136,256]{1,0:T(8,128)S(1)}, u32[]{:S(2)}, u32[]{:S(2)}) collective-permute-start(f32[136,256]{1,0:T(8,128)S(1)} %get-tuple-element.152), channel_id=1, source_target_pairs={{0,8},{4,12},{8,0},{12,4},{1,9},{5,13},{9,1},{13,5},{2,10},{6,14},... | collective-permute-start | bytes 417800 | tf_op jit(solution)/shard_map/ppermute | solution.py:344
  256.1 10.1 %collective-permute-start.24 = (f32[136,256]{1,0:T(8,128)S(1)}, f32[136,256]{1,0:T(8,128)S(1)}, u32[]{:S(2)}, u32[]{:S(2)}) collective-permute-start(f32[136,256]{1,0:T(8,128)S(1)} %get-tuple-element.151), channel_id=1, source_target_pairs={{0,12},{4,8},{8,4},{12,0},{1,13},{5,9},{9,5},{13,1},{2,14},{6,10},... | collective-permute-start | bytes 417800 | tf_op jit(solution)/shard_map/ppermute | solution.py:344
  266.3 5.9 %collective-permute-start.26 = (f32[128,256]{1,0:T(8,128)S(1)}, f32[128,256]{1,0:T(8,128)S(1)}, u32[]{:S(2)}, u32[]{:S(2)}) collective-permute-start(f32[128,256]{1,0:T(8,128)S(1)} %get-tuple-element.149), channel_id=1, source_target_pairs={{0,2},{1,3},{2,0},{3,1},{4,6},{5,7},{6,4},{7,5},{8,10},{9,11},{10,... | collective-permute-start | bytes 393224 | tf_op jit(solution)/shard_map/ppermute | solution.py:293
  266.9 5.2 %collective-permute-start.25 = (f32[128,256]{1,0:T(8,128)S(1)}, f32[128,256]{1,0:T(8,128)S(1)}, u32[]{:S(2)}, u32[]{:S(2)}) collective-permute-start(f32[128,256]{1,0:T(8,128)S(1)} %get-tuple-element.149), channel_id=1, source_target_pairs={{0,1},{1,0},{2,3},{3,2},{4,5},{5,4},{6,7},{7,6},{8,9},{9,8},{10,11... | collective-permute-start | bytes 393224 | tf_op jit(solution)/shard_map/ppermute | solution.py:293
  267.7 6.5 %collective-permute-start.30 = (f32[64,256]{1,0:T(8,128)S(1)}, f32[64,256]{1,0:T(8,128)S(1)}, u32[]{:S(2)}, u32[]{:S(2)}) collective-permute-start(f32[64,256]{1,0:T(8,128)S(1)} %get-tuple-element.146), channel_id=1, source_target_pairs={{0,12},{4,8},{8,4},{12,0},{1,13},{5,9},{9,5},{13,1},{2,14},{6,10},... | collective-permute-start | bytes 196616 | tf_op jit(solution)/shard_map/ppermute | solution.py:344
  270.2 7.9 %collective-permute-start.29 = (f32[64,256]{1,0:T(8,128)S(1)}, f32[64,256]{1,0:T(8,128)S(1)}, u32[]{:S(2)}, u32[]{:S(2)}) collective-permute-start(f32[64,256]{1,0:T(8,128)S(1)} %get-tuple-element.143), channel_id=1, source_target_pairs={{0,8},{4,12},{8,0},{12,4},{1,9},{5,13},{9,1},{13,5},{2,10},{6,14},... | collective-permute-start | bytes 196616 | tf_op jit(solution)/shard_map/ppermute | solution.py:344
  271.4 6.7 %collective-permute-start.28 = (f32[64,256]{1,0:T(8,128)S(1)}, f32[64,256]{1,0:T(8,128)S(1)}, u32[]{:S(2)}, u32[]{:S(2)}) collective-permute-start(f32[64,256]{1,0:T(8,128)S(1)} %get-tuple-element.140), channel_id=1, source_target_pairs={{0,4},{4,0},{8,12},{12,8},{1,5},{5,1},{9,13},{13,9},{2,6},{6,2},{1... | collective-permute-start | bytes 196616 | tf_op jit(solution)/shard_map/ppermute | solution.py:344
  272.2 2.0 collective-permute-start.27
  278.4 1.0 copy-start.11
  279.4 0.8 copy-start.12

commit v3 on v2

--- a/solution.py
+++ b/solution.py
@@ -10,7 +10,7 @@
 INNER = 2
 WIDTH = 256
 PAD = 8
-VMEM = 48 * 1024 * 1024
+VMEM = 20 * 1024 * 1024
 NT = (((1,), (1,)), ((), ()))
 
 
@@ -256,7 +256,7 @@
         name="update_piece",
         **extra,
     )(*given)
-    return backs, (kept, sent)
+    return backs, (kept, sent), begun
 
 
 def update_plain(m_blocks, h_blocks, rows, whole_w, sums, parts, doc, feat):
@@ -282,7 +282,7 @@
     if sums is not None:
         halves = [old + new for old, new in zip(sums, halves)]
     backs = [lax.dynamic_slice_in_dim(factor, (doc ^ k) * share, share, 0) for k in range(blocks)]
-    return backs, halves
+    return backs, halves, []
 
 
 def spread_feat(value, bits):
@@ -388,24 +388,24 @@
         place = (m_pieces[p], h_blocks, rows)
         if in_kernel:
             early = list(range(n_doc - 1)) if p and p == pieces - 1 else []
-            rows_back, sums = update_piece(*place, weights, sums, n_feat, early)
+            rows_back, sums, begun = update_piece(*place, weights, sums, n_feat, early)
         else:
-            rows_back, sums = update_plain(*place, whole_w, sums, n_feat, doc, feat)
+            rows_back, sums, begun = update_plain(*place, whole_w, sums, n_feat, doc, feat)
         backs.append(rows_back)
-
-    kept, other = add_feat(*sums, bits, feat)
-    batches = [b for b in (backs[:-1], backs[-1:]) if b]
 
     def give_back(batch, *earlier):
         rows_of = [jnp.concatenate([b[k] for b in batch], axis=0) for k in range(n_doc)]
         return [send(after(r, earlier), k) for k, r in enumerate(rows_of)]
 
-    returned = [give_back(b) for b in batches[:-1]]
-    kept = after(kept, [r for rows_of in returned for r in rows_of[1:]])
+    batches = [b for b in (backs[:1], backs[1:]) if b]
+    returned = [give_back(b, *begun) for b in batches[:-1]]
+    kept, sent = sums
+    kept, other = add_feat(kept, after(sent, [r for got in returned for r in got[1:]]), bits, feat)
+    returned.append(give_back(batches[-1]))
+    kept = after(kept, returned[-1][1:])
     total = kept[0] + other[0]
     for k in range(1, n_doc):
         total = total + send(kept[k] + other[k], k)
-    returned.append(give_back(batches[-1], total))
     new_part = w_part * total[:part_rows] / total[part_rows]
     new_parts = spread_feat(new_part, bits)
     new_doc = in_order(new_parts, feat)

time: 281 us -> 279 us (level)
  Pallas kernels: 57.2 us -> 51.6 us
  waiting for transfers between devices: 134 us -> 139 us
    ppermute x6, waiting for transfers between devices: 0.02 us -> 4.92 us  [spread_feat(): got[mask | 1 << j] = lax.ppermute(held, 'feat', pairs)]
    pallas_call x4, Pallas kernels: 39.6 us -> 35.8 us  [update_piece(): pl.pallas_call(functools.partial(piece_kernel, blocks, parts, rows, early...]
  transfers between devices with their start and end apart: 31 -> 31, of which waited for: 11 -> 13; matrix products, arithmetic and copies ran while one was open for 4% -> 4% of each run, Pallas kernels for 16% -> 17%
where the time goes in v3:
time: 279 us; the launch traced here: 278 us
  waiting for transfers between devices  139 us (50%)
  starting transfers between devices  72.6 us (26%)
  Pallas kernels  51.6 us (18%)
  local copies, waits for them, and re-layouts  11.3 us (4%)
    ppermute x23, waiting for transfers between devices, send(): return lax.ppermute(value, 'doc', xor_pairs(n_doc, k)) if k else value  131 us
    ppermute x23, starting transfers between devices, send(): return lax.ppermute(value, 'doc', xor_pairs(n_doc, k)) if k else value  68.3 us
    pallas_call x4, Pallas kernels, update_piece(): pl.pallas_call(functools.partial(piece_kernel, blocks, parts, rows, early...  35.8 us
    pallas_call x4, Pallas kernels, cut(): pl.pallas_call(functools.partial(cut_kernel, spec), out_shape=[jax.ShapeD...  12.7 us
    slice x12, local copies, waits for them, and re-layouts, body(): h_blocks = [after(m[at:at + share], ready) for m in m_pieces[source]]  8.53 us
  transfers between devices with their start and end apart: 31, of which 13 were waited for; matrix products, arithmetic and copies ran while one was open for 4% of the time, Pallas kernels for 17%

profile of v3, /device:TPU:0, one launch (start us, length us, event | category | flops | bytes accessed | tf_op | source)
XLA Modules:
  0.0 277.6 jit_solution(12262210578547968523)
XLA Ops:
  0.6 3.4 %cut_piece.4 = (f32[640,256]{1,0:T(8,128)}, f32[768,256]{1,0:T(8,128)}, f32[640,256]{1,0:T(8,128)}, f32[640,256]{1,0:T(8,128)}) custom-call(f32[512,4096]{1,0:T(8,128)} %refs_0_.4, f32[64,4096]{1,0:T(8,128)} %refs_1_.7, f32[512,256]{1,0:T(8,128)} %own_ref.1), custom_call_target="tpu_custom_call" | custom-call | bytes 5242880 | tf_op jit(solution)/shard_map/cut_piece/pallas_call | solution.py:74
  4.0 4.1 %collective-permute-start.7 = (f32[768,256]{1,0:T(8,128)}, f32[768,256]{1,0:T(8,128)S(1)}, u32[]{:S(2)}, u32[]{:S(2)}) collective-permute-start(f32[768,256]{1,0:T(8,128)} %get-tuple-element.86), channel_id=1, source_target_pairs={{0,8},{4,12},{8,0},{12,4},{1,9},{5,13},{9,1},{13,5},{2,10},{6,14},... | collective-permute-start | bytes 2359304 | tf_op jit(solution)/shard_map/ppermute | solution.py:344
  8.1 1.6 collective-permute-start
  9.7 30.8 %collective-permute-done.refs_1_ = f32[640,256]{1,0:T(8,128)S(1)} collective-permute-done((f32[640,256]{1,0:T(8,128)}, f32[640,256]{1,0:T(8,128)S(1)}, u32[]{:S(2)}, u32[]{:S(2)}) %collective-permute-start) | collective-permute-done | bytes 655392 | tf_op jit(solution)/shard_map/ppermute | solution.py:344
  40.5 3.4 %cut_piece.5 = (f32[576,256]{1,0:T(8,128)}, f32[576,256]{1,0:T(8,128)}, f32[576,256]{1,0:T(8,128)}, f32[576,256]{1,0:T(8,128)}) custom-call(f32[512,4096]{1,0:T(8,128)} %refs_0_.4, f32[64,4096]{1,0:T(8,128)} %refs_1_.7), custom_call_target="tpu_custom_call" | custom-call | bytes 4718592 | tf_op jit(solution)/shard_map/cut_piece/pallas_call | solution.py:74
  43.8 2.4 collective-permute-start.1
  46.3 1.9 collective-permute-start.12
  48.2 9.4 %collective-permute-done.7.refs_2_ = f32[768,256]{1,0:T(8,128)S(1)} collective-permute-done((f32[768,256]{1,0:T(8,128)}, f32[768,256]{1,0:T(8,128)S(1)}, u32[]{:S(2)}, u32[]{:S(2)}) %collective-permute-start.7) | collective-permute-done | bytes 786464 | tf_op jit(solution)/shard_map/ppermute | solution.py:344
  57.6 0.2 collective-permute-start.13
  57.8 24.8 %collective-permute-done.12 = f32[128,256]{1,0:T(8,128)S(1)} collective-permute-done((f32[128,256]{1,0:T(8,128)S(1)}, f32[128,256]{1,0:T(8,128)S(1)}, u32[]{:S(2)}, u32[]{:S(2)}) %collective-permute-start.12) | collective-permute-done | bytes 131104 | tf_op jit(solution)/shard_map/ppermute | solution.py:344
  82.6 1.3 collective-permute-start.3
  83.9 1.5 collective-permute-done.13
  85.5 1.6 collective-permute-start.15
  87.0 0.9 fusion.13
  87.9 0.8 slice.82.refs_4_
  88.7 3.1 %cut_piece.7 = (f32[576,256]{1,0:T(8,128)}, f32[576,256]{1,0:T(8,128)}, f32[576,256]{1,0:T(8,128)}, f32[576,256]{1,0:T(8,128)}) custom-call(f32[512,4096]{1,0:T(8,128)} %refs_0_.4, f32[64,4096]{1,0:T(8,128)} %refs_1_.7), custom_call_target="tpu_custom_call" | custom-call | bytes 4718592 | tf_op jit(solution)/shard_map/cut_piece/pallas_call | solution.py:74
  91.8 2.3 collective-permute-start.10
  94.1 2.6 collective-permute-start.11
  96.7 38.2 %collective-permute-done.2.refs_2_ = f32[576,256]{1,0:T(8,128)} collective-permute-done((f32[576,256]{1,0:T(8,128)}, f32[576,256]{1,0:T(8,128)}, u32[]{:S(2)}, u32[]{:S(2)}) %collective-permute-start.2) | collective-permute-done | bytes 589856 | tf_op jit(solution)/shard_map/ppermute | solution.py:344
  135.0 0.1 collective-permute-start.14
  135.1 0.5 collective-permute-start.16
  135.6 0.9 fusion.11
  136.5 0.8 slice.81.refs_3_.refs_4_
  137.3 2.9 %cut_piece.6 = (f32[512,256]{1,0:T(8,128)}, f32[512,256]{1,0:T(8,128)}, f32[512,256]{1,0:T(8,128)}, f32[512,256]{1,0:T(8,128)}) custom-call(f32[512,4096]{1,0:T(8,128)} %refs_0_.4, f32[64,4096]{1,0:T(8,128)} %refs_1_.7), custom_call_target="tpu_custom_call" | custom-call | bytes 4194304 | tf_op jit(solution)/shard_map/cut_piece/pallas_call | solution.py:74
  140.3 0.8 slice.117.refs_7_
  141.1 0.8 slice.116.refs_6_
  141.9 0.8 slice.115.refs_5_
  142.8 30.0 %collective-permute-start.4 = (f32[512,256]{1,0:T(8,128)}, f32[512,256]{1,0:T(8,128)S(1)}, u32[]{:S(2)}, u32[]{:S(2)}) collective-permute-start(f32[512,256]{1,0:T(8,128)} %get-tuple-element.83), channel_id=1, source_target_pairs={{0,4},{4,0},{8,12},{12,8},{1,5},{5,1},{9,13},{13,9},{2,6},{6,2},{1... | collective-permute-start | bytes 1572872 | tf_op jit(solution)/shard_map/ppermute | solution.py:344
  172.8 0.8 slice.120.refs_6_.refs_7_
  173.7 1.9 collective-permute-start.5
  175.6 0.8 slice.119.refs_5_.refs_6_
  176.5 1.5 collective-permute-start.6
  178.0 0.8 slice.118.refs_4_.refs_5_
  178.9 1.3 prepare_w.1
  180.1 8.7 %update_piece.4 = (f32[64,256]{1,0:T(8,128)S(1)}, f32[64,256]{1,0:T(8,128)S(1)}, f32[64,256]{1,0:T(8,128)S(1)}, f32[64,256]{1,0:T(8,128)S(1)}, f32[4,2,136,256]{...) custom-call(f32[640,256]{1,0:T(8,128)S(1)} %copy-done.2, f32[640,256]{1,0:T(8,128)S(1)} %copy-done.4, ...), custom_call_target="tpu_custom_call" | custom-call | flops 4026531840 | bytes 10485760 | tf_op jit(solution)/shard_map/update_piece/pallas_call | solution.py:249
  188.9 9.7 %update_piece.5 = (f32[64,256]{1,0:T(8,128)S(1)}, f32[64,256]{1,0:T(8,128)S(1)}, f32[64,256]{1,0:T(8,128)S(1)}, f32[64,256]{1,0:T(8,128)S(1)}, f32[4,2,136,256]{...) custom-call(f32[576,256]{1,0:T(8,128)S(1)} %copy-done.5, ...), custom_call_target="tpu_custom_call", output_to_operand_aliasing={{4}: (13, {}), {5}: (14, {})} | custom-call | flops 4026531840 | bytes 10485760 | tf_op jit(solution)/shard_map/update_piece/pallas_call | solution.py:249
  198.6 9.5 %update_piece.6 = (f32[64,256]{1,0:T(8,128)S(1)}, f32[64,256]{1,0:T(8,128)S(1)}, f32[64,256]{1,0:T(8,128)S(1)}, f32[64,256]{1,0:T(8,128)S(1)}, f32[4,2,136,256]{...) custom-call(f32[576,256]{1,0:T(8,128)S(1)} %copy-done.6, ...), custom_call_target="tpu_custom_call", output_to_operand_aliasing={{4}: (13, {}), {5}: (14, {})} | custom-call | flops 4026531840 | bytes 10485760 | tf_op jit(solution)/shard_map/update_piece/pallas_call | solution.py:249
  208.2 3.9 %collective-permute-done.5.refs_2_ = f32[512,256]{1,0:T(8,128)S(1)} collective-permute-done((f32[512,256]{1,0:T(8,128)}, f32[512,256]{1,0:T(8,128)S(1)}, u32[]{:S(2)}, u32[]{:S(2)}) %collective-permute-start.5) | collective-permute-done | bytes 524320 | tf_op jit(solution)/shard_map/ppermute | solution.py:344
  212.1 1.9 begin_piece.1.refs_13_
  214.0 3.4 %collective-permute-start.19 = (f32[64,256]{1,0:T(8,128)S(1)}, f32[64,256]{1,0:T(8,128)S(1)}, u32[]{:S(2)}, u32[]{:S(2)}) collective-permute-start(f32[64,256]{1,0:T(8,128)S(1)} %get-tuple-element.128), channel_id=1, source_target_pairs={{0,12},{4,8},{8,4},{12,0},{1,13},{5,9},{9,5},{13,1},{2,14},{6,10},... | collective-permute-start | bytes 196616 | tf_op jit(solution)/shard_map/ppermute | solution.py:344
  217.4 1.0 collective-permute-start.17
  218.4 7.8 %update_piece.7 = (f32[64,256]{1,0:T(8,128)S(1)}, f32[64,256]{1,0:T(8,128)S(1)}, f32[64,256]{1,0:T(8,128)S(1)}, f32[64,256]{1,0:T(8,128)S(1)}, f32[4,2,136,256]{...) custom-call(f32[512,256]{1,0:T(8,128)S(1)} %copy-done.1, ...), custom_call_target="tpu_custom_call", output_to_operand_aliasing={{4}: (14, {}), {5}: (15, {})} | custom-call | flops 4026531840 | bytes 10485760 | tf_op jit(solution)/shard_map/update_piece/pallas_call | solution.py:249
  226.2 1.5 collective-permute-done.18
  227.7 3.1 %collective-permute-done.20 = f32[4,2,136,256]{3,2,1,0:T(8,128)} collective-permute-done((f32[4,2,136,256]{3,2,1,0:T(8,128)}, f32[4,2,136,256]{3,2,1,0:T(8,128)}, u32[]{:S(2)}, u32[]{:S(2)}) %collective-permute-start.20) | collective-permute-done | bytes 1114144 | tf_op jit(solution)/shard_map/ppermute | solution.py:306
  230.8 1.2 add_bitcast_fusion
  232.0 1.5 collective-permute-start.24
  233.5 3.4 %collective-permute-start.23 = (f32[192,256]{1,0:T(8,128)S(1)}, f32[192,256]{1,0:T(8,128)S(1)}, u32[]{:S(2)}, u32[]{:S(2)}) collective-permute-start(f32[192,256]{1,0:T(8,128)S(1)} %pad_maximum_fusion.3), channel_id=1, source_target_pairs={{0,12},{4,8},{8,4},{12,0},{1,13},{5,9},{9,5},{13,1},{2,14},{6,10},... | collective-permute-start | bytes 589832 | tf_op jit(solution)/shard_map/ppermute | solution.py:344
  237.0 5.4 %collective-permute-start.22 = (f32[192,256]{1,0:T(8,128)S(1)}, f32[192,256]{1,0:T(8,128)S(1)}, u32[]{:S(2)}, u32[]{:S(2)}) collective-permute-start(f32[192,256]{1,0:T(8,128)S(1)} %pad_maximum_fusion.2), channel_id=1, source_target_pairs={{0,8},{4,12},{8,0},{12,4},{1,9},{5,13},{9,1},{13,5},{2,10},{6,14},... | collective-permute-start | bytes 589832 | tf_op jit(solution)/shard_map/ppermute | solution.py:344
  242.5 0.6 collective-permute-start.21
  243.1 1.1 fusion
  244.2 11.5 %collective-permute-done.22 = f32[192,256]{1,0:T(8,128)S(1)} collective-permute-done((f32[192,256]{1,0:T(8,128)S(1)}, f32[192,256]{1,0:T(8,128)S(1)}, u32[]{:S(2)}, u32[]{:S(2)}) %collective-permute-start.22) | collective-permute-done | bytes 196640 | tf_op jit(solution)/shard_map/ppermute | solution.py:344
  255.8 3.2 %collective-permute-start.26 = (f32[136,256]{1,0:T(8,128)S(1)}, f32[136,256]{1,0:T(8,128)S(1)}, u32[]{:S(2)}, u32[]{:S(2)}) collective-permute-start(f32[136,256]{1,0:T(8,128)S(1)} %get-tuple-element.154), channel_id=1, source_target_pairs={{0,8},{4,12},{8,0},{12,4},{1,9},{5,13},{9,1},{13,5},{2,10},{6,14},... | collective-permute-start | bytes 417800 | tf_op jit(solution)/shard_map/ppermute | solution.py:344
  259.0 1.2 collective-permute-start.27
  260.2 2.8 %collective-permute-done.25 = f32[136,256]{1,0:T(8,128)S(1)} collective-permute-done((f32[136,256]{1,0:T(8,128)S(1)}, f32[136,256]{1,0:T(8,128)S(1)}, u32[]{:S(2)}, u32[]{:S(2)}) %collective-permute-start.25) | collective-permute-done | bytes 139296 | tf_op jit(solution)/shard_map/ppermute | solution.py:344
  263.0 6.0 %collective-permute-done.26 = f32[136,256]{1,0:T(8,128)S(1)} collective-permute-done((f32[136,256]{1,0:T(8,128)S(1)}, f32[136,256]{1,0:T(8,128)S(1)}, u32[]{:S(2)}, u32[]{:S(2)}) %collective-permute-start.26) | collective-permute-done | bytes 139296 | tf_op jit(solution)/shard_map/ppermute | solution.py:344
  269.2 0.6 collective-permute-start.29
  269.9 0.1 copy.19
  270.1 0.1 copy.22
  270.3 0.1 copy.21
  270.5 0.1 copy.20
  270.6 3.6 %collective-permute-done.29 = f32[128,256]{1,0:T(8,128)S(1)} collective-permute-done((f32[128,256]{1,0:T(8,128)S(1)}, f32[128,256]{1,0:T(8,128)S(1)}, u32[]{:S(2)}, u32[]{:S(2)}) %collective-permute-start.29) | collective-permute-done | bytes 131104 | tf_op jit(solution)/shard_map/ppermute | solution.py:293
  274.3 1.3 collective-permute-done.30
  275.9 0.9 copy-done.7
  276.8 0.8 copy-done.8
  (72 shorter events, 0.9 us)
Async XLA Ops:
  4.0 53.6 %collective-permute-start.7 = (f32[768,256]{1,0:T(8,128)}, f32[768,256]{1,0:T(8,128)S(1)}, u32[]{:S(2)}, u32[]{:S(2)}) collective-permute-start(f32[768,256]{1,0:T(8,128)} %get-tuple-element.86), channel_id=1, source_target_pairs={{0,8},{4,12},{8,0},{12,4},{1,9},{5,13},{9,1},{13,5},{2,10},{6,14},... | collective-permute-start | bytes 2359304 | tf_op jit(solution)/shard_map/ppermute | solution.py:344
  8.1 32.3 %collective-permute-start = (f32[640,256]{1,0:T(8,128)}, f32[640,256]{1,0:T(8,128)S(1)}, u32[]{:S(2)}, u32[]{:S(2)}) collective-permute-start(f32[640,256]{1,0:T(8,128)} %get-tuple-element.76), channel_id=1, source_target_pairs={{0,4},{4,0},{8,12},{12,8},{1,5},{5,1},{9,13},{13,9},{2,6},{6,2},{1... | collective-permute-start | bytes 1966088 | tf_op jit(solution)/shard_map/ppermute | solution.py:344
  9.7 79.1 %collective-permute-start.8 = (f32[640,256]{1,0:T(8,128)}, f32[640,256]{1,0:T(8,128)}, u32[]{:S(2)}, u32[]{:S(2)}) collective-permute-start(f32[640,256]{1,0:T(8,128)} %get-tuple-element.87), channel_id=1, source_target_pairs={{0,12},{4,8},{8,4},{12,0},{1,13},{5,9},{9,5},{13,1},{2,14},{6,10},... | collective-permute-start | bytes 1966088 | tf_op jit(solution)/shard_map/ppermute | solution.py:344
  9.7 36.6 %copy-start = (f32[512,256]{1,0:T(8,128)S(1)}, f32[512,256]{1,0:T(8,128)}, u32[]{:S(2)}) copy-start(f32[512,256]{1,0:T(8,128)} %own_ref.1) | copy-start | bytes 1572868
  40.5 94.5 %copy-start.3 = (f32[640,256]{1,0:T(8,128)}, f32[640,256]{1,0:T(8,128)S(1)}, u32[]{:S(2)}) copy-start(f32[640,256]{1,0:T(8,128)S(1)} %collective-permute-done.refs_1_) | copy-start | bytes 1966084
  43.8 50.3 %collective-permute-start.1 = (f32[576,256]{1,0:T(8,128)}, f32[576,256]{1,0:T(8,128)}, u32[]{:S(2)}, u32[]{:S(2)}) collective-permute-start(f32[576,256]{1,0:T(8,128)} %get-tuple-element.78), channel_id=1, source_target_pairs={{0,4},{4,0},{8,12},{12,8},{1,5},{5,1},{9,13},{13,9},{2,6},{6,2},{1... | collective-permute-start | bytes 1769480 | tf_op jit(solution)/shard_map/ppermute | solution.py:344
  46.3 88.7 %collective-permute-start.2 = (f32[576,256]{1,0:T(8,128)}, f32[576,256]{1,0:T(8,128)}, u32[]{:S(2)}, u32[]{:S(2)}) collective-permute-start(f32[576,256]{1,0:T(8,128)} %get-tuple-element.79), channel_id=1, source_target_pairs={{0,8},{4,12},{8,0},{12,4},{1,9},{5,13},{9,1},{13,5},{2,10},{6,14},... | collective-permute-start | bytes 1769480 | tf_op jit(solution)/shard_map/ppermute | solution.py:344
  46.3 36.3 %collective-permute-start.12 = (f32[128,256]{1,0:T(8,128)S(1)}, f32[128,256]{1,0:T(8,128)S(1)}, u32[]{:S(2)}, u32[]{:S(2)}) collective-permute-start(f32[128,256]{1,0:T(8,128)S(1)} %constant_dynamic-slice_fusion), channel_id=1, source_target_pairs={{0,4},{4,0},{8,12},{12,8},{1,5},{5,1},{9,13},{13,9},{2,6},{6,2},{1... | collective-permute-start | bytes 393224 | tf_op jit(solution)/shard_map/ppermute | solution.py:344
  57.6 27.8 %collective-permute-start.13 = (f32[128,256]{1,0:T(8,128)S(1)}, f32[128,256]{1,0:T(8,128)S(1)}, u32[]{:S(2)}, u32[]{:S(2)}) collective-permute-start(f32[128,256]{1,0:T(8,128)S(1)} %slice.111), channel_id=1, source_target_pairs={{0,4},{4,0},{8,12},{12,8},{1,5},{5,1},{9,13},{13,9},{2,6},{6,2},{1... | collective-permute-start | bytes 393224 | tf_op jit(solution)/shard_map/ppermute | solution.py:344
  82.6 52.4 %collective-permute-start.3 = (f32[576,256]{1,0:T(8,128)}, f32[576,256]{1,0:T(8,128)}, u32[]{:S(2)}, u32[]{:S(2)}) collective-permute-start(f32[576,256]{1,0:T(8,128)} %get-tuple-element.80), channel_id=1, source_target_pairs={{0,12},{4,8},{8,4},{12,0},{1,13},{5,9},{9,5},{13,1},{2,14},{6,10},... | collective-permute-start | bytes 1769480 | tf_op jit(solution)/shard_map/ppermute | solution.py:344
  85.5 49.6 %collective-permute-start.15 = (f32[384,256]{1,0:T(8,128)S(1)}, f32[384,256]{1,0:T(8,128)S(1)}, u32[]{:S(2)}, u32[]{:S(2)}) collective-permute-start(f32[384,256]{1,0:T(8,128)S(1)} %pad_maximum_fusion.refs_0_), channel_id=1, source_target_pairs={{0,2},{1,3},{2,0},{3,1},{4,6},{5,7},{6,4},{7,5},{8,10},{9,11},{10,... | collective-permute-start | bytes 1179656 | tf_op jit(solution)/shard_map/ppermute | solution.py:293
  91.8 81.9 %collective-permute-start.10 = (f32[576,256]{1,0:T(8,128)}, f32[576,256]{1,0:T(8,128)}, u32[]{:S(2)}, u32[]{:S(2)}) collective-permute-start(f32[576,256]{1,0:T(8,128)} %get-tuple-element.91), channel_id=1, source_target_pairs={{0,8},{4,12},{8,0},{12,4},{1,9},{5,13},{9,1},{13,5},{2,10},{6,14},... | collective-permute-start | bytes 1769480 | tf_op jit(solution)/shard_map/ppermute | solution.py:344
  94.1 48.7 %collective-permute-start.11 = (f32[576,256]{1,0:T(8,128)}, f32[576,256]{1,0:T(8,128)}, u32[]{:S(2)}, u32[]{:S(2)}) collective-permute-start(f32[576,256]{1,0:T(8,128)} %get-tuple-element.92), channel_id=1, source_target_pairs={{0,12},{4,8},{8,4},{12,0},{1,13},{5,9},{9,5},{13,1},{2,14},{6,10},... | collective-permute-start | bytes 1769480 | tf_op jit(solution)/shard_map/ppermute | solution.py:344
  135.0 41.5 %collective-permute-start.9 = (f32[576,256]{1,0:T(8,128)}, f32[576,256]{1,0:T(8,128)}, u32[]{:S(2)}, u32[]{:S(2)}) collective-permute-start(f32[576,256]{1,0:T(8,128)} %get-tuple-element.90), channel_id=1, source_target_pairs={{0,4},{4,0},{8,12},{12,8},{1,5},{5,1},{9,13},{13,9},{2,6},{6,2},{1... | collective-permute-start | bytes 1769480 | tf_op jit(solution)/shard_map/ppermute | solution.py:344
  135.0 43.8 %collective-permute-start.14 = (f32[384,256]{1,0:T(8,128)S(1)}, f32[384,256]{1,0:T(8,128)S(1)}, u32[]{:S(2)}, u32[]{:S(2)}) collective-permute-start(f32[384,256]{1,0:T(8,128)S(1)} %pad_maximum_fusion.refs_0_), channel_id=1, source_target_pairs={{0,1},{1,0},{2,3},{3,2},{4,5},{5,4},{6,7},{7,6},{8,9},{9,8},{10,11... | collective-permute-start | bytes 1179656 | tf_op jit(solution)/shard_map/ppermute | solution.py:293
  135.1 43.8 %collective-permute-start.16 = (f32[384,256]{1,0:T(8,128)S(1)}, f32[384,256]{1,0:T(8,128)S(1)}, u32[]{:S(2)}, u32[]{:S(2)}) collective-permute-start(f32[384,256]{1,0:T(8,128)S(1)} %collective-permute-done.15.refs_2_), channel_id=1, source_target_pairs={{0,1},{1,0},{2,3},{3,2},{4,5},{5,4},{6,7},{7,6},{8,9},{9,8},{10,11... | collective-permute-start | bytes 1179656 | tf_op jit(solution)/shard_map/ppermute | solution.py:293
  142.8 65.4 %collective-permute-start.4 = (f32[512,256]{1,0:T(8,128)}, f32[512,256]{1,0:T(8,128)S(1)}, u32[]{:S(2)}, u32[]{:S(2)}) collective-permute-start(f32[512,256]{1,0:T(8,128)} %get-tuple-element.83), channel_id=1, source_target_pairs={{0,4},{4,0},{8,12},{12,8},{1,5},{5,1},{9,13},{13,9},{2,6},{6,2},{1... | collective-permute-start | bytes 1572872 | tf_op jit(solution)/shard_map/ppermute | solution.py:344
  173.7 38.4 %collective-permute-start.5 = (f32[512,256]{1,0:T(8,128)}, f32[512,256]{1,0:T(8,128)S(1)}, u32[]{:S(2)}, u32[]{:S(2)}) collective-permute-start(f32[512,256]{1,0:T(8,128)} %get-tuple-element.84), channel_id=1, source_target_pairs={{0,8},{4,12},{8,0},{12,4},{1,9},{5,13},{9,1},{13,5},{2,10},{6,14},... | collective-permute-start | bytes 1572872 | tf_op jit(solution)/shard_map/ppermute | solution.py:344
  176.5 3.7 %copy-start.2 = (f32[640,256]{1,0:T(8,128)S(1)}, f32[640,256]{1,0:T(8,128)}, u32[]{:S(2)}) copy-start(f32[640,256]{1,0:T(8,128)} %get-tuple-element.94.refs_0_) | copy-start | bytes 1966084
  176.5 3.7 %copy-start.4 = (f32[640,256]{1,0:T(8,128)S(1)}, f32[640,256]{1,0:T(8,128)}, u32[]{:S(2)}) copy-start(f32[640,256]{1,0:T(8,128)} %copy-done.3) | copy-start | bytes 1966084
  176.5 41.9 %collective-permute-start.6 = (f32[512,256]{1,0:T(8,128)}, f32[512,256]{1,0:T(8,128)S(1)}, u32[]{:S(2)}, u32[]{:S(2)}) collective-permute-start(f32[512,256]{1,0:T(8,128)} %get-tuple-element.85), channel_id=1, source_target_pairs={{0,12},{4,8},{8,4},{12,0},{1,13},{5,9},{9,5},{13,1},{2,14},{6,10},... | collective-permute-start | bytes 1572872 | tf_op jit(solution)/shard_map/ppermute | solution.py:344
  180.1 8.7 %copy-start.5 = (f32[576,256]{1,0:T(8,128)S(1)}, f32[576,256]{1,0:T(8,128)}, u32[]{:S(2)}) copy-start(f32[576,256]{1,0:T(8,128)} %get-tuple-element.93.refs_0_) | copy-start | bytes 1769476
  188.9 9.7 %copy-start.6 = (f32[576,256]{1,0:T(8,128)S(1)}, f32[576,256]{1,0:T(8,128)}, u32[]{:S(2)}) copy-start(f32[576,256]{1,0:T(8,128)} %get-tuple-element.89.refs_0_) | copy-start | bytes 1769476
  198.6 13.5 %copy-start.1 = (f32[512,256]{1,0:T(8,128)S(1)}, f32[512,256]{1,0:T(8,128)}, u32[]{:S(2)}) copy-start(f32[512,256]{1,0:T(8,128)} %get-tuple-element.82.refs_0_) | copy-start | bytes 1572868
  214.0 12.2 %collective-permute-start.19 = (f32[64,256]{1,0:T(8,128)S(1)}, f32[64,256]{1,0:T(8,128)S(1)}, u32[]{:S(2)}, u32[]{:S(2)}) collective-permute-start(f32[64,256]{1,0:T(8,128)S(1)} %get-tuple-element.128), channel_id=1, source_target_pairs={{0,12},{4,8},{8,4},{12,0},{1,13},{5,9},{9,5},{13,1},{2,14},{6,10},... | collective-permute-start | bytes 196616 | tf_op jit(solution)/shard_map/ppermute | solution.py:344
  217.4 10.3 %collective-permute-start.18 = (f32[64,256]{1,0:T(8,128)S(1)}, f32[64,256]{1,0:T(8,128)S(1)}, u32[]{:S(2)}, u32[]{:S(2)}) collective-permute-start(f32[64,256]{1,0:T(8,128)S(1)} %get-tuple-element.126), channel_id=1, source_target_pairs={{0,8},{4,12},{8,0},{12,4},{1,9},{5,13},{9,1},{13,5},{2,10},{6,14},... | collective-permute-start | bytes 196616 | tf_op jit(solution)/shard_map/ppermute | solution.py:344
  217.4 10.3 %collective-permute-start.17 = (f32[64,256]{1,0:T(8,128)S(1)}, f32[64,256]{1,0:T(8,128)S(1)}, u32[]{:S(2)}, u32[]{:S(2)}) collective-permute-start(f32[64,256]{1,0:T(8,128)S(1)} %get-tuple-element.124), channel_id=1, source_target_pairs={{0,4},{4,0},{8,12},{12,8},{1,5},{5,1},{9,13},{13,9},{2,6},{6,2},{1... | collective-permute-start | bytes 196616 | tf_op jit(solution)/shard_map/ppermute | solution.py:344
  227.7 3.1 %collective-permute-start.20 = (f32[4,2,136,256]{3,2,1,0:T(8,128)}, f32[4,2,136,256]{3,2,1,0:T(8,128)}, u32[]{:S(2)}, u32[]{:S(2)}) collective-permute-start(f32[4,2,136,256]{3,2,1,0:T(8,128)} %get-tuple-element.129), channel_id=1, source_target_pairs={{0,1},{1,0},{2,3},{3,2},{4,5},{5,4},{6,7},{7,6},{8,9},{9,8},{10,11... | collective-permute-start | bytes 3342344 | tf_op jit(solution)/shard_map/ppermute | solution.py:306
  232.0 23.7 %collective-permute-start.24 = (f32[4,136,256]{2,1,0:T(8,128)S(1)}, f32[4,136,256]{2,1,0:T(8,128)S(1)}, u32[]{:S(2)}, u32[]{:S(2)}) collective-permute-start(f32[4,136,256]{2,1,0:T(8,128)S(1)} %add_bitcast_fusion), channel_id=1, source_target_pairs={{0,2},{1,3},{2,0},{3,1},{4,6},{5,7},{6,4},{7,5},{8,10},{9,11},{10,... | collective-permute-start | bytes 1671176 | tf_op jit(solution)/shard_map/ppermute | solution.py:316
  233.5 10.7 %collective-permute-start.23 = (f32[192,256]{1,0:T(8,128)S(1)}, f32[192,256]{1,0:T(8,128)S(1)}, u32[]{:S(2)}, u32[]{:S(2)}) collective-permute-start(f32[192,256]{1,0:T(8,128)S(1)} %pad_maximum_fusion.3), channel_id=1, source_target_pairs={{0,12},{4,8},{8,4},{12,0},{1,13},{5,9},{9,5},{13,1},{2,14},{6,10},... | collective-permute-start | bytes 589832 | tf_op jit(solution)/shard_map/ppermute | solution.py:344
  237.0 18.7 %collective-permute-start.22 = (f32[192,256]{1,0:T(8,128)S(1)}, f32[192,256]{1,0:T(8,128)S(1)}, u32[]{:S(2)}, u32[]{:S(2)}) collective-permute-start(f32[192,256]{1,0:T(8,128)S(1)} %pad_maximum_fusion.2), channel_id=1, source_target_pairs={{0,8},{4,12},{8,0},{12,4},{1,9},{5,13},{9,1},{13,5},{2,10},{6,14},... | collective-permute-start | bytes 589832 | tf_op jit(solution)/shard_map/ppermute | solution.py:344
  242.5 13.2 %collective-permute-start.21 = (f32[192,256]{1,0:T(8,128)S(1)}, f32[192,256]{1,0:T(8,128)S(1)}, u32[]{:S(2)}, u32[]{:S(2)}) collective-permute-start(f32[192,256]{1,0:T(8,128)S(1)} %pad_maximum_fusion.1), channel_id=1, source_target_pairs={{0,4},{4,0},{8,12},{12,8},{1,5},{5,1},{9,13},{13,9},{2,6},{6,2},{1... | collective-permute-start | bytes 589832 | tf_op jit(solution)/shard_map/ppermute | solution.py:344
  255.8 7.3 %collective-permute-start.25 = (f32[136,256]{1,0:T(8,128)S(1)}, f32[136,256]{1,0:T(8,128)S(1)}, u32[]{:S(2)}, u32[]{:S(2)}) collective-permute-start(f32[136,256]{1,0:T(8,128)S(1)} %get-tuple-element.152), channel_id=1, source_target_pairs={{0,4},{4,0},{8,12},{12,8},{1,5},{5,1},{9,13},{13,9},{2,6},{6,2},{1... | collective-permute-start | bytes 417800 | tf_op jit(solution)/shard_map/ppermute | solution.py:344
  255.8 13.2 %collective-permute-start.26 = (f32[136,256]{1,0:T(8,128)S(1)}, f32[136,256]{1,0:T(8,128)S(1)}, u32[]{:S(2)}, u32[]{:S(2)}) collective-permute-start(f32[136,256]{1,0:T(8,128)S(1)} %get-tuple-element.154), channel_id=1, source_target_pairs={{0,8},{4,12},{8,0},{12,4},{1,9},{5,13},{9,1},{13,5},{2,10},{6,14},... | collective-permute-start | bytes 417800 | tf_op jit(solution)/shard_map/ppermute | solution.py:344
  259.0 10.1 %collective-permute-start.27 = (f32[136,256]{1,0:T(8,128)S(1)}, f32[136,256]{1,0:T(8,128)S(1)}, u32[]{:S(2)}, u32[]{:S(2)}) collective-permute-start(f32[136,256]{1,0:T(8,128)S(1)} %get-tuple-element.153), channel_id=1, source_target_pairs={{0,12},{4,8},{8,4},{12,0},{1,13},{5,9},{9,5},{13,1},{2,14},{6,10},... | collective-permute-start | bytes 417800 | tf_op jit(solution)/shard_map/ppermute | solution.py:344
  269.2 5.0 %collective-permute-start.29 = (f32[128,256]{1,0:T(8,128)S(1)}, f32[128,256]{1,0:T(8,128)S(1)}, u32[]{:S(2)}, u32[]{:S(2)}) collective-permute-start(f32[128,256]{1,0:T(8,128)S(1)} %get-tuple-element.151), channel_id=1, source_target_pairs={{0,2},{1,3},{2,0},{3,1},{4,6},{5,7},{6,4},{7,5},{8,10},{9,11},{10,... | collective-permute-start | bytes 393224 | tf_op jit(solution)/shard_map/ppermute | solution.py:293
  269.9 4.4 %collective-permute-start.28 = (f32[128,256]{1,0:T(8,128)S(1)}, f32[128,256]{1,0:T(8,128)S(1)}, u32[]{:S(2)}, u32[]{:S(2)}) collective-permute-start(f32[128,256]{1,0:T(8,128)S(1)} %get-tuple-element.151), channel_id=1, source_target_pairs={{0,1},{1,0},{2,3},{3,2},{4,5},{5,4},{6,7},{7,6},{8,9},{9,8},{10,11... | collective-permute-start | bytes 393224 | tf_op jit(solution)/shard_map/ppermute | solution.py:293
  274.3 1.3 collective-permute-start.30
  275.9 1.0 copy-start.7
  276.8 0.8 copy-start.8

commit v4 on v3

--- a/solution.py
+++ b/solution.py
@@ -351,11 +351,15 @@
         height = rows + share * len(riders[p])
         w_mask = n_doc // 2 if w_rides and p == 0 else -1
         given += [doc_factor] if w_mask > 0 else []
-        masks = [*others, 0]
-        place = (owned, starts[p], [starts[q] for q in riders[p]], widths[p], masks, height)
-        place += (w_mask, part_rows)
-        arrays = cut(given, *place) if in_kernel else cut_plain(given, doc, feat, *place)
-        got = {k: send(piece, k) for k, piece in zip(masks, arrays)}
+        got = {}
+        far = [k for k in others if k >= n_doc // 2]
+        near = [k for k in range(n_doc // 2 - 1, -1, -1)]
+        for masks in (far, near) if p == 0 else (far + near,):
+            place = (owned, starts[p], [starts[q] for q in riders[p]], widths[p], masks, height)
+            place += (w_mask, part_rows)
+            arrays = cut(given, *place) if in_kernel else cut_plain(given, doc, feat, *place)
+            got |= {k: send(piece, k) for k, piece in zip(masks, arrays)}
+            given = [after(given[0], arrays), *given[1:]]
         return [got[k] for k in range(n_doc)]
 
     m_pieces = []

time: 279 us -> 278 us (level)
  waiting for transfers between devices: 139 us -> 136 us
    pallas_call x4 -> x5, Pallas kernels: 12.7 us -> 14.2 us  [cut(): pl.pallas_call(functools.partial(cut_kernel, spec), out_shape=[jax.ShapeD...]
  transfers between devices with their start and end apart: 31 -> 31, of which waited for: 13 -> 13; matrix products, arithmetic and copies ran while one was open for 4% -> 4% of each run, Pallas kernels for 17% -> 18%
where the time goes in v4:
time: 278 us; the launch traced here: 277 us
  waiting for transfers between devices  136 us (49%)
  starting transfers between devices  72.7 us (26%)
  Pallas kernels  53.1 us (19%)
  local copies, waits for them, and re-layouts  11.3 us (4%)
    ppermute x23, waiting for transfers between devices, send(): return lax.ppermute(value, 'doc', xor_pairs(n_doc, k)) if k else value  128 us
    ppermute x23, starting transfers between devices, send(): return lax.ppermute(value, 'doc', xor_pairs(n_doc, k)) if k else value  68.4 us
    pallas_call x4, Pallas kernels, update_piece(): pl.pallas_call(functools.partial(piece_kernel, blocks, parts, rows, early...  35.8 us
    pallas_call x5, Pallas kernels, cut(): pl.pallas_call(functools.partial(cut_kernel, spec), out_shape=[jax.ShapeD...  14.2 us
    slice x12, local copies, waits for them, and re-layouts, body(): h_blocks = [after(m[at:at + share], ready) for m in m_pieces[source]]  8.53 us
  transfers between devices with their start and end apart: 31, of which 13 were waited for; matrix products, arithmetic and copies ran while one was open for 4% of the time, Pallas kernels for 18%

profile of v4, /device:TPU:0, one launch (start us, length us, event | category | flops | bytes accessed | tf_op | source)
XLA Modules:
  0.0 276.8 jit_solution(10249915375968345508)
XLA Ops:
  0.6 2.5 cut_piece.5
  3.1 4.1 %collective-permute-start.7 = (f32[768,256]{1,0:T(8,128)}, f32[768,256]{1,0:T(8,128)S(1)}, u32[]{:S(2)}, u32[]{:S(2)}) collective-permute-start(f32[768,256]{1,0:T(8,128)} %get-tuple-element.78), channel_id=1, source_target_pairs={{0,8},{4,12},{8,0},{12,4},{1,9},{5,13},{9,1},{13,5},{2,10},{6,14},... | collective-permute-start | bytes 2359304 | tf_op jit(solution)/shard_map/ppermute | solution.py:344
  7.2 2.4 cut_piece.6
  9.6 1.6 collective-permute-start
  11.2 28.3 %collective-permute-done.refs_1_ = f32[640,256]{1,0:T(8,128)S(1)} collective-permute-done((f32[640,256]{1,0:T(8,128)}, f32[640,256]{1,0:T(8,128)S(1)}, u32[]{:S(2)}, u32[]{:S(2)}) %collective-permute-start) | collective-permute-done | bytes 655392 | tf_op jit(solution)/shard_map/ppermute | solution.py:344
  39.6 3.4 %cut_piece.7 = (f32[576,256]{1,0:T(8,128)}, f32[576,256]{1,0:T(8,128)}, f32[576,256]{1,0:T(8,128)}, f32[576,256]{1,0:T(8,128)}) custom-call(f32[512,4096]{1,0:T(8,128)} %refs_0_.5, f32[64,4096]{1,0:T(8,128)} %refs_1_.9), custom_call_target="tpu_custom_call" | custom-call | bytes 4718592 | tf_op jit(solution)/shard_map/cut_piece/pallas_call | solution.py:74
  42.9 2.4 collective-permute-start.1
  45.4 1.9 collective-permute-start.12
  47.3 9.4 %collective-permute-done.7.refs_2_ = f32[768,256]{1,0:T(8,128)S(1)} collective-permute-done((f32[768,256]{1,0:T(8,128)}, f32[768,256]{1,0:T(8,128)S(1)}, u32[]{:S(2)}, u32[]{:S(2)}) %collective-permute-start.7) | collective-permute-done | bytes 786464 | tf_op jit(solution)/shard_map/ppermute | solution.py:344
  56.7 0.2 collective-permute-start.13
  56.9 24.8 %collective-permute-done.12 = f32[128,256]{1,0:T(8,128)S(1)} collective-permute-done((f32[128,256]{1,0:T(8,128)S(1)}, f32[128,256]{1,0:T(8,128)S(1)}, u32[]{:S(2)}, u32[]{:S(2)}) %collective-permute-start.12) | collective-permute-done | bytes 131104 | tf_op jit(solution)/shard_map/ppermute | solution.py:344
  81.7 1.3 collective-permute-start.3
  83.0 1.5 collective-permute-done.13
  84.6 1.6 collective-permute-start.15
  86.1 0.9 fusion.13
  87.0 0.8 slice.82.refs_4_
  87.9 3.1 %cut_piece.9 = (f32[576,256]{1,0:T(8,128)}, f32[576,256]{1,0:T(8,128)}, f32[576,256]{1,0:T(8,128)}, f32[576,256]{1,0:T(8,128)}) custom-call(f32[512,4096]{1,0:T(8,128)} %refs_0_.5, f32[64,4096]{1,0:T(8,128)} %refs_1_.9), custom_call_target="tpu_custom_call" | custom-call | bytes 4718592 | tf_op jit(solution)/shard_map/cut_piece/pallas_call | solution.py:74
  90.9 2.3 collective-permute-start.10
  93.2 2.6 collective-permute-start.11
  95.8 38.2 %collective-permute-done.2.refs_2_ = f32[576,256]{1,0:T(8,128)} collective-permute-done((f32[576,256]{1,0:T(8,128)}, f32[576,256]{1,0:T(8,128)}, u32[]{:S(2)}, u32[]{:S(2)}) %collective-permute-start.2) | collective-permute-done | bytes 589856 | tf_op jit(solution)/shard_map/ppermute | solution.py:344
  134.2 0.5 collective-permute-start.16
  134.7 0.9 fusion.11
  135.6 0.8 slice.81.refs_3_.refs_4_
  136.4 2.9 %cut_piece.8 = (f32[512,256]{1,0:T(8,128)}, f32[512,256]{1,0:T(8,128)}, f32[512,256]{1,0:T(8,128)}, f32[512,256]{1,0:T(8,128)}) custom-call(f32[512,4096]{1,0:T(8,128)} %refs_0_.5, f32[64,4096]{1,0:T(8,128)} %refs_1_.9), custom_call_target="tpu_custom_call" | custom-call | bytes 4194304 | tf_op jit(solution)/shard_map/cut_piece/pallas_call | solution.py:74
  139.4 0.8 slice.117.refs_7_
  140.2 0.8 slice.116.refs_6_
  141.1 0.8 slice.115.refs_5_
  141.9 30.0 %collective-permute-start.4 = (f32[512,256]{1,0:T(8,128)}, f32[512,256]{1,0:T(8,128)S(1)}, u32[]{:S(2)}, u32[]{:S(2)}) collective-permute-start(f32[512,256]{1,0:T(8,128)} %get-tuple-element.87), channel_id=1, source_target_pairs={{0,4},{4,0},{8,12},{12,8},{1,5},{5,1},{9,13},{13,9},{2,6},{6,2},{1... | collective-permute-start | bytes 1572872 | tf_op jit(solution)/shard_map/ppermute | solution.py:344
  171.9 0.8 slice.120.refs_6_.refs_7_
  172.8 1.9 collective-permute-start.5
  174.7 0.8 slice.119.refs_5_.refs_6_
  175.6 1.5 collective-permute-start.6
  177.1 0.8 slice.118.refs_4_.refs_5_
  178.0 1.3 prepare_w.1
  179.3 8.7 %update_piece.4 = (f32[64,256]{1,0:T(8,128)S(1)}, f32[64,256]{1,0:T(8,128)S(1)}, f32[64,256]{1,0:T(8,128)S(1)}, f32[64,256]{1,0:T(8,128)S(1)}, f32[4,2,136,256]{...) custom-call(f32[640,256]{1,0:T(8,128)S(1)} %copy-done.2, f32[640,256]{1,0:T(8,128)S(1)} %copy-done.4, ...), custom_call_target="tpu_custom_call" | custom-call | flops 4026531840 | bytes 10485760 | tf_op jit(solution)/shard_map/update_piece/pallas_call | solution.py:249
  188.0 9.7 %update_piece.5 = (f32[64,256]{1,0:T(8,128)S(1)}, f32[64,256]{1,0:T(8,128)S(1)}, f32[64,256]{1,0:T(8,128)S(1)}, f32[64,256]{1,0:T(8,128)S(1)}, f32[4,2,136,256]{...) custom-call(f32[576,256]{1,0:T(8,128)S(1)} %copy-done.5, ...), custom_call_target="tpu_custom_call", output_to_operand_aliasing={{4}: (13, {}), {5}: (14, {})} | custom-call | flops 4026531840 | bytes 10485760 | tf_op jit(solution)/shard_map/update_piece/pallas_call | solution.py:249
  197.7 9.5 %update_piece.6 = (f32[64,256]{1,0:T(8,128)S(1)}, f32[64,256]{1,0:T(8,128)S(1)}, f32[64,256]{1,0:T(8,128)S(1)}, f32[64,256]{1,0:T(8,128)S(1)}, f32[4,2,136,256]{...) custom-call(f32[576,256]{1,0:T(8,128)S(1)} %copy-done.6, ...), custom_call_target="tpu_custom_call", output_to_operand_aliasing={{4}: (13, {}), {5}: (14, {})} | custom-call | flops 4026531840 | bytes 10485760 | tf_op jit(solution)/shard_map/update_piece/pallas_call | solution.py:249
  207.3 3.9 %collective-permute-done.5.refs_2_ = f32[512,256]{1,0:T(8,128)S(1)} collective-permute-done((f32[512,256]{1,0:T(8,128)}, f32[512,256]{1,0:T(8,128)S(1)}, u32[]{:S(2)}, u32[]{:S(2)}) %collective-permute-start.5) | collective-permute-done | bytes 524320 | tf_op jit(solution)/shard_map/ppermute | solution.py:344
  211.2 1.8 begin_piece.1.refs_13_
  213.1 3.4 %collective-permute-start.19 = (f32[64,256]{1,0:T(8,128)S(1)}, f32[64,256]{1,0:T(8,128)S(1)}, u32[]{:S(2)}, u32[]{:S(2)}) collective-permute-start(f32[64,256]{1,0:T(8,128)S(1)} %get-tuple-element.130), channel_id=1, source_target_pairs={{0,12},{4,8},{8,4},{12,0},{1,13},{5,9},{9,5},{13,1},{2,14},{6,10},... | collective-permute-start | bytes 196616 | tf_op jit(solution)/shard_map/ppermute | solution.py:344
  216.5 1.0 collective-permute-start.17
  217.5 7.8 %update_piece.7 = (f32[64,256]{1,0:T(8,128)S(1)}, f32[64,256]{1,0:T(8,128)S(1)}, f32[64,256]{1,0:T(8,128)S(1)}, f32[64,256]{1,0:T(8,128)S(1)}, f32[4,2,136,256]{...) custom-call(f32[512,256]{1,0:T(8,128)S(1)} %copy-done.1, ...), custom_call_target="tpu_custom_call", output_to_operand_aliasing={{4}: (14, {}), {5}: (15, {})} | custom-call | flops 4026531840 | bytes 10485760 | tf_op jit(solution)/shard_map/update_piece/pallas_call | solution.py:249
  225.3 1.5 collective-permute-done.18
  226.8 3.1 %collective-permute-done.20 = f32[4,2,136,256]{3,2,1,0:T(8,128)} collective-permute-done((f32[4,2,136,256]{3,2,1,0:T(8,128)}, f32[4,2,136,256]{3,2,1,0:T(8,128)}, u32[]{:S(2)}, u32[]{:S(2)}) %collective-permute-start.20) | collective-permute-done | bytes 1114144 | tf_op jit(solution)/shard_map/ppermute | solution.py:306
  229.9 1.2 add_bitcast_fusion
  231.1 1.5 collective-permute-start.24
  232.6 3.4 %collective-permute-start.23 = (f32[192,256]{1,0:T(8,128)S(1)}, f32[192,256]{1,0:T(8,128)S(1)}, u32[]{:S(2)}, u32[]{:S(2)}) collective-permute-start(f32[192,256]{1,0:T(8,128)S(1)} %pad_maximum_fusion.3), channel_id=1, source_target_pairs={{0,12},{4,8},{8,4},{12,0},{1,13},{5,9},{9,5},{13,1},{2,14},{6,10},... | collective-permute-start | bytes 589832 | tf_op jit(solution)/shard_map/ppermute | solution.py:344
  236.1 5.4 %collective-permute-start.22 = (f32[192,256]{1,0:T(8,128)S(1)}, f32[192,256]{1,0:T(8,128)S(1)}, u32[]{:S(2)}, u32[]{:S(2)}) collective-permute-start(f32[192,256]{1,0:T(8,128)S(1)} %pad_maximum_fusion.2), channel_id=1, source_target_pairs={{0,8},{4,12},{8,0},{12,4},{1,9},{5,13},{9,1},{13,5},{2,10},{6,14},... | collective-permute-start | bytes 589832 | tf_op jit(solution)/shard_map/ppermute | solution.py:344
  241.6 0.6 collective-permute-start.21
  242.2 1.1 fusion
  243.3 11.5 %collective-permute-done.22 = f32[192,256]{1,0:T(8,128)S(1)} collective-permute-done((f32[192,256]{1,0:T(8,128)S(1)}, f32[192,256]{1,0:T(8,128)S(1)}, u32[]{:S(2)}, u32[]{:S(2)}) %collective-permute-start.22) | collective-permute-done | bytes 196640 | tf_op jit(solution)/shard_map/ppermute | solution.py:344
  254.9 3.2 %collective-permute-start.26 = (f32[136,256]{1,0:T(8,128)S(1)}, f32[136,256]{1,0:T(8,128)S(1)}, u32[]{:S(2)}, u32[]{:S(2)}) collective-permute-start(f32[136,256]{1,0:T(8,128)S(1)} %get-tuple-element.156), channel_id=1, source_target_pairs={{0,8},{4,12},{8,0},{12,4},{1,9},{5,13},{9,1},{13,5},{2,10},{6,14},... | collective-permute-start | bytes 417800 | tf_op jit(solution)/shard_map/ppermute | solution.py:344
  258.1 1.2 collective-permute-start.27
  259.3 2.8 %collective-permute-done.25 = f32[136,256]{1,0:T(8,128)S(1)} collective-permute-done((f32[136,256]{1,0:T(8,128)S(1)}, f32[136,256]{1,0:T(8,128)S(1)}, u32[]{:S(2)}, u32[]{:S(2)}) %collective-permute-start.25) | collective-permute-done | bytes 139296 | tf_op jit(solution)/shard_map/ppermute | solution.py:344
  262.1 6.0 %collective-permute-done.26 = f32[136,256]{1,0:T(8,128)S(1)} collective-permute-done((f32[136,256]{1,0:T(8,128)S(1)}, f32[136,256]{1,0:T(8,128)S(1)}, u32[]{:S(2)}, u32[]{:S(2)}) %collective-permute-start.26) | collective-permute-done | bytes 139296 | tf_op jit(solution)/shard_map/ppermute | solution.py:344
  268.3 0.6 collective-permute-start.29
  269.0 0.1 copy.19
  269.2 0.1 copy.22
  269.4 0.1 copy.21
  269.6 0.1 copy.20
  269.7 3.6 %collective-permute-done.29 = f32[128,256]{1,0:T(8,128)S(1)} collective-permute-done((f32[128,256]{1,0:T(8,128)S(1)}, f32[128,256]{1,0:T(8,128)S(1)}, u32[]{:S(2)}, u32[]{:S(2)}) %collective-permute-start.29) | collective-permute-done | bytes 131104 | tf_op jit(solution)/shard_map/ppermute | solution.py:293
  273.4 1.3 collective-permute-done.30
  275.0 0.9 copy-done.7
  276.0 0.8 copy-done.8
  (73 shorter events, 0.9 us)
Async XLA Ops:
  3.1 53.6 %collective-permute-start.7 = (f32[768,256]{1,0:T(8,128)}, f32[768,256]{1,0:T(8,128)S(1)}, u32[]{:S(2)}, u32[]{:S(2)}) collective-permute-start(f32[768,256]{1,0:T(8,128)} %get-tuple-element.78), channel_id=1, source_target_pairs={{0,8},{4,12},{8,0},{12,4},{1,9},{5,13},{9,1},{13,5},{2,10},{6,14},... | collective-permute-start | bytes 2359304 | tf_op jit(solution)/shard_map/ppermute | solution.py:344
  9.6 30.0 %collective-permute-start = (f32[640,256]{1,0:T(8,128)}, f32[640,256]{1,0:T(8,128)S(1)}, u32[]{:S(2)}, u32[]{:S(2)}) collective-permute-start(f32[640,256]{1,0:T(8,128)} %get-tuple-element.80), channel_id=1, source_target_pairs={{0,4},{4,0},{8,12},{12,8},{1,5},{5,1},{9,13},{13,9},{2,6},{6,2},{1... | collective-permute-start | bytes 1966088 | tf_op jit(solution)/shard_map/ppermute | solution.py:344
  11.2 76.6 %collective-permute-start.8 = (f32[640,256]{1,0:T(8,128)}, f32[640,256]{1,0:T(8,128)}, u32[]{:S(2)}, u32[]{:S(2)}) collective-permute-start(f32[640,256]{1,0:T(8,128)} %get-tuple-element.77), channel_id=1, source_target_pairs={{0,12},{4,8},{8,4},{12,0},{1,13},{5,9},{9,5},{13,1},{2,14},{6,10},... | collective-permute-start | bytes 1966088 | tf_op jit(solution)/shard_map/ppermute | solution.py:344
  11.2 34.1 %copy-start = (f32[512,256]{1,0:T(8,128)S(1)}, f32[512,256]{1,0:T(8,128)}, u32[]{:S(2)}) copy-start(f32[512,256]{1,0:T(8,128)} %own_ref.1) | copy-start | bytes 1572868
  39.6 94.5 %copy-start.3 = (f32[640,256]{1,0:T(8,128)}, f32[640,256]{1,0:T(8,128)S(1)}, u32[]{:S(2)}) copy-start(f32[640,256]{1,0:T(8,128)S(1)} %collective-permute-done.refs_1_) | copy-start | bytes 1966084
  42.9 50.3 %collective-permute-start.1 = (f32[576,256]{1,0:T(8,128)}, f32[576,256]{1,0:T(8,128)}, u32[]{:S(2)}, u32[]{:S(2)}) collective-permute-start(f32[576,256]{1,0:T(8,128)} %get-tuple-element.82), channel_id=1, source_target_pairs={{0,4},{4,0},{8,12},{12,8},{1,5},{5,1},{9,13},{13,9},{2,6},{6,2},{1... | collective-permute-start | bytes 1769480 | tf_op jit(solution)/shard_map/ppermute | solution.py:344
  45.4 88.7 %collective-permute-start.2 = (f32[576,256]{1,0:T(8,128)}, f32[576,256]{1,0:T(8,128)}, u32[]{:S(2)}, u32[]{:S(2)}) collective-permute-start(f32[576,256]{1,0:T(8,128)} %get-tuple-element.83), channel_id=1, source_target_pairs={{0,8},{4,12},{8,0},{12,4},{1,9},{5,13},{9,1},{13,5},{2,10},{6,14},... | collective-permute-start | bytes 1769480 | tf_op jit(solution)/shard_map/ppermute | solution.py:344
  45.4 36.3 %collective-permute-start.12 = (f32[128,256]{1,0:T(8,128)S(1)}, f32[128,256]{1,0:T(8,128)S(1)}, u32[]{:S(2)}, u32[]{:S(2)}) collective-permute-start(f32[128,256]{1,0:T(8,128)S(1)} %constant_dynamic-slice_fusion), channel_id=1, source_target_pairs={{0,4},{4,0},{8,12},{12,8},{1,5},{5,1},{9,13},{13,9},{2,6},{6,2},{1... | collective-permute-start | bytes 393224 | tf_op jit(solution)/shard_map/ppermute | solution.py:344
  56.7 27.8 %collective-permute-start.13 = (f32[128,256]{1,0:T(8,128)S(1)}, f32[128,256]{1,0:T(8,128)S(1)}, u32[]{:S(2)}, u32[]{:S(2)}) collective-permute-start(f32[128,256]{1,0:T(8,128)S(1)} %slice.111), channel_id=1, source_target_pairs={{0,4},{4,0},{8,12},{12,8},{1,5},{5,1},{9,13},{13,9},{2,6},{6,2},{1... | collective-permute-start | bytes 393224 | tf_op jit(solution)/shard_map/ppermute | solution.py:344
  81.7 52.4 %collective-permute-start.3 = (f32[576,256]{1,0:T(8,128)}, f32[576,256]{1,0:T(8,128)}, u32[]{:S(2)}, u32[]{:S(2)}) collective-permute-start(f32[576,256]{1,0:T(8,128)} %get-tuple-element.84), channel_id=1, source_target_pairs={{0,12},{4,8},{8,4},{12,0},{1,13},{5,9},{9,5},{13,1},{2,14},{6,10},... | collective-permute-start | bytes 1769480 | tf_op jit(solution)/shard_map/ppermute | solution.py:344
  84.6 49.6 %collective-permute-start.15 = (f32[384,256]{1,0:T(8,128)S(1)}, f32[384,256]{1,0:T(8,128)S(1)}, u32[]{:S(2)}, u32[]{:S(2)}) collective-permute-start(f32[384,256]{1,0:T(8,128)S(1)} %pad_maximum_fusion.refs_0_), channel_id=1, source_target_pairs={{0,2},{1,3},{2,0},{3,1},{4,6},{5,7},{6,4},{7,5},{8,10},{9,11},{10,... | collective-permute-start | bytes 1179656 | tf_op jit(solution)/shard_map/ppermute | solution.py:293
  90.9 81.9 %collective-permute-start.10 = (f32[576,256]{1,0:T(8,128)}, f32[576,256]{1,0:T(8,128)}, u32[]{:S(2)}, u32[]{:S(2)}) collective-permute-start(f32[576,256]{1,0:T(8,128)} %get-tuple-element.93), channel_id=1, source_target_pairs={{0,8},{4,12},{8,0},{12,4},{1,9},{5,13},{9,1},{13,5},{2,10},{6,14},... | collective-permute-start | bytes 1769480 | tf_op jit(solution)/shard_map/ppermute | solution.py:344
  93.2 48.7 %collective-permute-start.11 = (f32[576,256]{1,0:T(8,128)}, f32[576,256]{1,0:T(8,128)}, u32[]{:S(2)}, u32[]{:S(2)}) collective-permute-start(f32[576,256]{1,0:T(8,128)} %get-tuple-element.94), channel_id=1, source_target_pairs={{0,12},{4,8},{8,4},{12,0},{1,13},{5,9},{9,5},{13,1},{2,14},{6,10},... | collective-permute-start | bytes 1769480 | tf_op jit(solution)/shard_map/ppermute | solution.py:344
  134.1 41.5 %collective-permute-start.9 = (f32[576,256]{1,0:T(8,128)}, f32[576,256]{1,0:T(8,128)}, u32[]{:S(2)}, u32[]{:S(2)}) collective-permute-start(f32[576,256]{1,0:T(8,128)} %get-tuple-element.92), channel_id=1, source_target_pairs={{0,4},{4,0},{8,12},{12,8},{1,5},{5,1},{9,13},{13,9},{2,6},{6,2},{1... | collective-permute-start | bytes 1769480 | tf_op jit(solution)/shard_map/ppermute | solution.py:344
  134.1 43.8 %collective-permute-start.14 = (f32[384,256]{1,0:T(8,128)S(1)}, f32[384,256]{1,0:T(8,128)S(1)}, u32[]{:S(2)}, u32[]{:S(2)}) collective-permute-start(f32[384,256]{1,0:T(8,128)S(1)} %pad_maximum_fusion.refs_0_), channel_id=1, source_target_pairs={{0,1},{1,0},{2,3},{3,2},{4,5},{5,4},{6,7},{7,6},{8,9},{9,8},{10,11... | collective-permute-start | bytes 1179656 | tf_op jit(solution)/shard_map/ppermute | solution.py:293
  134.2 43.8 %collective-permute-start.16 = (f32[384,256]{1,0:T(8,128)S(1)}, f32[384,256]{1,0:T(8,128)S(1)}, u32[]{:S(2)}, u32[]{:S(2)}) collective-permute-start(f32[384,256]{1,0:T(8,128)S(1)} %collective-permute-done.15.refs_2_), channel_id=1, source_target_pairs={{0,1},{1,0},{2,3},{3,2},{4,5},{5,4},{6,7},{7,6},{8,9},{9,8},{10,11... | collective-permute-start | bytes 1179656 | tf_op jit(solution)/shard_map/ppermute | solution.py:293
  141.9 65.3 %collective-permute-start.4 = (f32[512,256]{1,0:T(8,128)}, f32[512,256]{1,0:T(8,128)S(1)}, u32[]{:S(2)}, u32[]{:S(2)}) collective-permute-start(f32[512,256]{1,0:T(8,128)} %get-tuple-element.87), channel_id=1, source_target_pairs={{0,4},{4,0},{8,12},{12,8},{1,5},{5,1},{9,13},{13,9},{2,6},{6,2},{1... | collective-permute-start | bytes 1572872 | tf_op jit(solution)/shard_map/ppermute | solution.py:344
  172.8 38.4 %collective-permute-start.5 = (f32[512,256]{1,0:T(8,128)}, f32[512,256]{1,0:T(8,128)S(1)}, u32[]{:S(2)}, u32[]{:S(2)}) collective-permute-start(f32[512,256]{1,0:T(8,128)} %get-tuple-element.88), channel_id=1, source_target_pairs={{0,8},{4,12},{8,0},{12,4},{1,9},{5,13},{9,1},{13,5},{2,10},{6,14},... | collective-permute-start | bytes 1572872 | tf_op jit(solution)/shard_map/ppermute | solution.py:344
  175.6 3.7 %copy-start.2 = (f32[640,256]{1,0:T(8,128)S(1)}, f32[640,256]{1,0:T(8,128)}, u32[]{:S(2)}) copy-start(f32[640,256]{1,0:T(8,128)} %get-tuple-element.96.refs_0_) | copy-start | bytes 1966084
  175.6 3.7 %copy-start.4 = (f32[640,256]{1,0:T(8,128)S(1)}, f32[640,256]{1,0:T(8,128)}, u32[]{:S(2)}) copy-start(f32[640,256]{1,0:T(8,128)} %copy-done.3) | copy-start | bytes 1966084
  175.6 41.9 %collective-permute-start.6 = (f32[512,256]{1,0:T(8,128)}, f32[512,256]{1,0:T(8,128)S(1)}, u32[]{:S(2)}, u32[]{:S(2)}) collective-permute-start(f32[512,256]{1,0:T(8,128)} %get-tuple-element.89), channel_id=1, source_target_pairs={{0,12},{4,8},{8,4},{12,0},{1,13},{5,9},{9,5},{13,1},{2,14},{6,10},... | collective-permute-start | bytes 1572872 | tf_op jit(solution)/shard_map/ppermute | solution.py:344
  179.2 8.7 %copy-start.5 = (f32[576,256]{1,0:T(8,128)S(1)}, f32[576,256]{1,0:T(8,128)}, u32[]{:S(2)}) copy-start(f32[576,256]{1,0:T(8,128)} %get-tuple-element.95.refs_0_) | copy-start | bytes 1769476
  188.0 9.7 %copy-start.6 = (f32[576,256]{1,0:T(8,128)S(1)}, f32[576,256]{1,0:T(8,128)}, u32[]{:S(2)}) copy-start(f32[576,256]{1,0:T(8,128)} %get-tuple-element.91.refs_0_) | copy-start | bytes 1769476
  197.7 13.5 %copy-start.1 = (f32[512,256]{1,0:T(8,128)S(1)}, f32[512,256]{1,0:T(8,128)}, u32[]{:S(2)}) copy-start(f32[512,256]{1,0:T(8,128)} %get-tuple-element.86.refs_0_) | copy-start | bytes 1572868
  213.1 12.2 %collective-permute-start.19 = (f32[64,256]{1,0:T(8,128)S(1)}, f32[64,256]{1,0:T(8,128)S(1)}, u32[]{:S(2)}, u32[]{:S(2)}) collective-permute-start(f32[64,256]{1,0:T(8,128)S(1)} %get-tuple-element.130), channel_id=1, source_target_pairs={{0,12},{4,8},{8,4},{12,0},{1,13},{5,9},{9,5},{13,1},{2,14},{6,10},... | collective-permute-start | bytes 196616 | tf_op jit(solution)/shard_map/ppermute | solution.py:344
  216.5 10.3 %collective-permute-start.18 = (f32[64,256]{1,0:T(8,128)S(1)}, f32[64,256]{1,0:T(8,128)S(1)}, u32[]{:S(2)}, u32[]{:S(2)}) collective-permute-start(f32[64,256]{1,0:T(8,128)S(1)} %get-tuple-element.128), channel_id=1, source_target_pairs={{0,8},{4,12},{8,0},{12,4},{1,9},{5,13},{9,1},{13,5},{2,10},{6,14},... | collective-permute-start | bytes 196616 | tf_op jit(solution)/shard_map/ppermute | solution.py:344
  216.5 10.3 %collective-permute-start.17 = (f32[64,256]{1,0:T(8,128)S(1)}, f32[64,256]{1,0:T(8,128)S(1)}, u32[]{:S(2)}, u32[]{:S(2)}) collective-permute-start(f32[64,256]{1,0:T(8,128)S(1)} %get-tuple-element.126), channel_id=1, source_target_pairs={{0,4},{4,0},{8,12},{12,8},{1,5},{5,1},{9,13},{13,9},{2,6},{6,2},{1... | collective-permute-start | bytes 196616 | tf_op jit(solution)/shard_map/ppermute | solution.py:344
  226.8 3.1 %collective-permute-start.20 = (f32[4,2,136,256]{3,2,1,0:T(8,128)}, f32[4,2,136,256]{3,2,1,0:T(8,128)}, u32[]{:S(2)}, u32[]{:S(2)}) collective-permute-start(f32[4,2,136,256]{3,2,1,0:T(8,128)} %get-tuple-element.131), channel_id=1, source_target_pairs={{0,1},{1,0},{2,3},{3,2},{4,5},{5,4},{6,7},{7,6},{8,9},{9,8},{10,11... | collective-permute-start | bytes 3342344 | tf_op jit(solution)/shard_map/ppermute | solution.py:306
  231.1 23.7 %collective-permute-start.24 = (f32[4,136,256]{2,1,0:T(8,128)S(1)}, f32[4,136,256]{2,1,0:T(8,128)S(1)}, u32[]{:S(2)}, u32[]{:S(2)}) collective-permute-start(f32[4,136,256]{2,1,0:T(8,128)S(1)} %add_bitcast_fusion), channel_id=1, source_target_pairs={{0,2},{1,3},{2,0},{3,1},{4,6},{5,7},{6,4},{7,5},{8,10},{9,11},{10,... | collective-permute-start | bytes 1671176 | tf_op jit(solution)/shard_map/ppermute | solution.py:316
  232.6 10.7 %collective-permute-start.23 = (f32[192,256]{1,0:T(8,128)S(1)}, f32[192,256]{1,0:T(8,128)S(1)}, u32[]{:S(2)}, u32[]{:S(2)}) collective-permute-start(f32[192,256]{1,0:T(8,128)S(1)} %pad_maximum_fusion.3), channel_id=1, source_target_pairs={{0,12},{4,8},{8,4},{12,0},{1,13},{5,9},{9,5},{13,1},{2,14},{6,10},... | collective-permute-start | bytes 589832 | tf_op jit(solution)/shard_map/ppermute | solution.py:344
  236.1 18.7 %collective-permute-start.22 = (f32[192,256]{1,0:T(8,128)S(1)}, f32[192,256]{1,0:T(8,128)S(1)}, u32[]{:S(2)}, u32[]{:S(2)}) collective-permute-start(f32[192,256]{1,0:T(8,128)S(1)} %pad_maximum_fusion.2), channel_id=1, source_target_pairs={{0,8},{4,12},{8,0},{12,4},{1,9},{5,13},{9,1},{13,5},{2,10},{6,14},... | collective-permute-start | bytes 589832 | tf_op jit(solution)/shard_map/ppermute | solution.py:344
  241.6 13.2 %collective-permute-start.21 = (f32[192,256]{1,0:T(8,128)S(1)}, f32[192,256]{1,0:T(8,128)S(1)}, u32[]{:S(2)}, u32[]{:S(2)}) collective-permute-start(f32[192,256]{1,0:T(8,128)S(1)} %pad_maximum_fusion.1), channel_id=1, source_target_pairs={{0,4},{4,0},{8,12},{12,8},{1,5},{5,1},{9,13},{13,9},{2,6},{6,2},{1... | collective-permute-start | bytes 589832 | tf_op jit(solution)/shard_map/ppermute | solution.py:344
  254.9 7.3 %collective-permute-start.25 = (f32[136,256]{1,0:T(8,128)S(1)}, f32[136,256]{1,0:T(8,128)S(1)}, u32[]{:S(2)}, u32[]{:S(2)}) collective-permute-start(f32[136,256]{1,0:T(8,128)S(1)} %get-tuple-element.154), channel_id=1, source_target_pairs={{0,4},{4,0},{8,12},{12,8},{1,5},{5,1},{9,13},{13,9},{2,6},{6,2},{1... | collective-permute-start | bytes 417800 | tf_op jit(solution)/shard_map/ppermute | solution.py:344
  254.9 13.2 %collective-permute-start.26 = (f32[136,256]{1,0:T(8,128)S(1)}, f32[136,256]{1,0:T(8,128)S(1)}, u32[]{:S(2)}, u32[]{:S(2)}) collective-permute-start(f32[136,256]{1,0:T(8,128)S(1)} %get-tuple-element.156), channel_id=1, source_target_pairs={{0,8},{4,12},{8,0},{12,4},{1,9},{5,13},{9,1},{13,5},{2,10},{6,14},... | collective-permute-start | bytes 417800 | tf_op jit(solution)/shard_map/ppermute | solution.py:344
  258.1 10.1 %collective-permute-start.27 = (f32[136,256]{1,0:T(8,128)S(1)}, f32[136,256]{1,0:T(8,128)S(1)}, u32[]{:S(2)}, u32[]{:S(2)}) collective-permute-start(f32[136,256]{1,0:T(8,128)S(1)} %get-tuple-element.155), channel_id=1, source_target_pairs={{0,12},{4,8},{8,4},{12,0},{1,13},{5,9},{9,5},{13,1},{2,14},{6,10},... | collective-permute-start | bytes 417800 | tf_op jit(solution)/shard_map/ppermute | solution.py:344
  268.3 5.0 %collective-permute-start.29 = (f32[128,256]{1,0:T(8,128)S(1)}, f32[128,256]{1,0:T(8,128)S(1)}, u32[]{:S(2)}, u32[]{:S(2)}) collective-permute-start(f32[128,256]{1,0:T(8,128)S(1)} %get-tuple-element.153), channel_id=1, source_target_pairs={{0,2},{1,3},{2,0},{3,1},{4,6},{5,7},{6,4},{7,5},{8,10},{9,11},{10,... | collective-permute-start | bytes 393224 | tf_op jit(solution)/shard_map/ppermute | solution.py:293
  269.0 4.4 %collective-permute-start.28 = (f32[128,256]{1,0:T(8,128)S(1)}, f32[128,256]{1,0:T(8,128)S(1)}, u32[]{:S(2)}, u32[]{:S(2)}) collective-permute-start(f32[128,256]{1,0:T(8,128)S(1)} %get-tuple-element.153), channel_id=1, source_target_pairs={{0,1},{1,0},{2,3},{3,2},{4,5},{5,4},{6,7},{7,6},{8,9},{9,8},{10,11... | collective-permute-start | bytes 393224 | tf_op jit(solution)/shard_map/ppermute | solution.py:293
  273.4 1.3 collective-permute-start.30
  275.0 1.0 copy-start.7
  276.0 0.8 copy-start.8

commit v5 on v4

--- a/solution.py
+++ b/solution.py
@@ -10,7 +10,7 @@
 INNER = 2
 WIDTH = 256
 PAD = 8
-VMEM = 20 * 1024 * 1024
+VMEM = 17 * 1024 * 1024
 NT = (((1,), (1,)), ((), ()))
 
 

time: 278 us -> 278 us (level)
  no operation moved by 1% of the time
where the time goes in v5:
time: 278 us; the launch traced here: 277 us
  waiting for transfers between devices  136 us (49%)
  starting transfers between devices  72.7 us (26%)
  Pallas kernels  53.1 us (19%)
  local copies, waits for them, and re-layouts  11.3 us (4%)
    ppermute x23, waiting for transfers between devices, send(): return lax.ppermute(value, 'doc', xor_pairs(n_doc, k)) if k else value  128 us
    ppermute x23, starting transfers between devices, send(): return lax.ppermute(value, 'doc', xor_pairs(n_doc, k)) if k else value  68.4 us
    pallas_call x4, Pallas kernels, update_piece(): pl.pallas_call(functools.partial(piece_kernel, blocks, parts, rows, early...  35.8 us
    pallas_call x5, Pallas kernels, cut(): pl.pallas_call(functools.partial(cut_kernel, spec), out_shape=[jax.ShapeD...  14.2 us
    slice x12, local copies, waits for them, and re-layouts, body(): h_blocks = [after(m[at:at + share], ready) for m in m_pieces[source]]  8.53 us
  transfers between devices with their start and end apart: 31, of which 13 were waited for; matrix products, arithmetic and copies ran while one was open for 4% of the time, Pallas kernels for 18%

profile of v5, /device:TPU:0, one launch (start us, length us, event | category | flops | bytes accessed | tf_op | source)
XLA Modules:
  0.0 276.8 jit_solution(14265768651474439313)
XLA Ops:
  0.6 2.5 cut_piece.5
  3.1 4.1 %collective-permute-start.7 = (f32[768,256]{1,0:T(8,128)}, f32[768,256]{1,0:T(8,128)S(1)}, u32[]{:S(2)}, u32[]{:S(2)}) collective-permute-start(f32[768,256]{1,0:T(8,128)} %get-tuple-element.78), channel_id=1, source_target_pairs={{0,8},{4,12},{8,0},{12,4},{1,9},{5,13},{9,1},{13,5},{2,10},{6,14},... | collective-permute-start | bytes 2359304 | tf_op jit(solution)/shard_map/ppermute | solution.py:344
  7.2 2.4 cut_piece.6
  9.6 1.6 collective-permute-start
  11.2 28.3 %collective-permute-done.refs_1_ = f32[640,256]{1,0:T(8,128)S(1)} collective-permute-done((f32[640,256]{1,0:T(8,128)}, f32[640,256]{1,0:T(8,128)S(1)}, u32[]{:S(2)}, u32[]{:S(2)}) %collective-permute-start) | collective-permute-done | bytes 655392 | tf_op jit(solution)/shard_map/ppermute | solution.py:344
  39.6 3.4 %cut_piece.7 = (f32[576,256]{1,0:T(8,128)}, f32[576,256]{1,0:T(8,128)}, f32[576,256]{1,0:T(8,128)}, f32[576,256]{1,0:T(8,128)}) custom-call(f32[512,4096]{1,0:T(8,128)} %refs_0_.5, f32[64,4096]{1,0:T(8,128)} %refs_1_.9), custom_call_target="tpu_custom_call" | custom-call | bytes 4718592 | tf_op jit(solution)/shard_map/cut_piece/pallas_call | solution.py:74
  42.9 2.4 collective-permute-start.1
  45.4 1.9 collective-permute-start.12
  47.3 9.4 %collective-permute-done.7.refs_2_ = f32[768,256]{1,0:T(8,128)S(1)} collective-permute-done((f32[768,256]{1,0:T(8,128)}, f32[768,256]{1,0:T(8,128)S(1)}, u32[]{:S(2)}, u32[]{:S(2)}) %collective-permute-start.7) | collective-permute-done | bytes 786464 | tf_op jit(solution)/shard_map/ppermute | solution.py:344
  56.7 0.2 collective-permute-start.13
  56.9 24.8 %collective-permute-done.12 = f32[128,256]{1,0:T(8,128)S(1)} collective-permute-done((f32[128,256]{1,0:T(8,128)S(1)}, f32[128,256]{1,0:T(8,128)S(1)}, u32[]{:S(2)}, u32[]{:S(2)}) %collective-permute-start.12) | collective-permute-done | bytes 131104 | tf_op jit(solution)/shard_map/ppermute | solution.py:344
  81.7 1.3 collective-permute-start.3
  83.0 1.5 collective-permute-done.13
  84.6 1.6 collective-permute-start.15
  86.1 0.9 fusion.13
  87.0 0.8 slice.82.refs_4_
  87.9 3.1 %cut_piece.9 = (f32[576,256]{1,0:T(8,128)}, f32[576,256]{1,0:T(8,128)}, f32[576,256]{1,0:T(8,128)}, f32[576,256]{1,0:T(8,128)}) custom-call(f32[512,4096]{1,0:T(8,128)} %refs_0_.5, f32[64,4096]{1,0:T(8,128)} %refs_1_.9), custom_call_target="tpu_custom_call" | custom-call | bytes 4718592 | tf_op jit(solution)/shard_map/cut_piece/pallas_call | solution.py:74
  90.9 2.3 collective-permute-start.10
  93.2 2.6 collective-permute-start.11
  95.8 38.2 %collective-permute-done.2.refs_2_ = f32[576,256]{1,0:T(8,128)} collective-permute-done((f32[576,256]{1,0:T(8,128)}, f32[576,256]{1,0:T(8,128)}, u32[]{:S(2)}, u32[]{:S(2)}) %collective-permute-start.2) | collective-permute-done | bytes 589856 | tf_op jit(solution)/shard_map/ppermute | solution.py:344
  134.2 0.5 collective-permute-start.16
  134.7 0.9 fusion.11
  135.6 0.8 slice.81.refs_3_.refs_4_
  136.4 2.9 %cut_piece.8 = (f32[512,256]{1,0:T(8,128)}, f32[512,256]{1,0:T(8,128)}, f32[512,256]{1,0:T(8,128)}, f32[512,256]{1,0:T(8,128)}) custom-call(f32[512,4096]{1,0:T(8,128)} %refs_0_.5, f32[64,4096]{1,0:T(8,128)} %refs_1_.9), custom_call_target="tpu_custom_call" | custom-call | bytes 4194304 | tf_op jit(solution)/shard_map/cut_piece/pallas_call | solution.py:74
  139.4 0.8 slice.117.refs_7_
  140.2 0.8 slice.116.refs_6_
  141.1 0.8 slice.115.refs_5_
  141.9 30.0 %collective-permute-start.4 = (f32[512,256]{1,0:T(8,128)}, f32[512,256]{1,0:T(8,128)S(1)}, u32[]{:S(2)}, u32[]{:S(2)}) collective-permute-start(f32[512,256]{1,0:T(8,128)} %get-tuple-element.87), channel_id=1, source_target_pairs={{0,4},{4,0},{8,12},{12,8},{1,5},{5,1},{9,13},{13,9},{2,6},{6,2},{1... | collective-permute-start | bytes 1572872 | tf_op jit(solution)/shard_map/ppermute | solution.py:344
  171.9 0.8 slice.120.refs_6_.refs_7_
  172.8 1.9 collective-permute-start.5
  174.7 0.8 slice.119.refs_5_.refs_6_
  175.6 1.5 collective-permute-start.6
  177.1 0.8 slice.118.refs_4_.refs_5_
  178.0 1.3 prepare_w.1
  179.3 8.7 %update_piece.4 = (f32[64,256]{1,0:T(8,128)S(1)}, f32[64,256]{1,0:T(8,128)S(1)}, f32[64,256]{1,0:T(8,128)S(1)}, f32[64,256]{1,0:T(8,128)S(1)}, f32[4,2,136,256]{...) custom-call(f32[640,256]{1,0:T(8,128)S(1)} %copy-done.2, f32[640,256]{1,0:T(8,128)S(1)} %copy-done.4, ...), custom_call_target="tpu_custom_call" | custom-call | flops 4026531840 | bytes 10485760 | tf_op jit(solution)/shard_map/update_piece/pallas_call | solution.py:249
  188.0 9.7 %update_piece.5 = (f32[64,256]{1,0:T(8,128)S(1)}, f32[64,256]{1,0:T(8,128)S(1)}, f32[64,256]{1,0:T(8,128)S(1)}, f32[64,256]{1,0:T(8,128)S(1)}, f32[4,2,136,256]{...) custom-call(f32[576,256]{1,0:T(8,128)S(1)} %copy-done.5, ...), custom_call_target="tpu_custom_call", output_to_operand_aliasing={{4}: (13, {}), {5}: (14, {})} | custom-call | flops 4026531840 | bytes 10485760 | tf_op jit(solution)/shard_map/update_piece/pallas_call | solution.py:249
  197.7 9.5 %update_piece.6 = (f32[64,256]{1,0:T(8,128)S(1)}, f32[64,256]{1,0:T(8,128)S(1)}, f32[64,256]{1,0:T(8,128)S(1)}, f32[64,256]{1,0:T(8,128)S(1)}, f32[4,2,136,256]{...) custom-call(f32[576,256]{1,0:T(8,128)S(1)} %copy-done.6, ...), custom_call_target="tpu_custom_call", output_to_operand_aliasing={{4}: (13, {}), {5}: (14, {})} | custom-call | flops 4026531840 | bytes 10485760 | tf_op jit(solution)/shard_map/update_piece/pallas_call | solution.py:249
  207.3 3.9 %collective-permute-done.5.refs_2_ = f32[512,256]{1,0:T(8,128)S(1)} collective-permute-done((f32[512,256]{1,0:T(8,128)}, f32[512,256]{1,0:T(8,128)S(1)}, u32[]{:S(2)}, u32[]{:S(2)}) %collective-permute-start.5) | collective-permute-done | bytes 524320 | tf_op jit(solution)/shard_map/ppermute | solution.py:344
  211.2 1.8 begin_piece.1.refs_13_
  213.1 3.4 %collective-permute-start.19 = (f32[64,256]{1,0:T(8,128)S(1)}, f32[64,256]{1,0:T(8,128)S(1)}, u32[]{:S(2)}, u32[]{:S(2)}) collective-permute-start(f32[64,256]{1,0:T(8,128)S(1)} %get-tuple-element.130), channel_id=1, source_target_pairs={{0,12},{4,8},{8,4},{12,0},{1,13},{5,9},{9,5},{13,1},{2,14},{6,10},... | collective-permute-start | bytes 196616 | tf_op jit(solution)/shard_map/ppermute | solution.py:344
  216.5 1.0 collective-permute-start.17
  217.5 7.8 %update_piece.7 = (f32[64,256]{1,0:T(8,128)S(1)}, f32[64,256]{1,0:T(8,128)S(1)}, f32[64,256]{1,0:T(8,128)S(1)}, f32[64,256]{1,0:T(8,128)S(1)}, f32[4,2,136,256]{...) custom-call(f32[512,256]{1,0:T(8,128)S(1)} %copy-done.1, ...), custom_call_target="tpu_custom_call", output_to_operand_aliasing={{4}: (14, {}), {5}: (15, {})} | custom-call | flops 4026531840 | bytes 10485760 | tf_op jit(solution)/shard_map/update_piece/pallas_call | solution.py:249
  225.3 1.5 collective-permute-done.18
  226.8 3.1 %collective-permute-done.20 = f32[4,2,136,256]{3,2,1,0:T(8,128)} collective-permute-done((f32[4,2,136,256]{3,2,1,0:T(8,128)}, f32[4,2,136,256]{3,2,1,0:T(8,128)}, u32[]{:S(2)}, u32[]{:S(2)}) %collective-permute-start.20) | collective-permute-done | bytes 1114144 | tf_op jit(solution)/shard_map/ppermute | solution.py:306
  229.9 1.2 add_bitcast_fusion
  231.1 1.5 collective-permute-start.24
  232.6 3.4 %collective-permute-start.23 = (f32[192,256]{1,0:T(8,128)S(1)}, f32[192,256]{1,0:T(8,128)S(1)}, u32[]{:S(2)}, u32[]{:S(2)}) collective-permute-start(f32[192,256]{1,0:T(8,128)S(1)} %pad_maximum_fusion.3), channel_id=1, source_target_pairs={{0,12},{4,8},{8,4},{12,0},{1,13},{5,9},{9,5},{13,1},{2,14},{6,10},... | collective-permute-start | bytes 589832 | tf_op jit(solution)/shard_map/ppermute | solution.py:344
  236.1 5.4 %collective-permute-start.22 = (f32[192,256]{1,0:T(8,128)S(1)}, f32[192,256]{1,0:T(8,128)S(1)}, u32[]{:S(2)}, u32[]{:S(2)}) collective-permute-start(f32[192,256]{1,0:T(8,128)S(1)} %pad_maximum_fusion.2), channel_id=1, source_target_pairs={{0,8},{4,12},{8,0},{12,4},{1,9},{5,13},{9,1},{13,5},{2,10},{6,14},... | collective-permute-start | bytes 589832 | tf_op jit(solution)/shard_map/ppermute | solution.py:344
  241.6 0.6 collective-permute-start.21
  242.2 1.1 fusion
  243.3 11.5 %collective-permute-done.22 = f32[192,256]{1,0:T(8,128)S(1)} collective-permute-done((f32[192,256]{1,0:T(8,128)S(1)}, f32[192,256]{1,0:T(8,128)S(1)}, u32[]{:S(2)}, u32[]{:S(2)}) %collective-permute-start.22) | collective-permute-done | bytes 196640 | tf_op jit(solution)/shard_map/ppermute | solution.py:344
  254.9 3.2 %collective-permute-start.26 = (f32[136,256]{1,0:T(8,128)S(1)}, f32[136,256]{1,0:T(8,128)S(1)}, u32[]{:S(2)}, u32[]{:S(2)}) collective-permute-start(f32[136,256]{1,0:T(8,128)S(1)} %get-tuple-element.156), channel_id=1, source_target_pairs={{0,8},{4,12},{8,0},{12,4},{1,9},{5,13},{9,1},{13,5},{2,10},{6,14},... | collective-permute-start | bytes 417800 | tf_op jit(solution)/shard_map/ppermute | solution.py:344
  258.1 1.2 collective-permute-start.27
  259.3 2.8 %collective-permute-done.25 = f32[136,256]{1,0:T(8,128)S(1)} collective-permute-done((f32[136,256]{1,0:T(8,128)S(1)}, f32[136,256]{1,0:T(8,128)S(1)}, u32[]{:S(2)}, u32[]{:S(2)}) %collective-permute-start.25) | collective-permute-done | bytes 139296 | tf_op jit(solution)/shard_map/ppermute | solution.py:344
  262.1 6.0 %collective-permute-done.26 = f32[136,256]{1,0:T(8,128)S(1)} collective-permute-done((f32[136,256]{1,0:T(8,128)S(1)}, f32[136,256]{1,0:T(8,128)S(1)}, u32[]{:S(2)}, u32[]{:S(2)}) %collective-permute-start.26) | collective-permute-done | bytes 139296 | tf_op jit(solution)/shard_map/ppermute | solution.py:344
  268.3 0.6 collective-permute-start.29
  269.0 0.1 copy.19
  269.2 0.1 copy.22
  269.4 0.1 copy.21
  269.6 0.1 copy.20
  269.7 3.6 %collective-permute-done.29 = f32[128,256]{1,0:T(8,128)S(1)} collective-permute-done((f32[128,256]{1,0:T(8,128)S(1)}, f32[128,256]{1,0:T(8,128)S(1)}, u32[]{:S(2)}, u32[]{:S(2)}) %collective-permute-start.29) | collective-permute-done | bytes 131104 | tf_op jit(solution)/shard_map/ppermute | solution.py:293
  273.4 1.3 collective-permute-done.30
  275.0 0.9 copy-done.7
  276.0 0.8 copy-done.8
  (73 shorter events, 0.9 us)
Async XLA Ops:
  3.1 53.6 %collective-permute-start.7 = (f32[768,256]{1,0:T(8,128)}, f32[768,256]{1,0:T(8,128)S(1)}, u32[]{:S(2)}, u32[]{:S(2)}) collective-permute-start(f32[768,256]{1,0:T(8,128)} %get-tuple-element.78), channel_id=1, source_target_pairs={{0,8},{4,12},{8,0},{12,4},{1,9},{5,13},{9,1},{13,5},{2,10},{6,14},... | collective-permute-start | bytes 2359304 | tf_op jit(solution)/shard_map/ppermute | solution.py:344
  9.6 30.0 %collective-permute-start = (f32[640,256]{1,0:T(8,128)}, f32[640,256]{1,0:T(8,128)S(1)}, u32[]{:S(2)}, u32[]{:S(2)}) collective-permute-start(f32[640,256]{1,0:T(8,128)} %get-tuple-element.80), channel_id=1, source_target_pairs={{0,4},{4,0},{8,12},{12,8},{1,5},{5,1},{9,13},{13,9},{2,6},{6,2},{1... | collective-permute-start | bytes 1966088 | tf_op jit(solution)/shard_map/ppermute | solution.py:344
  11.2 76.6 %collective-permute-start.8 = (f32[640,256]{1,0:T(8,128)}, f32[640,256]{1,0:T(8,128)}, u32[]{:S(2)}, u32[]{:S(2)}) collective-permute-start(f32[640,256]{1,0:T(8,128)} %get-tuple-element.77), channel_id=1, source_target_pairs={{0,12},{4,8},{8,4},{12,0},{1,13},{5,9},{9,5},{13,1},{2,14},{6,10},... | collective-permute-start | bytes 1966088 | tf_op jit(solution)/shard_map/ppermute | solution.py:344
  11.2 34.1 %copy-start = (f32[512,256]{1,0:T(8,128)S(1)}, f32[512,256]{1,0:T(8,128)}, u32[]{:S(2)}) copy-start(f32[512,256]{1,0:T(8,128)} %own_ref.1) | copy-start | bytes 1572868
  39.6 94.5 %copy-start.3 = (f32[640,256]{1,0:T(8,128)}, f32[640,256]{1,0:T(8,128)S(1)}, u32[]{:S(2)}) copy-start(f32[640,256]{1,0:T(8,128)S(1)} %collective-permute-done.refs_1_) | copy-start | bytes 1966084
  42.9 50.3 %collective-permute-start.1 = (f32[576,256]{1,0:T(8,128)}, f32[576,256]{1,0:T(8,128)}, u32[]{:S(2)}, u32[]{:S(2)}) collective-permute-start(f32[576,256]{1,0:T(8,128)} %get-tuple-element.82), channel_id=1, source_target_pairs={{0,4},{4,0},{8,12},{12,8},{1,5},{5,1},{9,13},{13,9},{2,6},{6,2},{1... | collective-permute-start | bytes 1769480 | tf_op jit(solution)/shard_map/ppermute | solution.py:344
  45.4 88.7 %collective-permute-start.2 = (f32[576,256]{1,0:T(8,128)}, f32[576,256]{1,0:T(8,128)}, u32[]{:S(2)}, u32[]{:S(2)}) collective-permute-start(f32[576,256]{1,0:T(8,128)} %get-tuple-element.83), channel_id=1, source_target_pairs={{0,8},{4,12},{8,0},{12,4},{1,9},{5,13},{9,1},{13,5},{2,10},{6,14},... | collective-permute-start | bytes 1769480 | tf_op jit(solution)/shard_map/ppermute | solution.py:344
  45.4 36.3 %collective-permute-start.12 = (f32[128,256]{1,0:T(8,128)S(1)}, f32[128,256]{1,0:T(8,128)S(1)}, u32[]{:S(2)}, u32[]{:S(2)}) collective-permute-start(f32[128,256]{1,0:T(8,128)S(1)} %constant_dynamic-slice_fusion), channel_id=1, source_target_pairs={{0,4},{4,0},{8,12},{12,8},{1,5},{5,1},{9,13},{13,9},{2,6},{6,2},{1... | collective-permute-start | bytes 393224 | tf_op jit(solution)/shard_map/ppermute | solution.py:344
  56.7 27.8 %collective-permute-start.13 = (f32[128,256]{1,0:T(8,128)S(1)}, f32[128,256]{1,0:T(8,128)S(1)}, u32[]{:S(2)}, u32[]{:S(2)}) collective-permute-start(f32[128,256]{1,0:T(8,128)S(1)} %slice.111), channel_id=1, source_target_pairs={{0,4},{4,0},{8,12},{12,8},{1,5},{5,1},{9,13},{13,9},{2,6},{6,2},{1... | collective-permute-start | bytes 393224 | tf_op jit(solution)/shard_map/ppermute | solution.py:344
  81.7 52.4 %collective-permute-start.3 = (f32[576,256]{1,0:T(8,128)}, f32[576,256]{1,0:T(8,128)}, u32[]{:S(2)}, u32[]{:S(2)}) collective-permute-start(f32[576,256]{1,0:T(8,128)} %get-tuple-element.84), channel_id=1, source_target_pairs={{0,12},{4,8},{8,4},{12,0},{1,13},{5,9},{9,5},{13,1},{2,14},{6,10},... | collective-permute-start | bytes 1769480 | tf_op jit(solution)/shard_map/ppermute | solution.py:344
  84.6 49.6 %collective-permute-start.15 = (f32[384,256]{1,0:T(8,128)S(1)}, f32[384,256]{1,0:T(8,128)S(1)}, u32[]{:S(2)}, u32[]{:S(2)}) collective-permute-start(f32[384,256]{1,0:T(8,128)S(1)} %pad_maximum_fusion.refs_0_), channel_id=1, source_target_pairs={{0,2},{1,3},{2,0},{3,1},{4,6},{5,7},{6,4},{7,5},{8,10},{9,11},{10,... | collective-permute-start | bytes 1179656 | tf_op jit(solution)/shard_map/ppermute | solution.py:293
  90.9 81.9 %collective-permute-start.10 = (f32[576,256]{1,0:T(8,128)}, f32[576,256]{1,0:T(8,128)}, u32[]{:S(2)}, u32[]{:S(2)}) collective-permute-start(f32[576,256]{1,0:T(8,128)} %get-tuple-element.93), channel_id=1, source_target_pairs={{0,8},{4,12},{8,0},{12,4},{1,9},{5,13},{9,1},{13,5},{2,10},{6,14},... | collective-permute-start | bytes 1769480 | tf_op jit(solution)/shard_map/ppermute | solution.py:344
  93.2 48.7 %collective-permute-start.11 = (f32[576,256]{1,0:T(8,128)}, f32[576,256]{1,0:T(8,128)}, u32[]{:S(2)}, u32[]{:S(2)}) collective-permute-start(f32[576,256]{1,0:T(8,128)} %get-tuple-element.94), channel_id=1, source_target_pairs={{0,12},{4,8},{8,4},{12,0},{1,13},{5,9},{9,5},{13,1},{2,14},{6,10},... | collective-permute-start | bytes 1769480 | tf_op jit(solution)/shard_map/ppermute | solution.py:344
  134.1 41.5 %collective-permute-start.9 = (f32[576,256]{1,0:T(8,128)}, f32[576,256]{1,0:T(8,128)}, u32[]{:S(2)}, u32[]{:S(2)}) collective-permute-start(f32[576,256]{1,0:T(8,128)} %get-tuple-element.92), channel_id=1, source_target_pairs={{0,4},{4,0},{8,12},{12,8},{1,5},{5,1},{9,13},{13,9},{2,6},{6,2},{1... | collective-permute-start | bytes 1769480 | tf_op jit(solution)/shard_map/ppermute | solution.py:344
  134.1 43.8 %collective-permute-start.14 = (f32[384,256]{1,0:T(8,128)S(1)}, f32[384,256]{1,0:T(8,128)S(1)}, u32[]{:S(2)}, u32[]{:S(2)}) collective-permute-start(f32[384,256]{1,0:T(8,128)S(1)} %pad_maximum_fusion.refs_0_), channel_id=1, source_target_pairs={{0,1},{1,0},{2,3},{3,2},{4,5},{5,4},{6,7},{7,6},{8,9},{9,8},{10,11... | collective-permute-start | bytes 1179656 | tf_op jit(solution)/shard_map/ppermute | solution.py:293
  134.2 43.8 %collective-permute-start.16 = (f32[384,256]{1,0:T(8,128)S(1)}, f32[384,256]{1,0:T(8,128)S(1)}, u32[]{:S(2)}, u32[]{:S(2)}) collective-permute-start(f32[384,256]{1,0:T(8,128)S(1)} %collective-permute-done.15.refs_2_), channel_id=1, source_target_pairs={{0,1},{1,0},{2,3},{3,2},{4,5},{5,4},{6,7},{7,6},{8,9},{9,8},{10,11... | collective-permute-start | bytes 1179656 | tf_op jit(solution)/shard_map/ppermute | solution.py:293
  141.9 65.3 %collective-permute-start.4 = (f32[512,256]{1,0:T(8,128)}, f32[512,256]{1,0:T(8,128)S(1)}, u32[]{:S(2)}, u32[]{:S(2)}) collective-permute-start(f32[512,256]{1,0:T(8,128)} %get-tuple-element.87), channel_id=1, source_target_pairs={{0,4},{4,0},{8,12},{12,8},{1,5},{5,1},{9,13},{13,9},{2,6},{6,2},{1... | collective-permute-start | bytes 1572872 | tf_op jit(solution)/shard_map/ppermute | solution.py:344
  172.8 38.4 %collective-permute-start.5 = (f32[512,256]{1,0:T(8,128)}, f32[512,256]{1,0:T(8,128)S(1)}, u32[]{:S(2)}, u32[]{:S(2)}) collective-permute-start(f32[512,256]{1,0:T(8,128)} %get-tuple-element.88), channel_id=1, source_target_pairs={{0,8},{4,12},{8,0},{12,4},{1,9},{5,13},{9,1},{13,5},{2,10},{6,14},... | collective-permute-start | bytes 1572872 | tf_op jit(solution)/shard_map/ppermute | solution.py:344
  175.6 3.7 %copy-start.2 = (f32[640,256]{1,0:T(8,128)S(1)}, f32[640,256]{1,0:T(8,128)}, u32[]{:S(2)}) copy-start(f32[640,256]{1,0:T(8,128)} %get-tuple-element.96.refs_0_) | copy-start | bytes 1966084
  175.6 3.7 %copy-start.4 = (f32[640,256]{1,0:T(8,128)S(1)}, f32[640,256]{1,0:T(8,128)}, u32[]{:S(2)}) copy-start(f32[640,256]{1,0:T(8,128)} %copy-done.3) | copy-start | bytes 1966084
  175.6 41.9 %collective-permute-start.6 = (f32[512,256]{1,0:T(8,128)}, f32[512,256]{1,0:T(8,128)S(1)}, u32[]{:S(2)}, u32[]{:S(2)}) collective-permute-start(f32[512,256]{1,0:T(8,128)} %get-tuple-element.89), channel_id=1, source_target_pairs={{0,12},{4,8},{8,4},{12,0},{1,13},{5,9},{9,5},{13,1},{2,14},{6,10},... | collective-permute-start | bytes 1572872 | tf_op jit(solution)/shard_map/ppermute | solution.py:344
  179.2 8.7 %copy-start.5 = (f32[576,256]{1,0:T(8,128)S(1)}, f32[576,256]{1,0:T(8,128)}, u32[]{:S(2)}) copy-start(f32[576,256]{1,0:T(8,128)} %get-tuple-element.95.refs_0_) | copy-start | bytes 1769476
  188.0 9.7 %copy-start.6 = (f32[576,256]{1,0:T(8,128)S(1)}, f32[576,256]{1,0:T(8,128)}, u32[]{:S(2)}) copy-start(f32[576,256]{1,0:T(8,128)} %get-tuple-element.91.refs_0_) | copy-start | bytes 1769476
  197.7 13.5 %copy-start.1 = (f32[512,256]{1,0:T(8,128)S(1)}, f32[512,256]{1,0:T(8,128)}, u32[]{:S(2)}) copy-start(f32[512,256]{1,0:T(8,128)} %get-tuple-element.86.refs_0_) | copy-start | bytes 1572868
  213.1 12.2 %collective-permute-start.19 = (f32[64,256]{1,0:T(8,128)S(1)}, f32[64,256]{1,0:T(8,128)S(1)}, u32[]{:S(2)}, u32[]{:S(2)}) collective-permute-start(f32[64,256]{1,0:T(8,128)S(1)} %get-tuple-element.130), channel_id=1, source_target_pairs={{0,12},{4,8},{8,4},{12,0},{1,13},{5,9},{9,5},{13,1},{2,14},{6,10},... | collective-permute-start | bytes 196616 | tf_op jit(solution)/shard_map/ppermute | solution.py:344
  216.5 10.3 %collective-permute-start.18 = (f32[64,256]{1,0:T(8,128)S(1)}, f32[64,256]{1,0:T(8,128)S(1)}, u32[]{:S(2)}, u32[]{:S(2)}) collective-permute-start(f32[64,256]{1,0:T(8,128)S(1)} %get-tuple-element.128), channel_id=1, source_target_pairs={{0,8},{4,12},{8,0},{12,4},{1,9},{5,13},{9,1},{13,5},{2,10},{6,14},... | collective-permute-start | bytes 196616 | tf_op jit(solution)/shard_map/ppermute | solution.py:344
  216.5 10.3 %collective-permute-start.17 = (f32[64,256]{1,0:T(8,128)S(1)}, f32[64,256]{1,0:T(8,128)S(1)}, u32[]{:S(2)}, u32[]{:S(2)}) collective-permute-start(f32[64,256]{1,0:T(8,128)S(1)} %get-tuple-element.126), channel_id=1, source_target_pairs={{0,4},{4,0},{8,12},{12,8},{1,5},{5,1},{9,13},{13,9},{2,6},{6,2},{1... | collective-permute-start | bytes 196616 | tf_op jit(solution)/shard_map/ppermute | solution.py:344
  226.8 3.1 %collective-permute-start.20 = (f32[4,2,136,256]{3,2,1,0:T(8,128)}, f32[4,2,136,256]{3,2,1,0:T(8,128)}, u32[]{:S(2)}, u32[]{:S(2)}) collective-permute-start(f32[4,2,136,256]{3,2,1,0:T(8,128)} %get-tuple-element.131), channel_id=1, source_target_pairs={{0,1},{1,0},{2,3},{3,2},{4,5},{5,4},{6,7},{7,6},{8,9},{9,8},{10,11... | collective-permute-start | bytes 3342344 | tf_op jit(solution)/shard_map/ppermute | solution.py:306
  231.1 23.7 %collective-permute-start.24 = (f32[4,136,256]{2,1,0:T(8,128)S(1)}, f32[4,136,256]{2,1,0:T(8,128)S(1)}, u32[]{:S(2)}, u32[]{:S(2)}) collective-permute-start(f32[4,136,256]{2,1,0:T(8,128)S(1)} %add_bitcast_fusion), channel_id=1, source_target_pairs={{0,2},{1,3},{2,0},{3,1},{4,6},{5,7},{6,4},{7,5},{8,10},{9,11},{10,... | collective-permute-start | bytes 1671176 | tf_op jit(solution)/shard_map/ppermute | solution.py:316
  232.6 10.7 %collective-permute-start.23 = (f32[192,256]{1,0:T(8,128)S(1)}, f32[192,256]{1,0:T(8,128)S(1)}, u32[]{:S(2)}, u32[]{:S(2)}) collective-permute-start(f32[192,256]{1,0:T(8,128)S(1)} %pad_maximum_fusion.3), channel_id=1, source_target_pairs={{0,12},{4,8},{8,4},{12,0},{1,13},{5,9},{9,5},{13,1},{2,14},{6,10},... | collective-permute-start | bytes 589832 | tf_op jit(solution)/shard_map/ppermute | solution.py:344
  236.1 18.7 %collective-permute-start.22 = (f32[192,256]{1,0:T(8,128)S(1)}, f32[192,256]{1,0:T(8,128)S(1)}, u32[]{:S(2)}, u32[]{:S(2)}) collective-permute-start(f32[192,256]{1,0:T(8,128)S(1)} %pad_maximum_fusion.2), channel_id=1, source_target_pairs={{0,8},{4,12},{8,0},{12,4},{1,9},{5,13},{9,1},{13,5},{2,10},{6,14},... | collective-permute-start | bytes 589832 | tf_op jit(solution)/shard_map/ppermute | solution.py:344
  241.6 13.2 %collective-permute-start.21 = (f32[192,256]{1,0:T(8,128)S(1)}, f32[192,256]{1,0:T(8,128)S(1)}, u32[]{:S(2)}, u32[]{:S(2)}) collective-permute-start(f32[192,256]{1,0:T(8,128)S(1)} %pad_maximum_fusion.1), channel_id=1, source_target_pairs={{0,4},{4,0},{8,12},{12,8},{1,5},{5,1},{9,13},{13,9},{2,6},{6,2},{1... | collective-permute-start | bytes 589832 | tf_op jit(solution)/shard_map/ppermute | solution.py:344
  254.9 7.3 %collective-permute-start.25 = (f32[136,256]{1,0:T(8,128)S(1)}, f32[136,256]{1,0:T(8,128)S(1)}, u32[]{:S(2)}, u32[]{:S(2)}) collective-permute-start(f32[136,256]{1,0:T(8,128)S(1)} %get-tuple-element.154), channel_id=1, source_target_pairs={{0,4},{4,0},{8,12},{12,8},{1,5},{5,1},{9,13},{13,9},{2,6},{6,2},{1... | collective-permute-start | bytes 417800 | tf_op jit(solution)/shard_map/ppermute | solution.py:344
  254.9 13.2 %collective-permute-start.26 = (f32[136,256]{1,0:T(8,128)S(1)}, f32[136,256]{1,0:T(8,128)S(1)}, u32[]{:S(2)}, u32[]{:S(2)}) collective-permute-start(f32[136,256]{1,0:T(8,128)S(1)} %get-tuple-element.156), channel_id=1, source_target_pairs={{0,8},{4,12},{8,0},{12,4},{1,9},{5,13},{9,1},{13,5},{2,10},{6,14},... | collective-permute-start | bytes 417800 | tf_op jit(solution)/shard_map/ppermute | solution.py:344
  258.1 10.1 %collective-permute-start.27 = (f32[136,256]{1,0:T(8,128)S(1)}, f32[136,256]{1,0:T(8,128)S(1)}, u32[]{:S(2)}, u32[]{:S(2)}) collective-permute-start(f32[136,256]{1,0:T(8,128)S(1)} %get-tuple-element.155), channel_id=1, source_target_pairs={{0,12},{4,8},{8,4},{12,0},{1,13},{5,9},{9,5},{13,1},{2,14},{6,10},... | collective-permute-start | bytes 417800 | tf_op jit(solution)/shard_map/ppermute | solution.py:344
  268.3 5.0 %collective-permute-start.29 = (f32[128,256]{1,0:T(8,128)S(1)}, f32[128,256]{1,0:T(8,128)S(1)}, u32[]{:S(2)}, u32[]{:S(2)}) collective-permute-start(f32[128,256]{1,0:T(8,128)S(1)} %get-tuple-element.153), channel_id=1, source_target_pairs={{0,2},{1,3},{2,0},{3,1},{4,6},{5,7},{6,4},{7,5},{8,10},{9,11},{10,... | collective-permute-start | bytes 393224 | tf_op jit(solution)/shard_map/ppermute | solution.py:293
  269.0 4.4 %collective-permute-start.28 = (f32[128,256]{1,0:T(8,128)S(1)}, f32[128,256]{1,0:T(8,128)S(1)}, u32[]{:S(2)}, u32[]{:S(2)}) collective-permute-start(f32[128,256]{1,0:T(8,128)S(1)} %get-tuple-element.153), channel_id=1, source_target_pairs={{0,1},{1,0},{2,3},{3,2},{4,5},{5,4},{6,7},{7,6},{8,9},{9,8},{10,11... | collective-permute-start | bytes 393224 | tf_op jit(solution)/shard_map/ppermute | solution.py:293
  273.4 1.3 collective-permute-start.30
  275.0 1.0 copy-start.7
  276.0 0.8 copy-start.8
